TPU v7x, 512 devices: a whole 4x8x8 slice. The times are simulated.
512 devices in a mesh: dp: 512 (over y, x, z, core).
Axes of the slice: x: 4, y: 8, z: 8, core: 2. Of those that a mesh axis runs over, the one named last changes fastest.
Arguments:
- query_raw: bfloat16 [36864, 3584], P('dp'), may hold values from -1.25 to 1.25
- passage_raw: bfloat16 [36864, 3584], P('dp'), may hold values from -1.25 to 1.25
- pairing: int32 [512, 72], P('dp'), may hold values from 0 to 71, as said below
Outputs:
- losses: float32 [36864], P('dp')
- query_grad: float32 [36864, 3584], P('dp')
- passage_grad: float32 [36864, 3584], P('dp')
Inputs may be any that keep to these rules, and one draw needn't show every extreme that they name: Row r of query block b is paired with row pairing[b, r] of passage block b; each row of pairing is a permutation of 0 to 71.
All inputs are finite; a program needn't handle non-finite values.
Results may differ from a plain program's by a relative error of at most 0.006.
Values may be sent and summed in bfloat16 or wider, within the bound.
No kernel may reach another device: no remote copies, remote signals or barrier semaphores. Data moves between devices by JAX's collectives and lax.ppermute only.
A program may use at most 64 MiB of HBM per device.

v0:
```python
import jax
import jax.numpy as jnp
from jax import lax
from jax.sharding import PartitionSpec as P

WINDOW = 3


INV_TEMP = 20.0
EPS = 1e-06


def passed_along(value, axis, steps):
    count = lax.axis_size(axis)
    pairs = [(source, (source + steps) % count) for source in range(count)]
    return lax.ppermute(value, axis, pairs)


def unit_rows(raw_rows):
    widened = raw_rows.astype(jnp.float32)
    scale_rows = lax.rsqrt(jnp.sum(widened * widened, axis=1, keepdims=True) + EPS)
    return (widened * scale_rows, scale_rows)


def contract(left_rows, right_rows):
    return lax.dot_general(
        left_rows, right_rows, (((1,), (1,)), ((), ())), preferred_element_type=jnp.float32
    )


def expand(weight_rows, key_rows):
    return jnp.dot(weight_rows, key_rows, preferred_element_type=jnp.float32)


def reverse_apply(weight_rows, row_data):
    return lax.dot_general(
        weight_rows, row_data, (((0,), (0,)), ((), ())), preferred_element_type=jnp.float32
    )


def similarity(left_rows, right_rows):
    return jnp.exp(INV_TEMP * contract(left_rows, right_rows) - INV_TEMP)


def centered(matrix):
    padding = jnp.zeros((matrix.shape[0], WINDOW * matrix.shape[1]), jnp.float32)
    return jnp.concatenate([padding, matrix, padding], axis=1)


def normalize_loss(query_total, passage_total, paired, positive):
    normalizer = query_total + jnp.sum(paired * passage_total[None, :], axis=1)
    reciprocal = 1.0 / normalizer
    passage_share = jnp.sum(paired * reciprocal[:, None], axis=0)
    losses = jnp.log(normalizer) + INV_TEMP - positive
    return (reciprocal, passage_share, losses)


def raw_gradient(unit_data, scale_rows, gradient):
    return (
        gradient - unit_data * jnp.sum(unit_data * gradient, axis=1, keepdims=True)
    ) * scale_rows


def key_move(payload, offset):
    return passed_along(payload, "dp", offset)


def grad_move(payload, offset):
    return passed_along(payload, "dp", offset)


def fetch_blocks(own_rows, direction, send_step):
    found_list = []
    for step_index in range(1, WINDOW + 1):
        found_list.append(send_step(own_rows, -direction * step_index))
    return found_list


def home_sum(part_list, direction, send_step):
    running = send_step(part_list[0], direction)
    for step_index in range(2, WINDOW + 1):
        running = running + send_step(part_list[step_index - 1], direction * step_index)
    return running


def per_device(query_raw, passage_raw, pairing):
    query_unit, query_scale = unit_rows(query_raw)
    passage_unit, passage_scale = unit_rows(passage_raw)
    query_low = query_unit.astype(jnp.bfloat16)
    passage_low = passage_unit.astype(jnp.bfloat16)
    row_count = query_low.shape[0]
    own_rows = jnp.stack([query_low, passage_low])
    paired = (pairing[0][:, None] == jnp.arange(row_count, dtype=jnp.int32)[None, :]).astype(
        jnp.float32
    )
    eye_rows = jnp.eye(row_count, dtype=jnp.float32)
    behind = fetch_blocks(own_rows, -1, key_move)
    ahead = fetch_blocks(own_rows, 1, key_move)
    window_rows = jnp.concatenate(behind[::-1] + [own_rows] + ahead, axis=1)
    query_keys = window_rows[0]
    passage_keys = window_rows[1]
    self_keep = 1.0 - centered(eye_rows)
    positive_center = centered(paired)
    score_cross = INV_TEMP * contract(query_low, passage_keys)
    exp_cross = jnp.exp(score_cross - INV_TEMP)
    exp_queries = similarity(query_low, query_keys) * self_keep
    exp_passages = similarity(passage_low, passage_keys) * self_keep
    exp_reverse = similarity(passage_low, query_keys) * (1.0 - centered(paired.T))
    query_total = jnp.sum(exp_cross, axis=1) + jnp.sum(exp_queries, axis=1)
    passage_total = jnp.sum(exp_passages, axis=1) + jnp.sum(exp_reverse, axis=1)
    center_range = slice(WINDOW * row_count, (WINDOW + 1) * row_count)
    positive = jnp.sum(score_cross[:, center_range] * paired, axis=1)
    reciprocal, passage_share, losses = normalize_loss(query_total, passage_total, paired, positive)
    cross_rows = (exp_cross * reciprocal[:, None] - positive_center).astype(jnp.bfloat16)
    query_rows = (exp_queries * reciprocal[:, None]).astype(jnp.bfloat16)
    reverse_rows = (exp_reverse * passage_share[:, None]).astype(jnp.bfloat16)
    passage_rows = (exp_passages * passage_share[:, None]).astype(jnp.bfloat16)
    query_sum = expand(cross_rows, passage_keys) + expand(query_rows, query_keys)
    passage_sum = expand(reverse_rows, query_keys) + expand(passage_rows, passage_keys)

    def key_part(position):
        column_range = slice(position * row_count, (position + 1) * row_count)
        query_part = reverse_apply(query_rows[:, column_range], query_low) + reverse_apply(
            reverse_rows[:, column_range], passage_low
        )
        passage_part = reverse_apply(cross_rows[:, column_range], query_low) + reverse_apply(
            passage_rows[:, column_range], passage_low
        )
        return jnp.stack([query_part, passage_part])

    ahead_parts = [key_part(WINDOW + step_index) for step_index in range(1, WINDOW + 1)]
    behind_parts = [key_part(WINDOW - step_index) for step_index in range(1, WINDOW + 1)]
    returned = (
        home_sum(ahead_parts, 1, grad_move)
        + home_sum(behind_parts, -1, grad_move)
        + key_part(WINDOW)
    )
    query_gradient = INV_TEMP * (query_sum + returned[0])
    passage_gradient = INV_TEMP * (passage_sum + returned[1])
    query_grad = raw_gradient(query_unit, query_scale, query_gradient)
    passage_grad = raw_gradient(passage_unit, passage_scale, passage_gradient)
    return (losses, query_grad, passage_grad)


def solution(mesh):
    in_specs = (P("dp", None), P("dp", None), P("dp", None))
    out_specs = (P("dp"), P("dp", None), P("dp", None))
    return jax.shard_map(
        per_device, mesh=mesh, in_specs=in_specs, out_specs=out_specs, check_vma=False
    )
```

profile of v0, /device:TPU:1, one launch (start us, length us, event | category | flops | bytes accessed | tf_op | source)
XLA Modules:
  0.0 274.1 jit_solution(7737269956463267148)
XLA Ops:
  0.6 1.2 fusion.46
  1.9 1.2 fusion.50
  3.2 1.4 fusion.118
  4.7 7.2 %collective-permute-start = (bf16[2,72,3584]{2,1,0:T(8,128)(2,1)S(1)}, bf16[2,72,3584]{2,1,0:T(8,128)(2,1)S(1)}, u32[]{:S(2)}, u32[]{:S(2)}) collective-permute-start(bf16[2,72,3584]{2,1,0:T(8,128)(2,1)S(1)} %pad_maximum_fusion.6), channel_id=1, source_target_pairs={{0,3},{1,4},{2,5},{3,6},{4,7},{5,8},{6,9},{7,10},{8,11},{9,12},{10... | collective-permute-start | bytes 3096584 | tf_op jit(solution)/shard_map/ppermute | solution.py:16
  11.9 4.0 %collective-permute-start.1 = (bf16[2,72,3584]{2,1,0:T(8,128)(2,1)S(1)}, bf16[2,72,3584]{2,1,0:T(8,128)(2,1)S(1)}, u32[]{:S(2)}, u32[]{:S(2)}) collective-permute-start(bf16[2,72,3584]{2,1,0:T(8,128)(2,1)S(1)} %pad_maximum_fusion.6), channel_id=1, source_target_pairs={{0,2},{1,3},{2,4},{3,5},{4,6},{5,7},{6,8},{7,9},{8,10},{9,11},{10,... | collective-permute-start | bytes 3096584 | tf_op jit(solution)/shard_map/ppermute | solution.py:16
  15.9 2.2 collective-permute-start.2
  18.1 2.1 collective-permute-start.3
  20.3 9.4 %collective-permute-start.4 = (bf16[2,72,3584]{2,1,0:T(8,128)(2,1)S(1)}, bf16[2,72,3584]{2,1,0:T(8,128)(2,1)S(1)}, u32[]{:S(2)}, u32[]{:S(2)}) collective-permute-start(bf16[2,72,3584]{2,1,0:T(8,128)(2,1)S(1)} %pad_maximum_fusion.6), channel_id=1, source_target_pairs={{0,510},{1,511},{2,0},{3,1},{4,2},{5,3},{6,4},{7,5},{8,6},{9,7},{1... | collective-permute-start | bytes 3096584 | tf_op jit(solution)/shard_map/ppermute | solution.py:16
  29.8 26.5 %collective-permute-done = bf16[2,72,3584]{2,1,0:T(8,128)(2,1)S(1)} collective-permute-done((bf16[2,72,3584]{2,1,0:T(8,128)(2,1)S(1)}, bf16[2,72,3584]{2,1,0:T(8,128)(2,1)S(1)}, u32[]{:S(2)}, u32[]{:S(2)}) %collective-permute-start) | collective-permute-done | bytes 1032224 | tf_op jit(solution)/shard_map/ppermute | solution.py:16
  56.3 4.5 %collective-permute-start.5 = (bf16[2,72,3584]{2,1,0:T(8,128)(2,1)S(1)}, bf16[2,72,3584]{2,1,0:T(8,128)(2,1)S(1)}, u32[]{:S(2)}, u32[]{:S(2)}) collective-permute-start(bf16[2,72,3584]{2,1,0:T(8,128)(2,1)S(1)} %pad_maximum_fusion.6), channel_id=1, source_target_pairs={{0,509},{1,510},{2,511},{3,0},{4,1},{5,2},{6,3},{7,4},{8,5},{9,6},... | collective-permute-start | bytes 3096584 | tf_op jit(solution)/shard_map/ppermute | solution.py:16
  60.9 16.1 %collective-permute-done.1 = bf16[2,72,3584]{2,1,0:T(8,128)(2,1)S(1)} collective-permute-done((bf16[2,72,3584]{2,1,0:T(8,128)(2,1)S(1)}, bf16[2,72,3584]{2,1,0:T(8,128)(2,1)S(1)}, u32[]{:S(2)}, u32[]{:S(2)}) %collective-permute-start.1) | collective-permute-done | bytes 1032224 | tf_op jit(solution)/shard_map/ppermute | solution.py:16
  77.0 1.8 collective-permute-done.2
  79.2 14.3 %collective-permute-done.5 = bf16[2,72,3584]{2,1,0:T(8,128)(2,1)S(1)} collective-permute-done((bf16[2,72,3584]{2,1,0:T(8,128)(2,1)S(1)}, bf16[2,72,3584]{2,1,0:T(8,128)(2,1)S(1)}, u32[]{:S(2)}, u32[]{:S(2)}) %collective-permute-start.5) | collective-permute-done | bytes 1032224 | tf_op jit(solution)/shard_map/ppermute | solution.py:16
  93.6 1.3 fusion.55
  94.9 1.3 fusion.136
  96.2 1.3 fusion.138
  97.5 1.3 fusion.137
  104.4 10.8 %collective-permute-start.11 = (f32[2,72,3584]{2,1,0:T(8,128)S(1)}, f32[2,72,3584]{2,1,0:T(8,128)S(1)}, u32[]{:S(2)}, u32[]{:S(2)}) collective-permute-start(f32[2,72,3584]{2,1,0:T(8,128)S(1)} %pad_maximum_fusion.5), channel_id=1, source_target_pairs={{0,509},{1,510},{2,511},{3,0},{4,1},{5,2},{6,3},{7,4},{8,5},{9,6},... | collective-permute-start | bytes 6193160 | tf_op jit(solution)/shard_map/ppermute | solution.py:16
  115.2 0.4 fusion.11
  116.2 2.6 collective-permute-start.9
  118.8 0.4 fusion.13
  119.3 0.4 fusion.12
  119.8 2.1 collective-permute-start.10
  122.0 0.4 fusion.9
  122.4 0.4 fusion.8
  122.9 4.2 %collective-permute-start.8 = (f32[2,72,3584]{2,1,0:T(8,128)S(1)}, f32[2,72,3584]{2,1,0:T(8,128)S(1)}, u32[]{:S(2)}, u32[]{:S(2)}) collective-permute-start(f32[2,72,3584]{2,1,0:T(8,128)S(1)} %pad_maximum_fusion.2), channel_id=1, source_target_pairs={{0,3},{1,4},{2,5},{3,6},{4,7},{5,8},{6,9},{7,10},{8,11},{9,12},{10... | collective-permute-start | bytes 6193160 | tf_op jit(solution)/shard_map/ppermute | solution.py:16
  127.6 0.4 fusion.4
  128.2 1.9 collective-permute-start.6
  130.5 0.4 fusion.7
  131.0 0.4 fusion.94
  131.4 0.4 fusion.6
  132.0 49.2 %collective-permute-done.11 = f32[2,72,3584]{2,1,0:T(8,128)S(1)} collective-permute-done((f32[2,72,3584]{2,1,0:T(8,128)S(1)}, f32[2,72,3584]{2,1,0:T(8,128)S(1)}, u32[]{:S(2)}, u32[]{:S(2)}) %collective-permute-start.11) | collective-permute-done | bytes 2064416 | tf_op jit(solution)/shard_map/ppermute | solution.py:16
  181.2 13.8 %collective-permute-start.7 = (f32[2,72,3584]{2,1,0:T(8,128)S(1)}, f32[2,72,3584]{2,1,0:T(8,128)}, u32[]{:S(2)}, u32[]{:S(2)}) collective-permute-start(f32[2,72,3584]{2,1,0:T(8,128)S(1)} %pad_maximum_fusion.1), channel_id=1, source_target_pairs={{0,2},{1,3},{2,4},{3,5},{4,6},{5,7},{6,8},{7,9},{8,10},{9,11},{10,... | collective-permute-start | bytes 6193160 | tf_op jit(solution)/shard_map/ppermute | solution.py:16
  195.0 0.4 fusion.61
  195.4 0.4 fusion.17
  196.3 0.4 fusion.16
  196.7 0.5 add_subtract_fusion
  197.3 0.8 fusion.21
  198.0 0.8 fusion.18
  198.8 1.8 collective-permute-done.9
  200.6 37.6 %collective-permute-done.10 = f32[2,72,3584]{2,1,0:T(8,128)S(1)} collective-permute-done((f32[2,72,3584]{2,1,0:T(8,128)S(1)}, f32[2,72,3584]{2,1,0:T(8,128)S(1)}, u32[]{:S(2)}, u32[]{:S(2)}) %collective-permute-start.10) | collective-permute-done | bytes 2064416 | tf_op jit(solution)/shard_map/ppermute | solution.py:16
  238.2 1.3 copy-done.2
  239.5 26.6 %collective-permute-done.7 = f32[2,72,3584]{2,1,0:T(8,128)} collective-permute-done((f32[2,72,3584]{2,1,0:T(8,128)S(1)}, f32[2,72,3584]{2,1,0:T(8,128)}, u32[]{:S(2)}, u32[]{:S(2)}) %collective-permute-start.7) | collective-permute-done | bytes 2064416 | tf_op jit(solution)/shard_map/ppermute | solution.py:16
  266.1 3.7 %maximum_add_fusion = f32[2,72,3584]{2,1,0:T(8,128)S(1)} fusion(f32[1,72,3584]{2,1,0:T(8,128)S(1)} %fusion.17, f32[1,72,3584]{2,1,0:T(8,128)S(1)} %fusion.16, f32[2,72,3584]{2,1,0:T(8,128)S(1)} %collective-permute-done.11, f32[2,72,3584]{2,1,0:T(8,128)S(1)} %collective-permute-done.9, f32[2,72,3584]{2,1,0:T(8,128)S(1)} %collective-permute-done.10, ...), kind=kLoop, calls=%fused_computation.48 | loop fusion | flops 3612672 | bytes 16515072 | tf_op jit(solution)/shard_map/add | solution.py:134
  269.8 1.0 fusion.43
  270.7 1.0 fusion.47
  271.7 1.2 fusion.45
  272.9 1.2 fusion.49
  (52 shorter events, 8.6 us)
Async XLA Ops:
  0.6 29.1 %copy-start.3 = (s32[1,72]{1,0:T(1,128)S(1)}, s32[1,72]{1,0:T(1,128)}, u32[]{:S(2)}) copy-start(s32[1,72]{1,0:T(1,128)} %param.5) | copy-start | bytes 868
  4.7 51.5 %collective-permute-start = (bf16[2,72,3584]{2,1,0:T(8,128)(2,1)S(1)}, bf16[2,72,3584]{2,1,0:T(8,128)(2,1)S(1)}, u32[]{:S(2)}, u32[]{:S(2)}) collective-permute-start(bf16[2,72,3584]{2,1,0:T(8,128)(2,1)S(1)} %pad_maximum_fusion.6), channel_id=1, source_target_pairs={{0,3},{1,4},{2,5},{3,6},{4,7},{5,8},{6,9},{7,10},{8,11},{9,12},{10... | collective-permute-start | bytes 3096584 | tf_op jit(solution)/shard_map/ppermute | solution.py:16
  11.9 65.0 %collective-permute-start.1 = (bf16[2,72,3584]{2,1,0:T(8,128)(2,1)S(1)}, bf16[2,72,3584]{2,1,0:T(8,128)(2,1)S(1)}, u32[]{:S(2)}, u32[]{:S(2)}) collective-permute-start(bf16[2,72,3584]{2,1,0:T(8,128)(2,1)S(1)} %pad_maximum_fusion.6), channel_id=1, source_target_pairs={{0,2},{1,3},{2,4},{3,5},{4,6},{5,7},{6,8},{7,9},{8,10},{9,11},{10,... | collective-permute-start | bytes 3096584 | tf_op jit(solution)/shard_map/ppermute | solution.py:16
  15.9 62.9 %collective-permute-start.2 = (bf16[2,72,3584]{2,1,0:T(8,128)(2,1)S(1)}, bf16[2,72,3584]{2,1,0:T(8,128)(2,1)S(1)}, u32[]{:S(2)}, u32[]{:S(2)}) collective-permute-start(bf16[2,72,3584]{2,1,0:T(8,128)(2,1)S(1)} %pad_maximum_fusion.6), channel_id=1, source_target_pairs={{0,1},{1,2},{2,3},{3,4},{4,5},{5,6},{6,7},{7,8},{8,9},{9,10},{10,1... | collective-permute-start | bytes 3096584 | tf_op jit(solution)/shard_map/ppermute | solution.py:16
  18.1 60.9 %collective-permute-start.3 = (bf16[2,72,3584]{2,1,0:T(8,128)(2,1)S(1)}, bf16[2,72,3584]{2,1,0:T(8,128)(2,1)S(1)}, u32[]{:S(2)}, u32[]{:S(2)}) collective-permute-start(bf16[2,72,3584]{2,1,0:T(8,128)(2,1)S(1)} %pad_maximum_fusion.6), channel_id=1, source_target_pairs={{0,511},{1,0},{2,1},{3,2},{4,3},{5,4},{6,5},{7,6},{8,7},{9,8},{10,... | collective-permute-start | bytes 3096584 | tf_op jit(solution)/shard_map/ppermute | solution.py:16
  20.3 58.8 %collective-permute-start.4 = (bf16[2,72,3584]{2,1,0:T(8,128)(2,1)S(1)}, bf16[2,72,3584]{2,1,0:T(8,128)(2,1)S(1)}, u32[]{:S(2)}, u32[]{:S(2)}) collective-permute-start(bf16[2,72,3584]{2,1,0:T(8,128)(2,1)S(1)} %pad_maximum_fusion.6), channel_id=1, source_target_pairs={{0,510},{1,511},{2,0},{3,1},{4,2},{5,3},{6,4},{7,5},{8,6},{9,7},{1... | collective-permute-start | bytes 3096584 | tf_op jit(solution)/shard_map/ppermute | solution.py:16
  56.3 37.3 %collective-permute-start.5 = (bf16[2,72,3584]{2,1,0:T(8,128)(2,1)S(1)}, bf16[2,72,3584]{2,1,0:T(8,128)(2,1)S(1)}, u32[]{:S(2)}, u32[]{:S(2)}) collective-permute-start(bf16[2,72,3584]{2,1,0:T(8,128)(2,1)S(1)} %pad_maximum_fusion.6), channel_id=1, source_target_pairs={{0,509},{1,510},{2,511},{3,0},{4,1},{5,2},{6,3},{7,4},{8,5},{9,6},... | collective-permute-start | bytes 3096584 | tf_op jit(solution)/shard_map/ppermute | solution.py:16
  79.0 14.6 %copy-start = (bf16[72,3584]{1,0:T(8,128)(2,1)S(1)}, bf16[72,3584]{1,0:T(8,128)(2,1)}, u32[]{:S(2)}) copy-start(bf16[72,3584]{1,0:T(8,128)(2,1)} %param.3) | copy-start | bytes 1548292
  79.2 15.7 %copy-start.1 = (bf16[72,3584]{1,0:T(8,128)(2,1)S(1)}, bf16[72,3584]{1,0:T(8,128)(2,1)}, u32[]{:S(2)}) copy-start(bf16[72,3584]{1,0:T(8,128)(2,1)} %param.4) | copy-start | bytes 1548292
  104.4 76.7 %collective-permute-start.11 = (f32[2,72,3584]{2,1,0:T(8,128)S(1)}, f32[2,72,3584]{2,1,0:T(8,128)S(1)}, u32[]{:S(2)}, u32[]{:S(2)}) collective-permute-start(f32[2,72,3584]{2,1,0:T(8,128)S(1)} %pad_maximum_fusion.5), channel_id=1, source_target_pairs={{0,509},{1,510},{2,511},{3,0},{4,1},{5,2},{6,3},{7,4},{8,5},{9,6},... | collective-permute-start | bytes 6193160 | tf_op jit(solution)/shard_map/ppermute | solution.py:16
  116.2 84.4 %collective-permute-start.9 = (f32[2,72,3584]{2,1,0:T(8,128)S(1)}, f32[2,72,3584]{2,1,0:T(8,128)S(1)}, u32[]{:S(2)}, u32[]{:S(2)}) collective-permute-start(f32[2,72,3584]{2,1,0:T(8,128)S(1)} %pad_maximum_fusion.3), channel_id=1, source_target_pairs={{0,511},{1,0},{2,1},{3,2},{4,3},{5,4},{6,5},{7,6},{8,7},{9,8},{10,... | collective-permute-start | bytes 6193160 | tf_op jit(solution)/shard_map/ppermute | solution.py:16
  119.8 118.3 %collective-permute-start.10 = (f32[2,72,3584]{2,1,0:T(8,128)S(1)}, f32[2,72,3584]{2,1,0:T(8,128)S(1)}, u32[]{:S(2)}, u32[]{:S(2)}) collective-permute-start(f32[2,72,3584]{2,1,0:T(8,128)S(1)} %pad_maximum_fusion.4), channel_id=1, source_target_pairs={{0,510},{1,511},{2,0},{3,1},{4,2},{5,3},{6,4},{7,5},{8,6},{9,7},{1... | collective-permute-start | bytes 6193160 | tf_op jit(solution)/shard_map/ppermute | solution.py:16
  122.9 115.2 %collective-permute-start.8 = (f32[2,72,3584]{2,1,0:T(8,128)S(1)}, f32[2,72,3584]{2,1,0:T(8,128)S(1)}, u32[]{:S(2)}, u32[]{:S(2)}) collective-permute-start(f32[2,72,3584]{2,1,0:T(8,128)S(1)} %pad_maximum_fusion.2), channel_id=1, source_target_pairs={{0,3},{1,4},{2,5},{3,6},{4,7},{5,8},{6,9},{7,10},{8,11},{9,12},{10... | collective-permute-start | bytes 6193160 | tf_op jit(solution)/shard_map/ppermute | solution.py:16
  128.2 110.0 %collective-permute-start.6 = (f32[2,72,3584]{2,1,0:T(8,128)S(1)}, f32[2,72,3584]{2,1,0:T(8,128)S(1)}, u32[]{:S(2)}, u32[]{:S(2)}) collective-permute-start(f32[2,72,3584]{2,1,0:T(8,128)S(1)} %pad_maximum_fusion), channel_id=1, source_target_pairs={{0,1},{1,2},{2,3},{3,4},{4,5},{5,6},{6,7},{7,8},{8,9},{9,10},{10,1... | collective-permute-start | bytes 6193160 | tf_op jit(solution)/shard_map/ppermute | solution.py:16
  181.2 84.9 %collective-permute-start.7 = (f32[2,72,3584]{2,1,0:T(8,128)S(1)}, f32[2,72,3584]{2,1,0:T(8,128)}, u32[]{:S(2)}, u32[]{:S(2)}) collective-permute-start(f32[2,72,3584]{2,1,0:T(8,128)S(1)} %pad_maximum_fusion.1), channel_id=1, source_target_pairs={{0,2},{1,3},{2,4},{3,5},{4,6},{5,7},{6,8},{7,9},{8,10},{9,11},{10,... | collective-permute-start | bytes 6193160 | tf_op jit(solution)/shard_map/ppermute | solution.py:16
  238.2 1.3 copy-start.2
where the time goes:
time: 275 us; the launch traced here: 274 us
  waiting for transfers between devices  174 us (63%)
  starting transfers between devices  65 us (24%)
  matrix products  20.1 us (7%)
  other arithmetic  12.3 us (4%)
    ppermute x12, waiting for transfers between devices, passed_along(): return lax.ppermute(value, axis, pairs)  174 us
    ppermute x12, starting transfers between devices, passed_along(): return lax.ppermute(value, axis, pairs)  65 us
    dot_general x28, matrix products, reverse_apply(): lax.dot_general(weight_rows, row_data, (((0,), (0,)), ((), ())), preferre...  11.5 us
  transfers between devices with their start and end apart: 12, of which 8 were waited for; matrix products, arithmetic and copies ran while one was open for 4% of the time, Pallas kernels for 0%

commit v1 on v0

v1 whole, which is shorter than its diff:
```python
import jax
import jax.numpy as jnp
from jax import lax
from jax.experimental import pallas as pl
from jax.experimental.pallas import tpu as pltpu
from jax.sharding import PartitionSpec as P

INV_TEMP = 20.0
EPS = 1e-06
TILE = 896
VMEM = pl.BlockSpec(memory_space=pltpu.VMEM)
HBM = pl.BlockSpec(memory_space=pl.ANY)


def contract(left_rows, right_rows):
    return lax.dot_general(
        left_rows, right_rows, (((1,), (1,)), ((), ())), preferred_element_type=jnp.float32
    )


def exp_score(score):
    return jnp.exp(INV_TEMP * score - INV_TEMP)


def eye_of(count):
    down = lax.broadcasted_iota(jnp.int32, (count, count), 0)
    across = lax.broadcasted_iota(jnp.int32, (count, count), 1)
    return (down == across).astype(jnp.float32)


def unit_kernel(query_any, passage_any, low_ref, scale_ref, query_ref, passage_ref, sems):
    copies = [
        pltpu.make_async_copy(query_any, query_ref, sems.at[0]),
        pltpu.make_async_copy(passage_any, passage_ref, sems.at[1]),
    ]
    for copy in copies:
        copy.start()
    for copy in copies:
        copy.wait()
    raw_rows = jnp.concatenate(
        [query_ref[...].astype(jnp.float32), passage_ref[...].astype(jnp.float32)], axis=0
    )
    scale_rows = lax.rsqrt(jnp.sum(raw_rows * raw_rows, axis=1, keepdims=True) + EPS)
    low_ref[...] = (raw_rows * scale_rows).astype(jnp.bfloat16)
    scale_ref[...] = scale_rows


def unit_rows(query_raw, passage_raw):
    rows, width = query_raw.shape
    return pl.pallas_call(
        unit_kernel,
        in_specs=[HBM, HBM],
        out_specs=(VMEM, VMEM),
        out_shape=(
            jax.ShapeDtypeStruct((2 * rows, width), jnp.bfloat16),
            jax.ShapeDtypeStruct((2 * rows, 1), jnp.float32),
        ),
        scratch_shapes=[
            pltpu.VMEM((rows, width), jnp.bfloat16),
            pltpu.VMEM((rows, width), jnp.bfloat16),
            pltpu.SemaphoreType.DMA((2,)),
        ],
        compiler_params=pltpu.CompilerParams(vmem_limit_bytes=121 * 2**19),
        cost_estimate=pl.CostEstimate(
            flops=6 * rows * width, bytes_accessed=8 * rows * width, transcendentals=0
        ),
        name="unit_rows",
    )(query_raw, passage_raw)


def first_far_kernel(own_ref, far_ref, mass_ref, score_ref, passed_ref):
    score_ref[...] = contract(own_ref[...], far_ref[...])
    passed_ref[...] = mass_ref[...]


def first_far(own, far, mass):
    count, width = own.shape
    square = jax.ShapeDtypeStruct((count, count), jnp.float32)
    return pl.pallas_call(
        first_far_kernel,
        in_specs=[VMEM] * 3,
        out_specs=(VMEM, VMEM),
        out_shape=(square, square),
        compiler_params=pltpu.CompilerParams(vmem_limit_bytes=16 * 2**20),
        cost_estimate=pl.CostEstimate(
            flops=2 * count * count * width, bytes_accessed=4 * count * width, transcendentals=0
        ),
        name="first_far",
    )(own, far, mass)


def total_kernel(
    partner_ref, own_ref, mate_ref, far_ref, far_score_ref, score_ref, mass_ref,
    mate_score_out, far_score_out, recip_ref, loss_ref,
):
    partner = partner_ref[...]
    eye = eye_of(partner.shape[0])
    own = own_ref[...]
    mate_score = contract(own, mate_ref[...])
    far_score = far_score_ref[...] + contract(own, far_ref[...])
    mate_score_out[...] = mate_score
    far_score_out[...] = far_score
    mass = mass_ref[...] + exp_score(mate_score) + exp_score(far_score)
    total_col = jnp.sum(mass, axis=1, keepdims=True)
    norm_row = jnp.sum((eye + partner) * total_col, axis=0, keepdims=True)
    recip_ref[...] = 1.0 / norm_row
    positive = jnp.sum(partner * score_ref[...], axis=0, keepdims=True)
    losses = jnp.log(norm_row) + INV_TEMP - INV_TEMP * positive
    loss_ref[...] = losses[:, : loss_ref.shape[1]]


def totals(partner, own, next_mate, far_second, far_score, own_score, mass):
    count, width = own.shape
    row = jax.ShapeDtypeStruct((1, count), jnp.float32)
    half_row = jax.ShapeDtypeStruct((1, count // 2), jnp.float32)
    square = jax.ShapeDtypeStruct((count, count), jnp.float32)
    return pl.pallas_call(
        total_kernel,
        in_specs=[VMEM] * 7,
        out_specs=(VMEM,) * 4,
        out_shape=(square, square, row, half_row),
        compiler_params=pltpu.CompilerParams(vmem_limit_bytes=16 * 2**20),
        cost_estimate=pl.CostEstimate(
            flops=4 * count * count * width,
            bytes_accessed=6 * count * width,
            transcendentals=2 * count * count,
        ),
        name="totals",
    )(partner, own, next_mate, far_second, far_score, own_score, mass)


def gradient_kernel(blocks, refs):
    partner_ref, scale_ref, own_row, mate_row, near_rows, next_rows, relay_rows = refs[:7]
    score_refs = refs[7 : 7 + blocks]
    key_refs = refs[7 + blocks : 8 + 2 * blocks]
    query_ref, passage_ref, query_out, passage_out, weight_ref, dot_ref = refs[8 + 2 * blocks :]
    count = partner_ref.shape[0]
    rows = count // 2
    step = pl.program_id(0)

    @pl.when(step == 0)
    def _():
        partner = partner_ref[...]
        eye = eye_of(count)
        recip_col = jnp.sum(eye * own_row[...], axis=1, keepdims=True)
        relayed = relay_rows[1:2, :]
        recip_rows = [
            own_row[...],
            mate_row[...],
            near_rows[0:1, :],
            near_rows[1:2, :],
            next_rows[0:1, :],
            next_rows[1:2, :],
            jnp.where(relayed > 0.0, relayed, next_rows[3:4, :]),
        ]
        along = jnp.zeros((count, count), jnp.float32)
        weights = []
        for index in range(blocks):
            score = score_refs[index][...]
            weight = exp_score(score) * (recip_col + recip_rows[index])
            if index == 0:
                weight = weight * (1.0 - eye) * (1.0 - 0.5 * partner) - partner
            low = weight.astype(jnp.bfloat16)
            along = along + low.astype(jnp.float32) * score
            weights.append(low)
        weight_ref[...] = jnp.concatenate(weights, axis=1)
        dot_ref[...] = INV_TEMP * jnp.sum(along, axis=1, keepdims=True)

    columns = pl.ds(pl.multiple_of(step * TILE, TILE), TILE)
    near_keys = [key_ref[:, columns] for key_ref in key_refs[: blocks - 1]]
    far_keys = key_refs[blocks - 1][:, columns] + key_refs[blocks][:, columns]
    keys = jnp.concatenate(near_keys + [far_keys], axis=0)
    gradient = jnp.dot(weight_ref[...], keys, preferred_element_type=jnp.float32)
    scale = scale_ref[...]
    along = dot_ref[...]
    for part, raw_ref, out_ref in ((0, query_ref, query_out), (1, passage_ref, passage_out)):
        span = slice(part * rows, (part + 1) * rows)
        unit = raw_ref[:, columns].astype(jnp.float32) * scale[span]
        out_ref[...] = (INV_TEMP * gradient[span] - unit * along[span]) * scale[span]


def gradients(partner, scale, recip_rows, scores, keys, query_raw, passage_raw):
    blocks = len(scores)
    rows, width = query_raw.shape
    count = 2 * rows
    out = jax.ShapeDtypeStruct((rows, width), jnp.float32)
    out_spec = pl.BlockSpec((rows, TILE), lambda step: (0, step))

    def body(*refs):
        gradient_kernel(blocks, refs)

    return pl.pallas_call(
        body,
        out_shape=(out, out),
        grid=(width // TILE,),
        in_specs=[VMEM] * (10 + 2 * blocks),
        out_specs=(out_spec, out_spec),
        scratch_shapes=[
            pltpu.VMEM((count, blocks * count), jnp.bfloat16),
            pltpu.VMEM((count, 1), jnp.float32),
        ],
        compiler_params=pltpu.CompilerParams(vmem_limit_bytes=32 * 2**20),
        cost_estimate=pl.CostEstimate(
            flops=2 * blocks * count * count * width,
            bytes_accessed=2 * blocks * count * width + 12 * rows * width,
            transcendentals=blocks * count * count,
        ),
        name="gradients",
    )(partner, scale, *recip_rows, *scores, *keys, query_raw, passage_raw)


def per_device(query_raw, passage_raw, pairing):
    size = lax.axis_size("dp")
    chips = size // 2
    rows = query_raw.shape[0]

    def swapped(value, partner_of):
        pairs = []
        for source in range(size):
            target = partner_of(source // 2, source % 2)
            if target is not None:
                pairs.append((source, (target[0] % chips) * 2 + target[1]))
        return lax.ppermute(value, "dp", pairs)

    def other_core(chip, core):
        return (chip, 1 - core)

    def near_chip(chip, core):
        return (chip ^ 1, core)

    def next_chip(chip, core):
        return (chip + 1 if chip % 2 else chip - 1, core)

    def far_over_next(chip, core):
        return (chip + 1 if core else chip - 1, 1 - core) if chip % 2 == core else None

    def far_over_near(chip, core):
        return (chip + 1 if core else chip - 1, 1 - core) if chip % 2 != core else None

    def near_from_direct(chip, core):
        return (chip ^ 1, core) if chip % 2 == core else None

    own, scale = unit_rows(query_raw, passage_raw)
    paired = (pairing[0][:, None] == jnp.arange(rows, dtype=jnp.int32)[None, :]).astype(jnp.float32)
    blank = jnp.zeros((rows, rows), jnp.float32)
    partner = jnp.block([[blank, paired], [paired.T, blank]])
    passage_row = jnp.arange(2 * rows)[:, None] >= rows
    keep = 1.0 - jnp.eye(2 * rows, dtype=jnp.float32) - jnp.where(passage_row, partner, 0.0)

    near = swapped(own, near_chip)
    next_block = swapped(own, next_chip)
    mate = swapped(own, other_core)
    far_first = swapped(near, far_over_next)
    near_mate = swapped(near, other_core)
    far_second = swapped(next_block, far_over_near)
    next_mate = swapped(next_block, other_core)

    keys = [own, mate, near, near_mate, next_block]
    scores = [contract(own, key) for key in keys]
    mass = exp_score(scores[0]) * keep
    for score in scores[1:]:
        mass = mass + exp_score(score)
    far_score, mass = first_far(own, far_first, mass)
    mate_score, far_score, recip, losses = totals(
        partner, own, next_mate, far_second, far_score, scores[0], mass
    )

    mate_row = swapped(recip, other_core)
    chip_rows = jnp.concatenate([recip, mate_row], axis=0)
    near_rows = swapped(chip_rows, near_chip)
    next_rows = swapped(jnp.concatenate([chip_rows, near_rows], axis=0), next_chip)
    relay_rows = swapped(next_rows, near_from_direct)

    query_grad, passage_grad = gradients(
        partner,
        scale,
        [recip, mate_row, near_rows, next_rows, relay_rows],
        scores + [mate_score, far_score],
        keys + [next_mate, far_first, far_second],
        query_raw,
        passage_raw,
    )
    return (losses.reshape(rows), query_grad, passage_grad)


def solution(mesh):
    in_specs = (P("dp", None), P("dp", None), P("dp", None))
    out_specs = (P("dp"), P("dp", None), P("dp", None))
    return jax.shard_map(
        per_device, mesh=mesh, in_specs=in_specs, out_specs=out_specs, check_vma=False
    )
```

time: 275 us -> 91.6 us (0.33)
  waiting for transfers between devices: 174 us -> 19.9 us
  matrix products: 20.1 us -> 4.11 us
  other arithmetic: 12.3 us -> 0.19 us
  Pallas kernels: 0 us -> 8.1 us
  starting transfers between devices: 65 us -> 58 us
    ppermute x12 -> x11, waiting for transfers between devices: 174 us -> 19.9 us  [swapped(): return lax.ppermute(value, 'dp', pairs)]
    dot_general x32 -> x0, matrix products: 15 us -> none  [the longest x28 11.5 us: reverse_apply(): lax.dot_general(weight_rows, row_data, (((0,), (0,)), ((), ())), preferre...]
    pallas_call x0 -> x4, Pallas kernels: none -> 8.1 us  [the longest x1 3.7 us: gradients(): pl.pallas_call(body, out_shape=(out, out), grid=(width // TILE,), in_spec...]
    ppermute x12 -> x11, starting transfers between devices: 65 us -> 58 us  [swapped(): return lax.ppermute(value, 'dp', pairs)]
    add x2 -> x0, other arithmetic: 3.67 us -> none  [the longest x1 3.66 us: per_device(): home_sum(ahead_parts, 1, grad_move) + home_sum(behind_parts, -1, grad_move)]
    reduce_sum x4 -> x0, other arithmetic: 2.86 us -> none  [the longest x2 2.49 us: unit_rows(): jnp.sum(widened * widened, axis=1, keepdims=True) + EPS]
  transfers between devices with their start and end apart: 12 -> 11, of which waited for: 8 -> 7; matrix products, arithmetic and copies ran while one was open for 4% -> 5% of each run, Pallas kernels for 0% -> 0%
where the time goes in v1:
time: 91.6 us; the launch traced here: 91.2 us
  starting transfers between devices  58 us (63%)
  waiting for transfers between devices  19.9 us (22%)
  Pallas kernels  8.1 us (9%)
  matrix products  4.11 us (4%)
    ppermute x11, starting transfers between devices, swapped(): return lax.ppermute(value, 'dp', pairs)  58 us
    ppermute x11, waiting for transfers between devices, swapped(): return lax.ppermute(value, 'dp', pairs)  19.9 us
    dot_general x5, matrix products, contract(): lax.dot_general(left_rows, right_rows, (((1,), (1,)), ((), ())), preferre...  4.11 us
    pallas_call x1, Pallas kernels, gradients(): pl.pallas_call(body, out_shape=(out, out), grid=(width // TILE,), in_spec...  3.7 us
    pallas_call x1, Pallas kernels, unit_rows(): pl.pallas_call(unit_kernel, in_specs=[HBM, HBM], out_specs=(VMEM, VMEM),...  2.61 us
  transfers between devices with their start and end apart: 11, of which 7 were waited for; matrix products, arithmetic and copies ran while one was open for 5% of the time, Pallas kernels for 0%

profile of v1, /device:TPU:1, one launch (start us, length us, event | category | flops | bytes accessed | tf_op | source)
XLA Modules:
  0.0 91.2 jit_solution(13945596781018094675)
XLA Ops:
  0.6 2.6 %unit_rows.1 = (bf16[144,3584]{1,0:T(8,128)(2,1)}, f32[144,1]{1,0:T(8,128)}) custom-call(bf16[72,3584]{1,0:T(8,128)(2,1)} %refs_22_.1, bf16[72,3584]{1,0:T(8,128)(2,1)} %refs_23_.1), custom_call_target="tpu_custom_call" | custom-call | flops 1548288 | bytes 2064384 | tf_op jit(solution)/shard_map/unit_rows/pallas_call | solution.py:50
  3.2 0.0 copy-start.4
  3.3 4.8 %collective-permute-start.3 = (bf16[144,3584]{1,0:T(8,128)(2,1)}, bf16[144,3584]{1,0:T(8,128)(2,1)S(1)}, u32[]{:S(2)}, u32[]{:S(2)}) collective-permute-start(bf16[144,3584]{1,0:T(8,128)(2,1)} %get-tuple-element.13.own_ref.refs_14_), channel_id=1, source_target_pairs={{0,2},{1,3},{2,0},{3,1},{4,6},{5,7},{6,4},{7,5},{8,10},{9,11},{10,... | collective-permute-start | bytes 3096584 | tf_op jit(solution)/shard_map/ppermute | solution.py:223
  8.1 13.9 %collective-permute-start = (bf16[144,3584]{1,0:T(8,128)(2,1)}, bf16[144,3584]{1,0:T(8,128)(2,1)S(1)}, u32[]{:S(2)}, u32[]{:S(2)}) collective-permute-start(bf16[144,3584]{1,0:T(8,128)(2,1)} %get-tuple-element.13.own_ref.refs_14_), channel_id=1, source_target_pairs={{0,510},{1,511},{2,4},{3,5},{4,2},{5,3},{6,8},{7,9},{8,6},{9,7},{1... | collective-permute-start | bytes 3096584 | tf_op jit(solution)/shard_map/ppermute | solution.py:223
  22.1 3.1 %collective-permute-start.5 = (bf16[144,3584]{1,0:T(8,128)(2,1)}, bf16[144,3584]{1,0:T(8,128)(2,1)S(1)}, u32[]{:S(2)}, u32[]{:S(2)}) collective-permute-start(bf16[144,3584]{1,0:T(8,128)(2,1)} %get-tuple-element.13.own_ref.refs_14_), channel_id=1, source_target_pairs={{0,1},{1,0},{2,3},{3,2},{4,5},{5,4},{6,7},{7,6},{8,9},{9,8},{10,11... | collective-permute-start | bytes 3096584 | tf_op jit(solution)/shard_map/ppermute | solution.py:223
  25.2 0.0 copy-done.4
  25.2 0.1 iota_compare_fusion.2
  25.3 1.5 %collective-permute-done.3.refs_16_ = bf16[144,3584]{1,0:T(8,128)(2,1)S(1)} collective-permute-done((bf16[144,3584]{1,0:T(8,128)(2,1)}, bf16[144,3584]{1,0:T(8,128)(2,1)S(1)}, u32[]{:S(2)}, u32[]{:S(2)}) %collective-permute-start.3) | collective-permute-done | bytes 1032224 | tf_op jit(solution)/shard_map/ppermute | solution.py:223
  26.8 7.2 %collective-permute-start.6 = (bf16[144,3584]{1,0:T(8,128)(2,1)S(1)}, bf16[144,3584]{1,0:T(8,128)(2,1)S(1)}, u32[]{:S(2)}, u32[]{:S(2)}) collective-permute-start(bf16[144,3584]{1,0:T(8,128)(2,1)S(1)} %collective-permute-done.3.refs_16_), channel_id=1, source_target_pairs={{0,1},{1,0},{2,3},{3,2},{4,5},{5,4},{6,7},{7,6},{8,9},{9,8},{10,11... | collective-permute-start | bytes 3096584 | tf_op jit(solution)/shard_map/ppermute | solution.py:223
  34.0 0.1 fusion.partner_ref.refs_0_
  34.1 0.0 copy-start
  34.1 2.3 %fusion.1.score_ref.refs_7_ = f32[144,144]{1,0:T(8,128)S(1)} fusion(bf16[144,3584]{1,0:T(8,128)(2,1)} %get-tuple-element.13.own_ref.refs_14_), kind=kOutput, calls=%fused_computation.9 | convolution fusion | flops 148635648 | bytes 1115136 | tf_op jit(solution)/shard_map/dot_general | solution.py:16
  36.4 0.7 collective-permute-start.4
  37.1 7.3 %collective-permute-done.refs_18_ = bf16[144,3584]{1,0:T(8,128)(2,1)S(1)} collective-permute-done((bf16[144,3584]{1,0:T(8,128)(2,1)}, bf16[144,3584]{1,0:T(8,128)(2,1)S(1)}, u32[]{:S(2)}, u32[]{:S(2)}) %collective-permute-start) | collective-permute-done | bytes 1032224 | tf_op jit(solution)/shard_map/ppermute | solution.py:223
  44.5 1.9 %collective-permute-start.2 = (bf16[144,3584]{1,0:T(8,128)(2,1)S(1)}, bf16[144,3584]{1,0:T(8,128)(2,1)S(1)}, u32[]{:S(2)}, u32[]{:S(2)}) collective-permute-start(bf16[144,3584]{1,0:T(8,128)(2,1)S(1)} %collective-permute-done.refs_18_), channel_id=1, source_target_pairs={{1,2},{2,1},{5,6},{6,5},{9,10},{10,9},{13,14},{14,13},{17,18},{18,... | collective-permute-start | bytes 3096584 | tf_op jit(solution)/shard_map/ppermute | solution.py:223
  46.4 8.2 %collective-permute-start.1 = (bf16[144,3584]{1,0:T(8,128)(2,1)S(1)}, bf16[144,3584]{1,0:T(8,128)(2,1)S(1)}, u32[]{:S(2)}, u32[]{:S(2)}) collective-permute-start(bf16[144,3584]{1,0:T(8,128)(2,1)S(1)} %collective-permute-done.refs_18_), channel_id=1, source_target_pairs={{0,1},{1,0},{2,3},{3,2},{4,5},{5,4},{6,7},{7,6},{8,9},{9,8},{10,11... | collective-permute-start | bytes 3096584 | tf_op jit(solution)/shard_map/ppermute | solution.py:223
  54.6 0.0 copy-done
  54.6 0.4 fusion.3.refs_9_
  55.0 0.0 collective-permute-done.5.refs_15_
  55.1 0.4 fusion.2.refs_8_
  55.5 0.0 collective-permute-done.6.refs_17_
  55.5 0.4 fusion.4.refs_10_
  55.9 0.5 exponential_add_fusion
  56.4 0.0 collective-permute-done.4.far_ref.refs_20_
  56.5 0.4 first_far.1
  56.9 3.8 %collective-permute-done.2.far_ref.refs_21_ = bf16[144,3584]{1,0:T(8,128)(2,1)S(1)} collective-permute-done((bf16[144,3584]{1,0:T(8,128)(2,1)S(1)}, bf16[144,3584]{1,0:T(8,128)(2,1)S(1)}, u32[]{:S(2)}, u32[]{:S(2)}) %collective-permute-start.2) | collective-permute-done | bytes 1032224 | tf_op jit(solution)/shard_map/ppermute | solution.py:223
  60.7 0.0 collective-permute-done.1.mate_ref.refs_19_
  60.7 0.0 copy-start.1
  60.7 0.0 copy-start.2
  60.7 0.0 copy-start.3
  60.7 1.4 %totals.1 = (f32[144,144]{1,0:T(8,128)S(1)}, f32[144,144]{1,0:T(8,128)S(1)}, f32[1,144]{1,0:T(1,128)S(1)}, f32[1,72]{1,0:T(1,128)}) custom-call(f32[144,144]{1,0:T(8,128)S(1)} %fusion.partner_ref.refs_0_, bf16[144,3584]{1,0:T(8,128)(2,1)S(1)} %copy-done, bf16[144,3584]{1,0:T(8,128)(2,1)S(1)} %collective-permute-done.1.mate_ref.refs_19_, ...), custom_call_target="tpu_custom_call" | custom-call | flops 297271296 | bytes 3096576 | tf_op jit(solution)/shard_map/totals/pallas_call | solution.py:117
  62.1 5.9 %collective-permute-start.7 = (f32[1,144]{1,0:T(1,128)S(1)}, f32[1,144]{1,0:T(1,128)S(1)}, u32[]{:S(2)}, u32[]{:S(2)}) collective-permute-start(f32[1,144]{1,0:T(1,128)S(1)} %get-tuple-element.18.refs_2_), channel_id=1, source_target_pairs={{0,1},{1,0},{2,3},{3,2},{4,5},{5,4},{6,7},{7,6},{8,9},{9,8},{10,11... | collective-permute-start | bytes 1736 | tf_op jit(solution)/shard_map/ppermute | solution.py:223
  68.0 0.8 collective-permute-done.7.refs_3_
  68.8 1.9 %collective-permute-start.8 = (f32[2,144]{1,0:T(2,128)S(1)}, f32[2,144]{1,0:T(2,128)S(1)}, u32[]{:S(2)}, u32[]{:S(2)}) collective-permute-start(f32[2,144]{1,0:T(2,128)S(1)} %pad_maximum_fusion.1), channel_id=1, source_target_pairs={{0,2},{1,3},{2,0},{3,1},{4,6},{5,7},{6,4},{7,5},{8,10},{9,11},{10,... | collective-permute-start | bytes 3464 | tf_op jit(solution)/shard_map/ppermute | solution.py:223
  70.7 2.4 %collective-permute-done.8.refs_4_ = f32[2,144]{1,0:T(2,128)S(1)} collective-permute-done((f32[2,144]{1,0:T(2,128)S(1)}, f32[2,144]{1,0:T(2,128)S(1)}, u32[]{:S(2)}, u32[]{:S(2)}) %collective-permute-start.8) | collective-permute-done | bytes 1184 | tf_op jit(solution)/shard_map/ppermute | solution.py:223
  73.1 9.0 %collective-permute-start.9 = (f32[4,144]{1,0:T(4,128)S(1)}, f32[4,144]{1,0:T(4,128)S(1)}, u32[]{:S(2)}, u32[]{:S(2)}) collective-permute-start(f32[4,144]{1,0:T(4,128)S(1)} %pad_maximum_fusion), channel_id=1, source_target_pairs={{0,510},{1,511},{2,4},{3,5},{4,2},{5,3},{6,8},{7,9},{8,6},{9,7},{1... | collective-permute-start | bytes 6920 | tf_op jit(solution)/shard_map/ppermute | solution.py:223
  82.1 1.0 %collective-permute-done.9.refs_5_ = f32[4,144]{1,0:T(4,128)S(1)} collective-permute-done((f32[4,144]{1,0:T(4,128)S(1)}, f32[4,144]{1,0:T(4,128)S(1)}, u32[]{:S(2)}, u32[]{:S(2)}) %collective-permute-start.9) | collective-permute-done | bytes 2336 | tf_op jit(solution)/shard_map/ppermute | solution.py:223
  83.1 1.3 %collective-permute-start.10 = (f32[4,144]{1,0:T(4,128)S(1)}, f32[4,144]{1,0:T(4,128)S(1)}, u32[]{:S(2)}, u32[]{:S(2)}) collective-permute-start(f32[4,144]{1,0:T(4,128)S(1)} %collective-permute-done.9.refs_5_), channel_id=1, source_target_pairs={{0,2},{3,1},{4,6},{7,5},{8,10},{11,9},{12,14},{15,13},{16,18},{19,... | collective-permute-start | bytes 6920 | tf_op jit(solution)/shard_map/ppermute | solution.py:223
  84.4 3.1 %collective-permute-done.10.refs_6_ = f32[4,144]{1,0:T(4,128)S(1)} collective-permute-done((f32[4,144]{1,0:T(4,128)S(1)}, f32[4,144]{1,0:T(4,128)S(1)}, u32[]{:S(2)}, u32[]{:S(2)}) %collective-permute-start.10) | collective-permute-done | bytes 2336 | tf_op jit(solution)/shard_map/ppermute | solution.py:223
  87.5 0.0 copy-done.1
  87.5 0.0 copy-done.2
  87.5 0.0 copy-done.3
  87.5 3.7 %gradients.1 = (f32[72,3584]{1,0:T(8,128)}, f32[72,3584]{1,0:T(8,128)}) custom-call(f32[144,144]{1,0:T(8,128)S(1)} %fusion.partner_ref.refs_0_, f32[144,1]{1,0:T(8,128)S(1)} %copy-done.3, f32[1,144]{1,0:T(1,128)S(1)} %get-tuple-element.18.refs_2_, f32[1,144]{1,0:T(1,128)S(1)} %collective-permute-done.7.refs_3_, f32[2,144]{1,0:T(2,128)S(1)} %collective-permute-done.8.refs_4_, ...), custom_call_target="tpu_custom_call" | custom-call | flops 1040449536 | bytes 10321920 | tf_op jit(solution)/shard_map/gradients/pallas_call | solution.py:192
  (3 shorter events, 0.0 us)
Async XLA Ops:
  3.2 22.0 %copy-start.4 = (s32[1,72]{1,0:T(1,128)S(1)}, s32[1,72]{1,0:T(1,128)}, u32[]{:S(2)}) copy-start(s32[1,72]{1,0:T(1,128)} %param.5) | copy-start | bytes 868
  3.3 23.5 %collective-permute-start.3 = (bf16[144,3584]{1,0:T(8,128)(2,1)}, bf16[144,3584]{1,0:T(8,128)(2,1)S(1)}, u32[]{:S(2)}, u32[]{:S(2)}) collective-permute-start(bf16[144,3584]{1,0:T(8,128)(2,1)} %get-tuple-element.13.own_ref.refs_14_), channel_id=1, source_target_pairs={{0,2},{1,3},{2,0},{3,1},{4,6},{5,7},{6,4},{7,5},{8,10},{9,11},{10,... | collective-permute-start | bytes 3096584 | tf_op jit(solution)/shard_map/ppermute | solution.py:223
  8.1 36.4 %collective-permute-start = (bf16[144,3584]{1,0:T(8,128)(2,1)}, bf16[144,3584]{1,0:T(8,128)(2,1)S(1)}, u32[]{:S(2)}, u32[]{:S(2)}) collective-permute-start(bf16[144,3584]{1,0:T(8,128)(2,1)} %get-tuple-element.13.own_ref.refs_14_), channel_id=1, source_target_pairs={{0,510},{1,511},{2,4},{3,5},{4,2},{5,3},{6,8},{7,9},{8,6},{9,7},{1... | collective-permute-start | bytes 3096584 | tf_op jit(solution)/shard_map/ppermute | solution.py:223
  22.1 33.0 %collective-permute-start.5 = (bf16[144,3584]{1,0:T(8,128)(2,1)}, bf16[144,3584]{1,0:T(8,128)(2,1)S(1)}, u32[]{:S(2)}, u32[]{:S(2)}) collective-permute-start(bf16[144,3584]{1,0:T(8,128)(2,1)} %get-tuple-element.13.own_ref.refs_14_), channel_id=1, source_target_pairs={{0,1},{1,0},{2,3},{3,2},{4,5},{5,4},{6,7},{7,6},{8,9},{9,8},{10,11... | collective-permute-start | bytes 3096584 | tf_op jit(solution)/shard_map/ppermute | solution.py:223
  26.8 28.7 %collective-permute-start.6 = (bf16[144,3584]{1,0:T(8,128)(2,1)S(1)}, bf16[144,3584]{1,0:T(8,128)(2,1)S(1)}, u32[]{:S(2)}, u32[]{:S(2)}) collective-permute-start(bf16[144,3584]{1,0:T(8,128)(2,1)S(1)} %collective-permute-done.3.refs_16_), channel_id=1, source_target_pairs={{0,1},{1,0},{2,3},{3,2},{4,5},{5,4},{6,7},{7,6},{8,9},{9,8},{10,11... | collective-permute-start | bytes 3096584 | tf_op jit(solution)/shard_map/ppermute | solution.py:223
  34.1 20.5 %copy-start = (bf16[144,3584]{1,0:T(8,128)(2,1)S(1)}, bf16[144,3584]{1,0:T(8,128)(2,1)}, u32[]{:S(2)}) copy-start(bf16[144,3584]{1,0:T(8,128)(2,1)} %get-tuple-element.13.own_ref.refs_14_) | copy-start | bytes 3096580
  36.4 20.0 %collective-permute-start.4 = (bf16[144,3584]{1,0:T(8,128)(2,1)S(1)}, bf16[144,3584]{1,0:T(8,128)(2,1)S(1)}, u32[]{:S(2)}, u32[]{:S(2)}) collective-permute-start(bf16[144,3584]{1,0:T(8,128)(2,1)S(1)} %collective-permute-done.3.refs_16_), channel_id=1, source_target_pairs={{0,511},{3,4},{4,3},{7,8},{8,7},{11,12},{12,11},{15,16},{16,15},{1... | collective-permute-start | bytes 3096584 | tf_op jit(solution)/shard_map/ppermute | solution.py:223
  44.5 16.2 %collective-permute-start.2 = (bf16[144,3584]{1,0:T(8,128)(2,1)S(1)}, bf16[144,3584]{1,0:T(8,128)(2,1)S(1)}, u32[]{:S(2)}, u32[]{:S(2)}) collective-permute-start(bf16[144,3584]{1,0:T(8,128)(2,1)S(1)} %collective-permute-done.refs_18_), channel_id=1, source_target_pairs={{1,2},{2,1},{5,6},{6,5},{9,10},{10,9},{13,14},{14,13},{17,18},{18,... | collective-permute-start | bytes 3096584 | tf_op jit(solution)/shard_map/ppermute | solution.py:223
  46.4 14.3 %collective-permute-start.1 = (bf16[144,3584]{1,0:T(8,128)(2,1)S(1)}, bf16[144,3584]{1,0:T(8,128)(2,1)S(1)}, u32[]{:S(2)}, u32[]{:S(2)}) collective-permute-start(bf16[144,3584]{1,0:T(8,128)(2,1)S(1)} %collective-permute-done.refs_18_), channel_id=1, source_target_pairs={{0,1},{1,0},{2,3},{3,2},{4,5},{5,4},{6,7},{7,6},{8,9},{9,8},{10,11... | collective-permute-start | bytes 3096584 | tf_op jit(solution)/shard_map/ppermute | solution.py:223
  60.7 26.8 %copy-start.1 = (bf16[72,3584]{1,0:T(8,128)(2,1)S(1)}, bf16[72,3584]{1,0:T(8,128)(2,1)}, u32[]{:S(2)}) copy-start(bf16[72,3584]{1,0:T(8,128)(2,1)} %refs_22_.1) | copy-start | bytes 1548292
  60.7 26.8 %copy-start.2 = (bf16[72,3584]{1,0:T(8,128)(2,1)S(1)}, bf16[72,3584]{1,0:T(8,128)(2,1)}, u32[]{:S(2)}) copy-start(bf16[72,3584]{1,0:T(8,128)(2,1)} %refs_23_.1) | copy-start | bytes 1548292
  60.7 26.8 %copy-start.3 = (f32[144,1]{1,0:T(8,128)S(1)}, f32[144,1]{1,0:T(8,128)}, u32[]{:S(2)}) copy-start(f32[144,1]{1,0:T(8,128)} %get-tuple-element.17.refs_1_) | copy-start | bytes 1732
  62.1 6.7 %collective-permute-start.7 = (f32[1,144]{1,0:T(1,128)S(1)}, f32[1,144]{1,0:T(1,128)S(1)}, u32[]{:S(2)}, u32[]{:S(2)}) collective-permute-start(f32[1,144]{1,0:T(1,128)S(1)} %get-tuple-element.18.refs_2_), channel_id=1, source_target_pairs={{0,1},{1,0},{2,3},{3,2},{4,5},{5,4},{6,7},{7,6},{8,9},{9,8},{10,11... | collective-permute-start | bytes 1736 | tf_op jit(solution)/shard_map/ppermute | solution.py:223
  68.8 4.3 %collective-permute-start.8 = (f32[2,144]{1,0:T(2,128)S(1)}, f32[2,144]{1,0:T(2,128)S(1)}, u32[]{:S(2)}, u32[]{:S(2)}) collective-permute-start(f32[2,144]{1,0:T(2,128)S(1)} %pad_maximum_fusion.1), channel_id=1, source_target_pairs={{0,2},{1,3},{2,0},{3,1},{4,6},{5,7},{6,4},{7,5},{8,10},{9,11},{10,... | collective-permute-start | bytes 3464 | tf_op jit(solution)/shard_map/ppermute | solution.py:223
  73.1 10.0 %collective-permute-start.9 = (f32[4,144]{1,0:T(4,128)S(1)}, f32[4,144]{1,0:T(4,128)S(1)}, u32[]{:S(2)}, u32[]{:S(2)}) collective-permute-start(f32[4,144]{1,0:T(4,128)S(1)} %pad_maximum_fusion), channel_id=1, source_target_pairs={{0,510},{1,511},{2,4},{3,5},{4,2},{5,3},{6,8},{7,9},{8,6},{9,7},{1... | collective-permute-start | bytes 6920 | tf_op jit(solution)/shard_map/ppermute | solution.py:223
  83.1 4.3 %collective-permute-start.10 = (f32[4,144]{1,0:T(4,128)S(1)}, f32[4,144]{1,0:T(4,128)S(1)}, u32[]{:S(2)}, u32[]{:S(2)}) collective-permute-start(f32[4,144]{1,0:T(4,128)S(1)} %collective-permute-done.9.refs_5_), channel_id=1, source_target_pairs={{0,2},{3,1},{4,6},{7,5},{8,10},{11,9},{12,14},{15,13},{16,18},{19,... | collective-permute-start | bytes 6920 | tf_op jit(solution)/shard_map/ppermute | solution.py:223

commit v2 on v1

--- a/solution.py
+++ b/solution.py
@@ -8,6 +8,7 @@
 INV_TEMP = 20.0
 EPS = 1e-06
 TILE = 896
+RING = 16
 VMEM = pl.BlockSpec(memory_space=pltpu.VMEM)
 HBM = pl.BlockSpec(memory_space=pl.ANY)
 
@@ -68,6 +69,40 @@
     )(query_raw, passage_raw)
 
 
+def early_kernel(partner_ref, own_ref, mate_ref, near_ref, next_ref, *outs):
+    *score_outs, mass_ref = outs
+    partner = partner_ref[...]
+    count = partner.shape[0]
+    down = lax.broadcasted_iota(jnp.int32, (count, count), 0)
+    keep = 1.0 - eye_of(count) - jnp.where(down >= count // 2, partner, 0.0)
+    own = own_ref[...]
+    mass = jnp.zeros((count, count), jnp.float32)
+    for key_ref, score_out in zip((own_ref, mate_ref, near_ref, next_ref), score_outs):
+        score = contract(own, key_ref[...])
+        score_out[...] = score
+        share = exp_score(score)
+        mass = mass + (share * keep if key_ref is own_ref else share)
+    mass_ref[...] = mass
+
+
+def early_scores(partner, own, mate, near, next_block):
+    count, width = own.shape
+    square = jax.ShapeDtypeStruct((count, count), jnp.float32)
+    return pl.pallas_call(
+        early_kernel,
+        in_specs=[VMEM] * 5,
+        out_specs=(VMEM,) * 5,
+        out_shape=(square,) * 5,
+        compiler_params=pltpu.CompilerParams(vmem_limit_bytes=16 * 2**20),
+        cost_estimate=pl.CostEstimate(
+            flops=8 * count * count * width,
+            bytes_accessed=8 * count * width,
+            transcendentals=4 * count * count,
+        ),
+        name="early_scores",
+    )(partner, own, mate, near, next_block)
+
+
 def first_far_kernel(own_ref, far_ref, mass_ref, score_ref, passed_ref):
     score_ref[...] = contract(own_ref[...], far_ref[...])
     passed_ref[...] = mass_ref[...]
@@ -90,50 +125,54 @@
 
 
 def total_kernel(
-    partner_ref, own_ref, mate_ref, far_ref, far_score_ref, score_ref, mass_ref,
-    mate_score_out, far_score_out, recip_ref, loss_ref,
+    partner_ref, own_ref, near_mate_ref, next_mate_ref, far_ref, far_score_ref, score_ref, mass_ref,
+    near_mate_out, next_mate_out, far_score_out, recip_ref, loss_ref,
 ):
     partner = partner_ref[...]
     eye = eye_of(partner.shape[0])
     own = own_ref[...]
-    mate_score = contract(own, mate_ref[...])
-    far_score = far_score_ref[...] + contract(own, far_ref[...])
-    mate_score_out[...] = mate_score
-    far_score_out[...] = far_score
-    mass = mass_ref[...] + exp_score(mate_score) + exp_score(far_score)
+    mass = mass_ref[...]
+    for score, score_out in (
+        (contract(own, near_mate_ref[...]), near_mate_out),
+        (contract(own, next_mate_ref[...]), next_mate_out),
+        (far_score_ref[...] + contract(own, far_ref[...]), far_score_out),
+    ):
+        score_out[...] = score
+        mass = mass + exp_score(score)
     total_col = jnp.sum(mass, axis=1, keepdims=True)
     norm_row = jnp.sum((eye + partner) * total_col, axis=0, keepdims=True)
-    recip_ref[...] = 1.0 / norm_row
+    recip_ref[...] = jnp.broadcast_to(1.0 / norm_row, recip_ref.shape)
     positive = jnp.sum(partner * score_ref[...], axis=0, keepdims=True)
     losses = jnp.log(norm_row) + INV_TEMP - INV_TEMP * positive
     loss_ref[...] = losses[:, : loss_ref.shape[1]]
 
 
-def totals(partner, own, next_mate, far_second, far_score, own_score, mass):
+def totals(partner, own, near_mate, next_mate, far_second, far_score, own_score, mass):
     count, width = own.shape
-    row = jax.ShapeDtypeStruct((1, count), jnp.float32)
+    spread = jax.ShapeDtypeStruct((RING, count), jnp.float32)
     half_row = jax.ShapeDtypeStruct((1, count // 2), jnp.float32)
     square = jax.ShapeDtypeStruct((count, count), jnp.float32)
     return pl.pallas_call(
         total_kernel,
-        in_specs=[VMEM] * 7,
-        out_specs=(VMEM,) * 4,
-        out_shape=(square, square, row, half_row),
+        in_specs=[VMEM] * 8,
+        out_specs=(VMEM,) * 5,
+        out_shape=(square, square, square, spread, half_row),
         compiler_params=pltpu.CompilerParams(vmem_limit_bytes=16 * 2**20),
         cost_estimate=pl.CostEstimate(
-            flops=4 * count * count * width,
-            bytes_accessed=6 * count * width,
-            transcendentals=2 * count * count,
+            flops=6 * count * count * width,
+            bytes_accessed=8 * count * width,
+            transcendentals=3 * count * count,
         ),
         name="totals",
-    )(partner, own, next_mate, far_second, far_score, own_score, mass)
+    )(partner, own, near_mate, next_mate, far_second, far_score, own_score, mass)
 
 
 def gradient_kernel(blocks, refs):
-    partner_ref, scale_ref, own_row, mate_row, near_rows, next_rows, relay_rows = refs[:7]
-    score_refs = refs[7 : 7 + blocks]
-    key_refs = refs[7 + blocks : 8 + 2 * blocks]
-    query_ref, passage_ref, query_out, passage_out, weight_ref, dot_ref = refs[8 + 2 * blocks :]
+    partner_ref, scale_ref, ring_rows, beyond_rows = refs[:4]
+    score_refs = refs[4 : 4 + blocks]
+    key_refs = refs[4 + blocks : 10 + blocks]
+    first_ref, second_ref = refs[10 + blocks : 12 + blocks]
+    query_ref, passage_ref, query_out, passage_out, weight_ref, dot_ref = refs[12 + blocks :]
     count = partner_ref.shape[0]
     rows = count // 2
     step = pl.program_id(0)
@@ -142,22 +181,25 @@
     def _():
         partner = partner_ref[...]
         eye = eye_of(count)
-        recip_col = jnp.sum(eye * own_row[...], axis=1, keepdims=True)
-        relayed = relay_rows[1:2, :]
-        recip_rows = [
-            own_row[...],
-            mate_row[...],
-            near_rows[0:1, :],
-            near_rows[1:2, :],
-            next_rows[0:1, :],
-            next_rows[1:2, :],
-            jnp.where(relayed > 0.0, relayed, next_rows[3:4, :]),
-        ]
+        index = lax.axis_index("dp")
+        place = lax.rem(index, RING)
+        side = 1 - 2 * lax.rem(index, 2)
+        turn = 2 - 4 * lax.rem(lax.div(index, 2), 2)
+
+        def recip_row(offset):
+            spot = place + offset
+            wrapped = lax.rem(spot + RING, RING)
+            inside = (spot >= 0) & (spot < RING)
+            held = ring_rows[pl.ds(wrapped, 1), :]
+            return jnp.where(inside, held, beyond_rows[pl.ds(wrapped, 1), :])
+
+        recip_col = jnp.sum(eye * recip_row(0), axis=1, keepdims=True)
+        offsets = [0, side, turn, -turn, turn + side, side - turn, -3 * side]
         along = jnp.zeros((count, count), jnp.float32)
         weights = []
         for index in range(blocks):
             score = score_refs[index][...]
-            weight = exp_score(score) * (recip_col + recip_rows[index])
+            weight = exp_score(score) * (recip_col + recip_row(offsets[index]))
             if index == 0:
                 weight = weight * (1.0 - eye) * (1.0 - 0.5 * partner) - partner
             low = weight.astype(jnp.bfloat16)
@@ -167,8 +209,8 @@
         dot_ref[...] = INV_TEMP * jnp.sum(along, axis=1, keepdims=True)
 
     columns = pl.ds(pl.multiple_of(step * TILE, TILE), TILE)
-    near_keys = [key_ref[:, columns] for key_ref in key_refs[: blocks - 1]]
-    far_keys = key_refs[blocks - 1][:, columns] + key_refs[blocks][:, columns]
+    near_keys = [key_ref[:, columns] for key_ref in key_refs]
+    far_keys = first_ref[:, columns] + second_ref[:, columns]
     keys = jnp.concatenate(near_keys + [far_keys], axis=0)
     gradient = jnp.dot(weight_ref[...], keys, preferred_element_type=jnp.float32)
     scale = scale_ref[...]
@@ -179,7 +221,7 @@
         out_ref[...] = (INV_TEMP * gradient[span] - unit * along[span]) * scale[span]
 
 
-def gradients(partner, scale, recip_rows, scores, keys, query_raw, passage_raw):
+def gradients(partner, scale, ring_rows, beyond_rows, scores, keys, query_raw, passage_raw):
     blocks = len(scores)
     rows, width = query_raw.shape
     count = 2 * rows
@@ -193,7 +235,7 @@
         body,
         out_shape=(out, out),
         grid=(width // TILE,),
-        in_specs=[VMEM] * (10 + 2 * blocks),
+        in_specs=[VMEM] * (14 + blocks),
         out_specs=(out_spec, out_spec),
         scratch_shapes=[
             pltpu.VMEM((count, blocks * count), jnp.bfloat16),
@@ -206,7 +248,7 @@
             transcendentals=blocks * count * count,
         ),
         name="gradients",
-    )(partner, scale, *recip_rows, *scores, *keys, query_raw, passage_raw)
+    )(partner, scale, ring_rows, beyond_rows, *scores, *keys, query_raw, passage_raw)
 
 
 def per_device(query_raw, passage_raw, pairing):
@@ -237,46 +279,46 @@
     def far_over_near(chip, core):
         return (chip + 1 if core else chip - 1, 1 - core) if chip % 2 != core else None
 
-    def near_from_direct(chip, core):
-        return (chip ^ 1, core) if chip % 2 == core else None
+    def over_border(chip, core):
+        place = 2 * chip % RING + core
+        steps = {13: 5, 14: 2, 15: 2, 0: -2, 1: -2, 2: -5}
+        if place not in steps:
+            return None
+        target = 2 * chip + core + steps[place]
+        return (target // 2, target % 2)
 
     own, scale = unit_rows(query_raw, passage_raw)
     paired = (pairing[0][:, None] == jnp.arange(rows, dtype=jnp.int32)[None, :]).astype(jnp.float32)
     blank = jnp.zeros((rows, rows), jnp.float32)
     partner = jnp.block([[blank, paired], [paired.T, blank]])
-    passage_row = jnp.arange(2 * rows)[:, None] >= rows
-    keep = 1.0 - jnp.eye(2 * rows, dtype=jnp.float32) - jnp.where(passage_row, partner, 0.0)
 
     near = swapped(own, near_chip)
     next_block = swapped(own, next_chip)
     mate = swapped(own, other_core)
     far_first = swapped(near, far_over_next)
+    far_second = swapped(next_block, far_over_near)
     near_mate = swapped(near, other_core)
-    far_second = swapped(next_block, far_over_near)
     next_mate = swapped(next_block, other_core)
 
-    keys = [own, mate, near, near_mate, next_block]
-    scores = [contract(own, key) for key in keys]
-    mass = exp_score(scores[0]) * keep
-    for score in scores[1:]:
-        mass = mass + exp_score(score)
+    *scores, mass = early_scores(partner, own, mate, near, next_block)
     far_score, mass = first_far(own, far_first, mass)
-    mate_score, far_score, recip, losses = totals(
-        partner, own, next_mate, far_second, far_score, scores[0], mass
-    )
-
-    mate_row = swapped(recip, other_core)
-    chip_rows = jnp.concatenate([recip, mate_row], axis=0)
-    near_rows = swapped(chip_rows, near_chip)
-    next_rows = swapped(jnp.concatenate([chip_rows, near_rows], axis=0), next_chip)
-    relay_rows = swapped(next_rows, near_from_direct)
+    *late_scores, spread, losses = totals(
+        partner, own, near_mate, next_mate, far_second, far_score, scores[0], mass
+    )
+
+    groups = [list(range(start, start + RING)) for start in range(0, size, RING)]
+    ring_rows = lax.all_to_all(
+        spread, "dp", split_axis=0, concat_axis=0, axis_index_groups=groups, tiled=True
+    )
+    beyond_rows = swapped(ring_rows, over_border)
 
     query_grad, passage_grad = gradients(
         partner,
         scale,
-        [recip, mate_row, near_rows, next_rows, relay_rows],
-        scores + [mate_score, far_score],
-        keys + [next_mate, far_first, far_second],
+        ring_rows,
+        beyond_rows,
+        scores + late_scores,
+        [own, mate, near, next_block, near_mate, next_mate, far_first, far_second],
         query_raw,
         passage_raw,
     )

time: 91.6 us -> 86.7 us (0.947)
  starting transfers between devices: 58 us -> 39.2 us
  blocking collectives: 0 us -> 8.92 us
  waiting for transfers between devices: 19.9 us -> 26.3 us
  matrix products: 4.11 us -> 0 us
  Pallas kernels: 8.1 us -> 9.58 us
  local copies, waits for them, and re-layouts: 0.02 us -> 1.26 us
    ppermute x11 -> x8, starting transfers between devices: 58 us -> 39.2 us  [swapped(): return lax.ppermute(value, 'dp', pairs)]
    all_to_all x0 -> x1, blocking collectives: none -> 8.92 us  [per_device(): lax.all_to_all(spread, 'dp', split_axis=0, concat_axis=0, axis_index_grou...]
    ppermute x11 -> x8, waiting for transfers between devices: 19.9 us -> 26.3 us  [swapped(): return lax.ppermute(value, 'dp', pairs)]
    dot_general x5 -> x0, matrix products: 4.11 us -> none  [contract(): lax.dot_general(left_rows, right_rows, (((1,), (1,)), ((), ())), preferre...]
    pallas_call x1 -> x2, Pallas kernels: 1.36 us -> 2.86 us  [the longest x1 1.6 us: totals(): pl.pallas_call(total_kernel, in_specs=[VMEM] * 8, out_specs=(VMEM,) * 5,...]
    unnamed x10 -> x13, local copies, waits for them, and re-layouts: 0.02 us -> 1.24 us
  transfers between devices with their start and end apart: 11 -> 8, of which waited for: 7 -> 4; matrix products, arithmetic and copies ran while one was open for 5% -> 0% of each run, Pallas kernels for 0% -> 2%
where the time goes in v2:
time: 86.7 us; the launch traced here: 86.3 us
  starting transfers between devices  39.2 us (45%)
  waiting for transfers between devices  26.3 us (30%)
  Pallas kernels  9.58 us (11%)
  blocking collectives  8.92 us (10%)
  local copies, waits for them, and re-layouts  1.26 us (1%)
    ppermute x8, starting transfers between devices, swapped(): return lax.ppermute(value, 'dp', pairs)  39.2 us
    ppermute x8, waiting for transfers between devices, swapped(): return lax.ppermute(value, 'dp', pairs)  26.3 us
    all_to_all x1, blocking collectives, per_device(): lax.all_to_all(spread, 'dp', split_axis=0, concat_axis=0, axis_index_grou...  8.92 us
    pallas_call x1, Pallas kernels, gradients(): pl.pallas_call(body, out_shape=(out, out), grid=(width // TILE,), in_spec...  3.68 us
    pallas_call x1, Pallas kernels, unit_rows(): pl.pallas_call(unit_kernel, in_specs=[HBM, HBM], out_specs=(VMEM, VMEM),...  2.61 us
  transfers between devices with their start and end apart: 8, of which 4 were waited for; matrix products, arithmetic and copies ran while one was open for 0% of the time, Pallas kernels for 2%

profile of v2, /device:TPU:1, one launch (start us, length us, event | category | flops | bytes accessed | tf_op | source)
XLA Modules:
  0.0 86.3 jit_solution(4045374350296133661)
XLA Ops:
  0.6 2.6 %unit_rows.1 = (bf16[144,3584]{1,0:T(8,128)(2,1)}, f32[144,1]{1,0:T(8,128)}) custom-call(bf16[72,3584]{1,0:T(8,128)(2,1)} %refs_19_.1, bf16[72,3584]{1,0:T(8,128)(2,1)} %refs_20_.1), custom_call_target="tpu_custom_call" | custom-call | flops 1548288 | bytes 2064384 | tf_op jit(solution)/shard_map/unit_rows/pallas_call | solution.py:51
  3.2 0.0 copy-start.5
  3.3 4.8 %collective-permute-start = (bf16[144,3584]{1,0:T(8,128)(2,1)}, bf16[144,3584]{1,0:T(8,128)(2,1)S(1)}, u32[]{:S(2)}, u32[]{:S(2)}) collective-permute-start(bf16[144,3584]{1,0:T(8,128)(2,1)} %get-tuple-element.19.own_ref.refs_11_), channel_id=1, source_target_pairs={{0,2},{1,3},{2,0},{3,1},{4,6},{5,7},{6,4},{7,5},{8,10},{9,11},{10,... | collective-permute-start | bytes 3096584 | tf_op jit(solution)/shard_map/ppermute | solution.py:265
  8.1 13.9 %collective-permute-start.2 = (bf16[144,3584]{1,0:T(8,128)(2,1)}, bf16[144,3584]{1,0:T(8,128)(2,1)S(1)}, u32[]{:S(2)}, u32[]{:S(2)}) collective-permute-start(bf16[144,3584]{1,0:T(8,128)(2,1)} %get-tuple-element.19.own_ref.refs_11_), channel_id=1, source_target_pairs={{0,510},{1,511},{2,4},{3,5},{4,2},{5,3},{6,8},{7,9},{8,6},{9,7},{1... | collective-permute-start | bytes 3096584 | tf_op jit(solution)/shard_map/ppermute | solution.py:265
  22.1 3.1 %collective-permute-start.6 = (bf16[144,3584]{1,0:T(8,128)(2,1)}, bf16[144,3584]{1,0:T(8,128)(2,1)S(1)}, u32[]{:S(2)}, u32[]{:S(2)}) collective-permute-start(bf16[144,3584]{1,0:T(8,128)(2,1)} %get-tuple-element.19.own_ref.refs_11_), channel_id=1, source_target_pairs={{0,1},{1,0},{2,3},{3,2},{4,5},{5,4},{6,7},{7,6},{8,9},{9,8},{10,11... | collective-permute-start | bytes 3096584 | tf_op jit(solution)/shard_map/ppermute | solution.py:265
  25.2 1.6 %collective-permute-done.near_ref.refs_13_ = bf16[144,3584]{1,0:T(8,128)(2,1)S(1)} collective-permute-done((bf16[144,3584]{1,0:T(8,128)(2,1)}, bf16[144,3584]{1,0:T(8,128)(2,1)S(1)}, u32[]{:S(2)}, u32[]{:S(2)}) %collective-permute-start) | collective-permute-done | bytes 1032224 | tf_op jit(solution)/shard_map/ppermute | solution.py:265
  26.8 0.7 collective-permute-start.5
  27.5 16.9 %collective-permute-done.2.next_ref.refs_14_ = bf16[144,3584]{1,0:T(8,128)(2,1)S(1)} collective-permute-done((bf16[144,3584]{1,0:T(8,128)(2,1)}, bf16[144,3584]{1,0:T(8,128)(2,1)S(1)}, u32[]{:S(2)}, u32[]{:S(2)}) %collective-permute-start.2) | collective-permute-done | bytes 1032224 | tf_op jit(solution)/shard_map/ppermute | solution.py:265
  44.5 1.9 %collective-permute-start.4 = (bf16[144,3584]{1,0:T(8,128)(2,1)S(1)}, bf16[144,3584]{1,0:T(8,128)(2,1)S(1)}, u32[]{:S(2)}, u32[]{:S(2)}) collective-permute-start(bf16[144,3584]{1,0:T(8,128)(2,1)S(1)} %collective-permute-done.2.next_ref.refs_14_), channel_id=1, source_target_pairs={{1,2},{2,1},{5,6},{6,5},{9,10},{10,9},{13,14},{14,13},{17,18},{18,... | collective-permute-start | bytes 3096584 | tf_op jit(solution)/shard_map/ppermute | solution.py:265
  46.4 2.3 %collective-permute-start.3 = (bf16[144,3584]{1,0:T(8,128)(2,1)S(1)}, bf16[144,3584]{1,0:T(8,128)(2,1)S(1)}, u32[]{:S(2)}, u32[]{:S(2)}) collective-permute-start(bf16[144,3584]{1,0:T(8,128)(2,1)S(1)} %collective-permute-done.2.next_ref.refs_14_), channel_id=1, source_target_pairs={{0,1},{1,0},{2,3},{3,2},{4,5},{5,4},{6,7},{7,6},{8,9},{9,8},{10,11... | collective-permute-start | bytes 3096584 | tf_op jit(solution)/shard_map/ppermute | solution.py:265
  48.7 2.0 %collective-permute-start.1 = (bf16[144,3584]{1,0:T(8,128)(2,1)S(1)}, bf16[144,3584]{1,0:T(8,128)(2,1)S(1)}, u32[]{:S(2)}, u32[]{:S(2)}) collective-permute-start(bf16[144,3584]{1,0:T(8,128)(2,1)S(1)} %collective-permute-done.near_ref.refs_13_), channel_id=1, source_target_pairs={{0,1},{1,0},{2,3},{3,2},{4,5},{5,4},{6,7},{7,6},{8,9},{9,8},{10,11... | collective-permute-start | bytes 3096584 | tf_op jit(solution)/shard_map/ppermute | solution.py:265
  50.7 0.0 copy-done.5
  50.7 0.1 iota_compare_fusion.1
  50.8 0.1 fusion.partner_ref.refs_0_
  50.9 0.0 collective-permute-done.6.mate_ref.refs_12_
  50.9 0.0 copy-start
  50.9 1.2 %copy-done = bf16[144,3584]{1,0:T(8,128)(2,1)S(1)} copy-done((bf16[144,3584]{1,0:T(8,128)(2,1)S(1)}, bf16[144,3584]{1,0:T(8,128)(2,1)}, u32[]{:S(2)}) %copy-start) | copy-done | bytes 1032216
  52.1 1.3 %early_scores.1 = (f32[144,144]{1,0:T(8,128)S(1)}, f32[144,144]{1,0:T(8,128)S(1)}, f32[144,144]{1,0:T(8,128)S(1)}, f32[144,144]{1,0:T(8,128)S(1)}, f32[144,144]{1,0:T(8,128)S(1)}) custom-call(f32[144,144]{1,0:T(8,128)S(1)} %fusion.partner_ref.refs_0_, bf16[144,3584]{1,0:T(8,128)(2,1)S(1)} %copy-done, ...), custom_call_target="tpu_custom_call" | custom-call | flops 594542592 | bytes 4128768 | tf_op jit(solution)/shard_map/early_scores/pallas_call | solution.py:91
  53.4 0.0 collective-permute-done.5.far_ref.refs_17_
  53.4 0.4 first_far.1
  53.9 6.5 %collective-permute-done.4.far_ref.refs_18_ = bf16[144,3584]{1,0:T(8,128)(2,1)S(1)} collective-permute-done((bf16[144,3584]{1,0:T(8,128)(2,1)S(1)}, bf16[144,3584]{1,0:T(8,128)(2,1)S(1)}, u32[]{:S(2)}, u32[]{:S(2)}) %collective-permute-start.4) | collective-permute-done | bytes 1032224 | tf_op jit(solution)/shard_map/ppermute | solution.py:265
  60.4 0.0 collective-permute-done.3.next_mate_ref.refs_16_
  60.4 0.0 collective-permute-done.1.near_mate_ref.refs_15_
  60.4 0.0 copy-start.1
  60.4 0.0 copy-start.2
  60.4 0.0 copy-start.3
  60.4 1.6 %totals.1 = (f32[144,144]{1,0:T(8,128)S(1)}, f32[144,144]{1,0:T(8,128)S(1)}, f32[144,144]{1,0:T(8,128)S(1)}, f32[16,144]{1,0:T(8,128)S(1)}, f32[1,72]{1,0:T(1,128)}) custom-call(f32[144,144]{1,0:T(8,128)S(1)} %fusion.partner_ref.refs_0_, bf16[144,3584]{1,0:T(8,128)(2,1)S(1)} %copy-done, bf16[144,3584]{1,0:T(8,128)(2,1)S(1)} %collective-permute-done.1.near_mate_ref.refs_15_, ...), custom_call_target="tpu_custom_call" | custom-call | flops 445906944 | bytes 4128768 | tf_op jit(solution)/shard_map/totals/pallas_call | solution.py:155
  62.0 0.0 copy-start.4
  62.1 8.9 %all_to_all.11 = f32[16,1,144]{2,1,0:T(1,128)S(1)} all-to-all(f32[16,1,144]{2,1,0:T(1,128)S(1)} %copy.6), channel_id=1, replica_groups={{0,1,2,3,4,5,6,7,8,9,10,11,12,13,14,15},{16,17,18,19,20,21,22,23,24,25,..., dimensions={0} | all-to-all | bytes 18432 | tf_op jit(solution)/shard_map/all_to_all | solution.py:310
  71.0 10.4 %collective-permute-start.7 = (f32[16,144]{1,0:T(8,128)S(1)}, f32[16,144]{1,0:T(8,128)S(1)}, u32[]{:S(2)}, u32[]{:S(2)}) collective-permute-start(f32[16,144]{1,0:T(8,128)S(1)} %bitcast.6), channel_id=1, source_target_pairs={{0,510},{1,511},{2,509},{13,18},{14,16},{15,17},{16,14},{17,15},{1... | collective-permute-start | bytes 27656 | tf_op jit(solution)/shard_map/ppermute | solution.py:265
  81.3 1.2 %collective-permute-done.7.refs_3_ = f32[16,144]{1,0:T(8,128)S(1)} collective-permute-done((f32[16,144]{1,0:T(8,128)S(1)}, f32[16,144]{1,0:T(8,128)S(1)}, u32[]{:S(2)}, u32[]{:S(2)}) %collective-permute-start.7) | collective-permute-done | bytes 9248 | tf_op jit(solution)/shard_map/ppermute | solution.py:265
  82.6 0.0 copy-done.1
  82.6 0.0 copy-done.2
  82.6 0.0 copy-done.3
  82.6 0.0 copy-done.4
  82.6 3.7 %gradients.1 = (f32[72,3584]{1,0:T(8,128)}, f32[72,3584]{1,0:T(8,128)}) custom-call(f32[144,144]{1,0:T(8,128)S(1)} %fusion.partner_ref.refs_0_, f32[144,1]{1,0:T(8,128)S(1)} %copy-done.4, f32[16,144]{1,0:T(8,128)S(1)} %bitcast.7, f32[16,144]{1,0:T(8,128)S(1)} %collective-permute-done.7.refs_3_, f32[144,144]{1,0:T(8,128)S(1)} %get-tuple-element.22.score_ref.refs_4_, ...), custom_call_target="tpu_custom_call" | custom-call | flops 1040449536 | bytes 10321920 | tf_op jit(solution)/shard_map/gradients/pallas_call | solution.py:234
  (2 shorter events, 0.0 us)
Async XLA Ops:
  3.2 47.5 %copy-start.5 = (s32[1,72]{1,0:T(1,128)S(1)}, s32[1,72]{1,0:T(1,128)}, u32[]{:S(2)}) copy-start(s32[1,72]{1,0:T(1,128)} %param.5) | copy-start | bytes 868
  3.3 23.5 %collective-permute-start = (bf16[144,3584]{1,0:T(8,128)(2,1)}, bf16[144,3584]{1,0:T(8,128)(2,1)S(1)}, u32[]{:S(2)}, u32[]{:S(2)}) collective-permute-start(bf16[144,3584]{1,0:T(8,128)(2,1)} %get-tuple-element.19.own_ref.refs_11_), channel_id=1, source_target_pairs={{0,2},{1,3},{2,0},{3,1},{4,6},{5,7},{6,4},{7,5},{8,10},{9,11},{10,... | collective-permute-start | bytes 3096584 | tf_op jit(solution)/shard_map/ppermute | solution.py:265
  8.1 36.4 %collective-permute-start.2 = (bf16[144,3584]{1,0:T(8,128)(2,1)}, bf16[144,3584]{1,0:T(8,128)(2,1)S(1)}, u32[]{:S(2)}, u32[]{:S(2)}) collective-permute-start(bf16[144,3584]{1,0:T(8,128)(2,1)} %get-tuple-element.19.own_ref.refs_11_), channel_id=1, source_target_pairs={{0,510},{1,511},{2,4},{3,5},{4,2},{5,3},{6,8},{7,9},{8,6},{9,7},{1... | collective-permute-start | bytes 3096584 | tf_op jit(solution)/shard_map/ppermute | solution.py:265
  22.1 28.9 %collective-permute-start.6 = (bf16[144,3584]{1,0:T(8,128)(2,1)}, bf16[144,3584]{1,0:T(8,128)(2,1)S(1)}, u32[]{:S(2)}, u32[]{:S(2)}) collective-permute-start(bf16[144,3584]{1,0:T(8,128)(2,1)} %get-tuple-element.19.own_ref.refs_11_), channel_id=1, source_target_pairs={{0,1},{1,0},{2,3},{3,2},{4,5},{5,4},{6,7},{7,6},{8,9},{9,8},{10,11... | collective-permute-start | bytes 3096584 | tf_op jit(solution)/shard_map/ppermute | solution.py:265
  26.8 26.6 %collective-permute-start.5 = (bf16[144,3584]{1,0:T(8,128)(2,1)S(1)}, bf16[144,3584]{1,0:T(8,128)(2,1)S(1)}, u32[]{:S(2)}, u32[]{:S(2)}) collective-permute-start(bf16[144,3584]{1,0:T(8,128)(2,1)S(1)} %collective-permute-done.near_ref.refs_13_), channel_id=1, source_target_pairs={{0,511},{3,4},{4,3},{7,8},{8,7},{11,12},{12,11},{15,16},{16,15},{1... | collective-permute-start | bytes 3096584 | tf_op jit(solution)/shard_map/ppermute | solution.py:265
  44.5 15.9 %collective-permute-start.4 = (bf16[144,3584]{1,0:T(8,128)(2,1)S(1)}, bf16[144,3584]{1,0:T(8,128)(2,1)S(1)}, u32[]{:S(2)}, u32[]{:S(2)}) collective-permute-start(bf16[144,3584]{1,0:T(8,128)(2,1)S(1)} %collective-permute-done.2.next_ref.refs_14_), channel_id=1, source_target_pairs={{1,2},{2,1},{5,6},{6,5},{9,10},{10,9},{13,14},{14,13},{17,18},{18,... | collective-permute-start | bytes 3096584 | tf_op jit(solution)/shard_map/ppermute | solution.py:265
  46.4 14.0 %collective-permute-start.3 = (bf16[144,3584]{1,0:T(8,128)(2,1)S(1)}, bf16[144,3584]{1,0:T(8,128)(2,1)S(1)}, u32[]{:S(2)}, u32[]{:S(2)}) collective-permute-start(bf16[144,3584]{1,0:T(8,128)(2,1)S(1)} %collective-permute-done.2.next_ref.refs_14_), channel_id=1, source_target_pairs={{0,1},{1,0},{2,3},{3,2},{4,5},{5,4},{6,7},{7,6},{8,9},{9,8},{10,11... | collective-permute-start | bytes 3096584 | tf_op jit(solution)/shard_map/ppermute | solution.py:265
  48.7 11.7 %collective-permute-start.1 = (bf16[144,3584]{1,0:T(8,128)(2,1)S(1)}, bf16[144,3584]{1,0:T(8,128)(2,1)S(1)}, u32[]{:S(2)}, u32[]{:S(2)}) collective-permute-start(bf16[144,3584]{1,0:T(8,128)(2,1)S(1)} %collective-permute-done.near_ref.refs_13_), channel_id=1, source_target_pairs={{0,1},{1,0},{2,3},{3,2},{4,5},{5,4},{6,7},{7,6},{8,9},{9,8},{10,11... | collective-permute-start | bytes 3096584 | tf_op jit(solution)/shard_map/ppermute | solution.py:265
  50.9 1.2 %copy-start = (bf16[144,3584]{1,0:T(8,128)(2,1)S(1)}, bf16[144,3584]{1,0:T(8,128)(2,1)}, u32[]{:S(2)}) copy-start(bf16[144,3584]{1,0:T(8,128)(2,1)} %get-tuple-element.19.own_ref.refs_11_) | copy-start | bytes 3096580
  60.4 22.2 %copy-start.1 = (bf16[144,3584]{1,0:T(8,128)(2,1)S(1)}, bf16[144,3584]{1,0:T(8,128)(2,1)}, u32[]{:S(2)}) copy-start(bf16[144,3584]{1,0:T(8,128)(2,1)} %get-tuple-element.19.own_ref.refs_11_) | copy-start | bytes 3096580
  60.4 22.2 %copy-start.2 = (bf16[72,3584]{1,0:T(8,128)(2,1)S(1)}, bf16[72,3584]{1,0:T(8,128)(2,1)}, u32[]{:S(2)}) copy-start(bf16[72,3584]{1,0:T(8,128)(2,1)} %refs_19_.1) | copy-start | bytes 1548292
  60.4 22.2 %copy-start.3 = (bf16[72,3584]{1,0:T(8,128)(2,1)S(1)}, bf16[72,3584]{1,0:T(8,128)(2,1)}, u32[]{:S(2)}) copy-start(bf16[72,3584]{1,0:T(8,128)(2,1)} %refs_20_.1) | copy-start | bytes 1548292
  62.0 20.6 %copy-start.4 = (f32[144,1]{1,0:T(8,128)S(1)}, f32[144,1]{1,0:T(8,128)}, u32[]{:S(2)}) copy-start(f32[144,1]{1,0:T(8,128)} %get-tuple-element.25.refs_1_) | copy-start | bytes 1732
  71.0 11.6 %collective-permute-start.7 = (f32[16,144]{1,0:T(8,128)S(1)}, f32[16,144]{1,0:T(8,128)S(1)}, u32[]{:S(2)}, u32[]{:S(2)}) collective-permute-start(f32[16,144]{1,0:T(8,128)S(1)} %bitcast.6), channel_id=1, source_target_pairs={{0,510},{1,511},{2,509},{13,18},{14,16},{15,17},{16,14},{17,15},{1... | collective-permute-start | bytes 27656 | tf_op jit(solution)/shard_map/ppermute | solution.py:265

commit v3 on v1

v3 whole, which is shorter than its diff:
```python
import functools

import jax
import jax.numpy as jnp
from jax import lax
from jax.experimental import pallas as pl
from jax.experimental.pallas import tpu as pltpu
from jax.sharding import PartitionSpec as P

INV_TEMP = 20.0
EPS = 1e-06
TILE = 896
SPREAD = 8
VMEM = pl.BlockSpec(memory_space=pltpu.VMEM)
HBM = pl.BlockSpec(memory_space=pl.ANY)


def contract(left_rows, right_rows):
    return lax.dot_general(
        left_rows, right_rows, (((1,), (1,)), ((), ())), preferred_element_type=jnp.float32
    )


def exp_score(score):
    return jnp.exp(INV_TEMP * score - INV_TEMP)


def eye_of(count):
    down = lax.broadcasted_iota(jnp.int32, (count, count), 0)
    across = lax.broadcasted_iota(jnp.int32, (count, count), 1)
    return (down == across).astype(jnp.float32)


def unit_kernel(
    query_any, passage_any, own_ref, first_ref, second_ref, scale_ref, query_ref, passage_ref, sems
):
    copies = [
        pltpu.make_async_copy(query_any, query_ref, sems.at[0]),
        pltpu.make_async_copy(passage_any, passage_ref, sems.at[1]),
    ]
    for copy in copies:
        copy.start()
    for copy in copies:
        copy.wait()
    raw_rows = jnp.concatenate(
        [query_ref[...].astype(jnp.float32), passage_ref[...].astype(jnp.float32)], axis=0
    )
    scale_rows = lax.rsqrt(jnp.sum(raw_rows * raw_rows, axis=1, keepdims=True) + EPS)
    low_rows = (raw_rows * scale_rows).astype(jnp.bfloat16)
    width = first_ref.shape[1]
    own_ref[...] = low_rows
    first_ref[...] = low_rows[:, :width]
    second_ref[...] = low_rows[:, width:]
    scale_ref[...] = scale_rows


def unit_rows(query_raw, passage_raw):
    rows, width = query_raw.shape
    whole = jax.ShapeDtypeStruct((2 * rows, width), jnp.bfloat16)
    half = jax.ShapeDtypeStruct((2 * rows, width // 2), jnp.bfloat16)
    return pl.pallas_call(
        unit_kernel,
        in_specs=[HBM, HBM],
        out_specs=(VMEM, VMEM, VMEM, VMEM),
        out_shape=(whole, half, half, jax.ShapeDtypeStruct((2 * rows, 1), jnp.float32)),
        scratch_shapes=[
            pltpu.VMEM((rows, width), jnp.bfloat16),
            pltpu.VMEM((rows, width), jnp.bfloat16),
            pltpu.SemaphoreType.DMA((2,)),
        ],
        compiler_params=pltpu.CompilerParams(vmem_limit_bytes=121 * 2**19),
        cost_estimate=pl.CostEstimate(
            flops=6 * rows * width, bytes_accessed=8 * rows * width, transcendentals=0
        ),
        name="unit_rows",
    )(query_raw, passage_raw)


def score_call(body, name, count, outs, operands, passed=()):
    size = sum(operand.size for operand in operands)
    return pl.pallas_call(
        body,
        in_specs=[VMEM] * len(operands),
        out_specs=[VMEM] * (len(outs) + len(passed)),
        out_shape=[jax.ShapeDtypeStruct(shape, jnp.float32) for shape in outs]
        + [jax.ShapeDtypeStruct(value.shape, value.dtype) for value in passed],
        compiler_params=pltpu.CompilerParams(vmem_limit_bytes=16 * 2**20),
        cost_estimate=pl.CostEstimate(
            flops=2 * count * size, bytes_accessed=2 * size, transcendentals=count * count
        ),
        name=name,
    )(*operands)


def halves_score(own, first, second):
    width = first.shape[1]
    return contract(own[:, :width], first) + contract(own[:, width:], second)


def early_kernel(
    partner_ref, own_ref, near_ref, next_first, next_second, *outs
):
    *score_outs, mass_ref, blank_ref, passed_ref = outs
    partner = partner_ref[...]
    count = partner.shape[0]
    down = lax.broadcasted_iota(jnp.int32, (count, count), 0)
    keep = 1.0 - eye_of(count) - jnp.where(down >= count // 2, partner, 0.0)
    own = own_ref[...]
    scores = [
        contract(own, own),
        contract(own, near_ref[...]),
        halves_score(own, next_first[...], next_second[...]),
    ]
    mass = exp_score(scores[0]) * keep
    for score in scores[1:]:
        mass = mass + exp_score(score)
    for score, score_out in zip(scores, score_outs):
        score_out[...] = score
    mass_ref[...] = mass
    blank_ref[...] = jnp.zeros((count, count), jnp.float32)
    passed_ref[...] = next_first[...]


def far_kernel(place, own_ref, far_ref, sum_ref, score_ref):
    width = far_ref.shape[1]
    own = own_ref[:, place * width : (place + 1) * width]
    score_ref[...] = sum_ref[...] + contract(own, far_ref[...])


def far_scores(own, far, score_sum, place):
    count = own.shape[0]
    body = functools.partial(far_kernel, place)
    return score_call(body, "far_scores", count, [(count, count)], [own, far, score_sum])[0]


def side_kernel(place, sum_ref, own_ref, key_ref, sum_out, score_out):
    width = key_ref.shape[1]
    sum_out[...] = sum_ref[...]
    score_out[...] = contract(own_ref[:, place * width : (place + 1) * width], key_ref[...])


def side_scores(own, key, score_sum, place):
    count = own.shape[0]
    body = functools.partial(side_kernel, place)
    return score_call(body, "side_scores", count, [(count, count)] * 2, [score_sum, own, key])


def total_kernel(
    far_score_ref, mass_ref, score_ref, partner_ref, own_ref, own_mate_score, near_mate_ref, mate_first, mate_second,
    near_mate_out, next_mate_out, recip_ref, spread_ref, loss_ref,
):
    partner = partner_ref[...]
    own = own_ref[...]
    mass = mass_ref[...] + exp_score(far_score_ref[...])
    mass = mass + exp_score(own_mate_score[...])
    near_score = contract(own, near_mate_ref[...])
    near_mate_out[...] = near_score
    mass = mass + exp_score(near_score)
    next_score = halves_score(own, mate_first[...], mate_second[...])
    next_mate_out[...] = next_score
    mass = mass + exp_score(next_score)
    total_col = jnp.sum(mass, axis=1, keepdims=True)
    eye = eye_of(partner.shape[0])
    norm_row = jnp.sum((eye + partner) * total_col, axis=0, keepdims=True)
    recip_ref[...] = 1.0 / norm_row
    spread_ref[...] = jnp.broadcast_to(1.0 / norm_row, spread_ref.shape)
    positive = jnp.sum(partner * score_ref[...], axis=0, keepdims=True)
    losses = jnp.log(norm_row) + INV_TEMP - INV_TEMP * positive
    loss_ref[...] = losses[:, : loss_ref.shape[1]]


def known_kernel(
    partner_ref, own_row, mate_row, far_row, own_score, mate_score, far_score, weight_ref, dot_ref
):
    partner = partner_ref[...]
    eye = eye_of(partner.shape[0])
    recip_col = jnp.sum(eye * own_row[...], axis=1, keepdims=True)
    along = jnp.zeros(partner.shape, jnp.float32)
    for index, (row_ref, score_ref) in enumerate(
        ((own_row, own_score), (mate_row, mate_score), (far_row, far_score))
    ):
        score = score_ref[...]
        weight = exp_score(score) * (recip_col + row_ref[0:1, :])
        if index == 0:
            weight = weight * (1.0 - eye) * (1.0 - 0.5 * partner) - partner
        low = weight.astype(jnp.bfloat16)
        along = along + low.astype(jnp.float32) * score
        weight_ref[index] = low
    dot_ref[...] = along


def known_weights(partner, rows, scores):
    count = partner.shape[0]
    return pl.pallas_call(
        known_kernel,
        in_specs=[VMEM] * 7,
        out_specs=(VMEM, VMEM),
        out_shape=(
            jax.ShapeDtypeStruct((3, count, count), jnp.bfloat16),
            jax.ShapeDtypeStruct((count, count), jnp.float32),
        ),
        compiler_params=pltpu.CompilerParams(vmem_limit_bytes=16 * 2**20),
        cost_estimate=pl.CostEstimate(
            flops=40 * count * count,
            bytes_accessed=32 * count * count,
            transcendentals=3 * count * count,
        ),
        name="known_weights",
    )(partner, *rows, *scores)


def gradient_kernel(
    known_ref, along_ref, scale_ref, own_row, next_rows, near_rows, *refs
):
    score_refs = refs[:4]
    own_ref, mate_ref, near_ref, near_mate, far_first = refs[4:9]
    half_refs = refs[9:12], refs[12:15]
    query_ref, passage_ref, query_out, passage_out, weight_ref, dot_ref = refs[15:]
    count = along_ref.shape[0]
    rows = count // 2
    step = pl.program_id(0)

    @pl.when(step == 0)
    def _():
        recip_col = jnp.sum(eye_of(count) * own_row[...], axis=1, keepdims=True)
        along = along_ref[...]
        recip_rows = [near_rows[0:1, :], next_rows[0:1, :], near_rows[1:2, :], next_rows[1:2, :]]
        weights = [known_ref[0], known_ref[1]]
        for score_ref, recip_row in zip(score_refs, recip_rows):
            score = score_ref[...]
            low = (exp_score(score) * (recip_col + recip_row)).astype(jnp.bfloat16)
            along = along + low.astype(jnp.float32) * score
            weights.append(low)
        weights.append(known_ref[2])
        weight_ref[...] = jnp.concatenate(weights, axis=1)
        dot_ref[...] = INV_TEMP * jnp.sum(along, axis=1, keepdims=True)

    half_steps = pl.num_programs(0) // 2
    whole = pl.ds(pl.multiple_of(step * TILE, TILE), TILE)

    def emit(half):
        next_ref, next_mate, far_second = half_refs[half]
        columns = pl.ds(pl.multiple_of((step - half * half_steps) * TILE, TILE), TILE)
        keys = [
            own_ref[:, whole],
            mate_ref[:, whole],
            near_ref[:, whole],
            next_ref[:, columns],
            near_mate[:, whole],
            next_mate[:, columns],
            far_first[:, whole] + far_second[:, columns],
        ]
        keys = jnp.concatenate(keys, axis=0)
        gradient = jnp.dot(weight_ref[...], keys, preferred_element_type=jnp.float32)
        scale = scale_ref[...]
        along = dot_ref[...]
        for part, raw_ref, out_ref in ((0, query_ref, query_out), (1, passage_ref, passage_out)):
            span = slice(part * rows, (part + 1) * rows)
            unit = raw_ref[:, whole].astype(jnp.float32) * scale[span]
            out_ref[...] = (INV_TEMP * gradient[span] - unit * along[span]) * scale[span]

    @pl.when(step < half_steps)
    def _():
        emit(0)

    @pl.when(step >= half_steps)
    def _():
        emit(1)


def gradients(known, scale, recip_rows, scores, keys, query_raw, passage_raw):
    blocks = 7
    rows, width = query_raw.shape
    count = 2 * rows
    out = jax.ShapeDtypeStruct((rows, width), jnp.float32)
    out_spec = pl.BlockSpec((rows, TILE), lambda step: (0, step))

    return pl.pallas_call(
        gradient_kernel,
        out_shape=(out, out),
        grid=(width // TILE,),
        in_specs=[VMEM] * (12 + len(scores) + len(keys) - 4),
        out_specs=(out_spec, out_spec),
        scratch_shapes=[
            pltpu.VMEM((count, blocks * count), jnp.bfloat16),
            pltpu.VMEM((count, 1), jnp.float32),
        ],
        compiler_params=pltpu.CompilerParams(vmem_limit_bytes=32 * 2**20),
        cost_estimate=pl.CostEstimate(
            flops=2 * blocks * count * count * width,
            bytes_accessed=2 * blocks * count * width + 12 * rows * width,
            transcendentals=blocks * count * count,
        ),
        name="gradients",
    )(*known, scale, *recip_rows, *scores, *keys, query_raw, passage_raw)


def per_device(query_raw, passage_raw, pairing):
    size = lax.axis_size("dp")
    chips = size // 2
    rows = query_raw.shape[0]

    def swapped(value, partner_of):
        pairs = []
        for source in range(size):
            target = partner_of(source // 2, source % 2)
            if target is not None:
                pairs.append((source, (target[0] % chips) * 2 + target[1]))
        return lax.ppermute(value, "dp", pairs)

    def other_core(chip, core):
        return (chip, 1 - core)

    def near_chip(chip, core):
        return (chip ^ 1, core)

    def next_chip(chip, core):
        return (chip + 1 if chip % 2 else chip - 1, core)

    def far_over_next(chip, core):
        return (chip + 1 if core else chip - 1, 1 - core) if chip % 2 == core else None

    def far_over_near(chip, core):
        return (chip + 1 if core else chip - 1, 1 - core) if chip % 2 != core else None

    def chip_beyond(chip, core):
        return (chip + 2 if core else chip - 2, 1 - core)

    own, first, second, scale = unit_rows(query_raw, passage_raw)
    paired = (pairing[0][:, None] == jnp.arange(rows, dtype=jnp.int32)[None, :]).astype(jnp.float32)
    blank = jnp.zeros((rows, rows), jnp.float32)
    partner = jnp.block([[blank, paired], [paired.T, blank]])

    near = swapped(own, near_chip)
    next_halves = [swapped(half, next_chip) for half in (first, second)]
    mate = swapped(own, other_core)
    far_first = swapped(near, far_over_next)
    far_second = [swapped(half, far_over_near) for half in next_halves]
    near_mate = swapped(near, other_core)

    count = 2 * rows
    square = (count, count)
    *scores, mass, far_score, passed = score_call(
        early_kernel,
        "early_scores",
        count,
        [square] * 5,
        [partner, own, near, *next_halves],
        [next_halves[0]],
    )
    next_mate = [swapped(half, other_core) for half in (passed, next_halves[1])]
    far_score, mate_score = side_scores(own, mate, far_score, 0)
    far_score = far_scores(own, far_second[0], far_score, 0)
    far_score = far_scores(own, far_second[1], far_score, 1)
    far_score = far_scores(own, far_first, far_score, 0)
    near_mate_score, next_mate_score, recip, spread, losses = score_call(
        total_kernel,
        "totals",
        count,
        [square, square, (1, count), (SPREAD, count), (1, rows)],
        [far_score, mass, scores[0], partner, own, mate_score, near_mate, *next_mate],
    )

    mate_row = swapped(recip, other_core)
    chip_rows = jnp.concatenate([recip, mate_row], axis=0)
    next_rows = swapped(chip_rows, next_chip)
    near_rows = swapped(chip_rows, near_chip)
    far_row = swapped(spread, chip_beyond)

    known = known_weights(partner, [recip, mate_row, far_row], [scores[0], mate_score, far_score])
    query_grad, passage_grad = gradients(
        known,
        scale,
        [recip, next_rows, near_rows],
        scores[1:] + [near_mate_score, next_mate_score],
        [own, mate, near, near_mate, far_first]
        + [next_halves[0], next_mate[0], far_second[0]]
        + [next_halves[1], next_mate[1], far_second[1]],
        query_raw,
        passage_raw,
    )
    return (losses.reshape(rows), query_grad, passage_grad)


def solution(mesh):
    in_specs = (P("dp", None), P("dp", None), P("dp", None))
    out_specs = (P("dp"), P("dp", None), P("dp", None))
    return jax.shard_map(
        per_device, mesh=mesh, in_specs=in_specs, out_specs=out_specs, check_vma=False
    )
```

time: 91.6 us -> 85.7 us (0.936)
  the two profiles are of different devices: /device:TPU:1 before, /device:TPU:32 now
where the time goes in v3:
time: 85.7 us; the launch traced here: 85.1 us
  starting transfers between devices  55.2 us (64%)
  waiting for transfers between devices  17 us (20%)
  Pallas kernels  10.5 us (12%)
  local copies, waits for them, and re-layouts  1.24 us (1%)
  between operations  0.94 us (1%)
    ppermute x14, starting transfers between devices, swapped(): return lax.ppermute(value, 'dp', pairs)  55.2 us
    ppermute x14, waiting for transfers between devices, swapped(): return lax.ppermute(value, 'dp', pairs)  17 us
    pallas_call x6, Pallas kernels, score_call(): pl.pallas_call(body, in_specs=[VMEM] * len(operands), out_specs=[VMEM] *...  3.79 us
    pallas_call x1, Pallas kernels, gradients(): pl.pallas_call(gradient_kernel, out_shape=(out, out), grid=(width // TILE...  3.58 us
    pallas_call x1, Pallas kernels, unit_rows(): pl.pallas_call(unit_kernel, in_specs=[HBM, HBM], out_specs=(VMEM, VMEM, V...  2.93 us
  transfers between devices with their start and end apart: 14, of which 3 were waited for; matrix products, arithmetic and copies ran while one was open for 0% of the time, Pallas kernels for 3%

profile of v3, /device:TPU:32, one launch (start us, length us, event | category | flops | bytes accessed | tf_op | source)
XLA Modules:
  0.0 85.1 jit_solution(13838002402262248117)
XLA Ops:
  0.6 2.9 %unit_rows.1 = (bf16[144,3584]{1,0:T(8,128)(2,1)}, bf16[144,1792]{1,0:T(8,128)(2,1)}, bf16[144,1792]{1,0:T(8,128)(2,1)}, f32[144,1]{1,0:T(8,128)}) custom-call(bf16[72,3584]{1,0:T(8,128)(2,1)} %refs_15_.1, bf16[72,3584]{1,0:T(8,128)(2,1)} %refs_16_.1), custom_call_target="tpu_custom_call" | custom-call | flops 1548288 | bytes 2064384 | tf_op jit(solution)/shard_map/unit_rows/pallas_call | solution.py:61
  3.6 4.3 %collective-permute-start = (bf16[144,3584]{1,0:T(8,128)(2,1)}, bf16[144,3584]{1,0:T(8,128)(2,1)S(1)}, u32[]{:S(2)}, u32[]{:S(2)}) collective-permute-start(bf16[144,3584]{1,0:T(8,128)(2,1)} %get-tuple-element.24.own_ref.refs_4_), channel_id=1, source_target_pairs={{0,2},{1,3},{2,0},{3,1},{4,6},{5,7},{6,4},{7,5},{8,10},{9,11},{10,... | collective-permute-start | bytes 3096584 | tf_op jit(solution)/shard_map/ppermute | solution.py:309
  7.9 11.2 %collective-permute-start.4 = (bf16[144,1792]{1,0:T(8,128)(2,1)}, bf16[144,1792]{1,0:T(8,128)(2,1)S(1)}, u32[]{:S(2)}, u32[]{:S(2)}) collective-permute-start(bf16[144,1792]{1,0:T(8,128)(2,1)} %get-tuple-element.26), channel_id=1, source_target_pairs={{0,510},{1,511},{2,4},{3,5},{4,2},{5,3},{6,8},{7,9},{8,6},{9,7},{1... | collective-permute-start | bytes 1548296 | tf_op jit(solution)/shard_map/ppermute | solution.py:309
  19.1 1.9 %collective-permute-start.6 = (bf16[144,3584]{1,0:T(8,128)(2,1)}, bf16[144,3584]{1,0:T(8,128)(2,1)S(1)}, u32[]{:S(2)}, u32[]{:S(2)}) collective-permute-start(bf16[144,3584]{1,0:T(8,128)(2,1)} %get-tuple-element.24.own_ref.refs_4_), channel_id=1, source_target_pairs={{0,1},{1,0},{2,3},{3,2},{4,5},{5,4},{6,7},{7,6},{8,9},{9,8},{10,11... | collective-permute-start | bytes 3096584 | tf_op jit(solution)/shard_map/ppermute | solution.py:309
  21.0 0.0 copy-start.5
  21.0 1.9 %collective-permute-start.2 = (bf16[144,1792]{1,0:T(8,128)(2,1)}, bf16[144,1792]{1,0:T(8,128)(2,1)S(1)}, u32[]{:S(2)}, u32[]{:S(2)}) collective-permute-start(bf16[144,1792]{1,0:T(8,128)(2,1)} %get-tuple-element.25), channel_id=1, source_target_pairs={{0,510},{1,511},{2,4},{3,5},{4,2},{5,3},{6,8},{7,9},{8,6},{9,7},{1... | collective-permute-start | bytes 1548296 | tf_op jit(solution)/shard_map/ppermute | solution.py:309
  22.9 7.9 %collective-permute-done.near_ref.refs_6_ = bf16[144,3584]{1,0:T(8,128)(2,1)S(1)} collective-permute-done((bf16[144,3584]{1,0:T(8,128)(2,1)}, bf16[144,3584]{1,0:T(8,128)(2,1)S(1)}, u32[]{:S(2)}, u32[]{:S(2)}) %collective-permute-start) | collective-permute-done | bytes 1032224 | tf_op jit(solution)/shard_map/ppermute | solution.py:309
  30.9 10.9 %collective-permute-start.1 = (bf16[144,3584]{1,0:T(8,128)(2,1)S(1)}, bf16[144,3584]{1,0:T(8,128)(2,1)S(1)}, u32[]{:S(2)}, u32[]{:S(2)}) collective-permute-start(bf16[144,3584]{1,0:T(8,128)(2,1)S(1)} %collective-permute-done.near_ref.refs_6_), channel_id=1, source_target_pairs={{0,511},{3,4},{4,3},{7,8},{8,7},{11,12},{12,11},{15,16},{16,15},{1... | collective-permute-start | bytes 3096584 | tf_op jit(solution)/shard_map/ppermute | solution.py:309
  41.8 0.0 collective-permute-done.4.next_first.refs_9_
  41.8 0.7 collective-permute-start.5
  42.5 1.9 %collective-permute-start.7 = (bf16[144,3584]{1,0:T(8,128)(2,1)S(1)}, bf16[144,3584]{1,0:T(8,128)(2,1)S(1)}, u32[]{:S(2)}, u32[]{:S(2)}) collective-permute-start(bf16[144,3584]{1,0:T(8,128)(2,1)S(1)} %collective-permute-done.near_ref.refs_6_), channel_id=1, source_target_pairs={{0,1},{1,0},{2,3},{3,2},{4,5},{5,4},{6,7},{7,6},{8,9},{9,8},{10,11... | collective-permute-start | bytes 3096584 | tf_op jit(solution)/shard_map/ppermute | solution.py:309
  44.5 0.0 copy-done.5
  44.5 0.1 iota_compare_fusion.1
  44.5 0.0 collective-permute-done.2.next_second.refs_12_
  44.6 0.7 collective-permute-start.3
  45.3 0.1 fusion.partner_ref
  45.4 0.0 copy-start
  45.4 1.2 %copy-done = bf16[144,3584]{1,0:T(8,128)(2,1)S(1)} copy-done((bf16[144,3584]{1,0:T(8,128)(2,1)S(1)}, bf16[144,3584]{1,0:T(8,128)(2,1)}, u32[]{:S(2)}) %copy-start) | copy-done | bytes 1032216
  46.6 1.0 %early_scores.1 = (f32[144,144]{1,0:T(8,128)S(1)}, f32[144,144]{1,0:T(8,128)S(1)}, f32[144,144]{1,0:T(8,128)S(1)}, f32[144,144]{1,0:T(8,128)S(1)}, f32[144,144]{...) custom-call(f32[144,144]{1,0:T(8,128)S(1)} %fusion.partner_ref, bf16[144,3584]{1,0:T(8,128)(2,1)S(1)} %copy-done, ...), custom_call_target="tpu_custom_call" | custom-call | flops 451878912 | bytes 3138048 | tf_op jit(solution)/shard_map/early_scores/pallas_call | solution.py:81
  47.6 0.0 collective-permute-done.5.far_ref.refs_11_
  47.6 3.6 %collective-permute-start.9 = (bf16[144,1792]{1,0:T(8,128)(2,1)S(1)}, bf16[144,1792]{1,0:T(8,128)(2,1)S(1)}, u32[]{:S(2)}, u32[]{:S(2)}) collective-permute-start(bf16[144,1792]{1,0:T(8,128)(2,1)S(1)} %collective-permute-done.2.next_second.refs_12_), channel_id=1, source_target_pairs={{0,1},{1,0},{2,3},{3,2},{4,5},{5,4},{6,7},{7,6},{8,9},{9,8},{10,11... | collective-permute-start | bytes 1548296 | tf_op jit(solution)/shard_map/ppermute | solution.py:309
  51.2 0.0 collective-permute-done.6.key_ref.refs_5_
  51.2 1.9 %collective-permute-start.8 = (bf16[144,1792]{1,0:T(8,128)(2,1)S(1)}, bf16[144,1792]{1,0:T(8,128)(2,1)S(1)}, u32[]{:S(2)}, u32[]{:S(2)}) collective-permute-start(bf16[144,1792]{1,0:T(8,128)(2,1)S(1)} %get-tuple-element.32), channel_id=1, source_target_pairs={{0,1},{1,0},{2,3},{3,2},{4,5},{5,4},{6,7},{7,6},{8,9},{9,8},{10,11... | collective-permute-start | bytes 1548296 | tf_op jit(solution)/shard_map/ppermute | solution.py:309
  53.2 0.4 side_scores.1
  53.6 0.3 far_scores.3.sum_ref
  53.9 0.0 collective-permute-done.3.far_ref.refs_14_
  53.9 0.3 far_scores.4.sum_ref
  54.2 0.0 collective-permute-done.1.far_ref.refs_8_
  54.3 0.4 far_scores.5.far_score_ref.far_score
  54.7 0.0 collective-permute-done.9.mate_second.refs_13_
  54.7 0.3 collective-permute-done.8.mate_first.refs_10_
  55.0 0.0 collective-permute-done.7.near_mate_ref.refs_7_
  55.0 1.3 %totals.1 = (f32[144,144]{1,0:T(8,128)S(1)}, f32[144,144]{1,0:T(8,128)S(1)}, f32[1,144]{1,0:T(1,128)S(1)}, f32[8,144]{1,0:T(8,128)S(1)}, f32[1,72]{1,0:T(1,128)}) custom-call(f32[144,144]{1,0:T(8,128)S(1)} %far_scores.5.far_score_ref.far_score, f32[144,144]{1,0:T(8,128)S(1)} %get-tuple-element.29.mass_ref, ...), custom_call_target="tpu_custom_call" | custom-call | flops 475766784 | bytes 3303936 | tf_op jit(solution)/shard_map/totals/pallas_call | solution.py:81
  56.4 3.3 %collective-permute-start.10 = (f32[1,144]{1,0:T(1,128)S(1)}, f32[1,144]{1,0:T(1,128)S(1)}, u32[]{:S(2)}, u32[]{:S(2)}) collective-permute-start(f32[1,144]{1,0:T(1,128)S(1)} %get-tuple-element.34.own_row), channel_id=1, source_target_pairs={{0,1},{1,0},{2,3},{3,2},{4,5},{5,4},{6,7},{7,6},{8,9},{9,8},{10,11... | collective-permute-start | bytes 1736 | tf_op jit(solution)/shard_map/ppermute | solution.py:309
  59.7 6.2 %collective-permute-start.11 = (f32[8,144]{1,0:T(8,128)S(1)}, f32[8,144]{1,0:T(8,128)S(1)}, u32[]{:S(2)}, u32[]{:S(2)}) collective-permute-start(f32[8,144]{1,0:T(8,128)S(1)} %get-tuple-element.35), channel_id=1, source_target_pairs={{0,509},{1,4},{2,511},{3,6},{4,1},{5,8},{6,3},{7,10},{8,5},{9,12},... | collective-permute-start | bytes 13832 | tf_op jit(solution)/shard_map/ppermute | solution.py:309
  65.9 0.0 collective-permute-done.10.mate_row
  65.9 0.0 copy-start.4
  65.9 4.7 %collective-permute-start.13 = (f32[2,144]{1,0:T(2,128)S(1)}, f32[2,144]{1,0:T(2,128)S(1)}, u32[]{:S(2)}, u32[]{:S(2)}) collective-permute-start(f32[2,144]{1,0:T(2,128)S(1)} %pad_maximum_fusion), channel_id=1, source_target_pairs={{0,2},{1,3},{2,0},{3,1},{4,6},{5,7},{6,4},{7,5},{8,10},{9,11},{10,... | collective-permute-start | bytes 3464 | tf_op jit(solution)/shard_map/ppermute | solution.py:309
  70.6 1.9 %collective-permute-start.12 = (f32[2,144]{1,0:T(2,128)S(1)}, f32[2,144]{1,0:T(2,128)S(1)}, u32[]{:S(2)}, u32[]{:S(2)}) collective-permute-start(f32[2,144]{1,0:T(2,128)S(1)} %pad_maximum_fusion), channel_id=1, source_target_pairs={{0,510},{1,511},{2,4},{3,5},{4,2},{5,3},{6,8},{7,9},{8,6},{9,7},{1... | collective-permute-start | bytes 3464 | tf_op jit(solution)/shard_map/ppermute | solution.py:309
  72.5 0.0 collective-permute-done.11.far_row
  72.5 0.2 known_weights.1
  72.8 0.0 collective-permute-done.13.near_rows
  72.8 8.8 %collective-permute-done.12.next_rows = f32[2,144]{1,0:T(2,128)S(1)} collective-permute-done((f32[2,144]{1,0:T(2,128)S(1)}, f32[2,144]{1,0:T(2,128)S(1)}, u32[]{:S(2)}, u32[]{:S(2)}) %collective-permute-start.12) | collective-permute-done | bytes 1184 | tf_op jit(solution)/shard_map/ppermute | solution.py:309
  81.5 0.0 copy-done.1
  81.5 0.0 copy-done.3
  81.5 0.0 copy-done.2
  81.5 0.0 copy-done.4
  81.5 3.6 %gradients.1 = (f32[72,3584]{1,0:T(8,128)}, f32[72,3584]{1,0:T(8,128)}) custom-call(bf16[3,144,144]{2,1,0:T(8,128)(2,1)S(1)} %get-tuple-element.36.known_ref, f32[144,144]{1,0:T(8,128)S(1)} %get-tuple-element.37.along_ref, f32[144,1]{1,0:T(8,128)S(1)} %copy-done.4, f32[1,144]{1,0:T(1,128)S(1)} %get-tuple-element.34.own_row, ...), custom_call_target="tpu_custom_call" | custom-call | flops 1040449536 | bytes 10321920 | tf_op jit(solution)/shard_map/gradients/pallas_call | solution.py:278
  (4 shorter events, 0.0 us)
Async XLA Ops:
  3.6 27.3 %collective-permute-start = (bf16[144,3584]{1,0:T(8,128)(2,1)}, bf16[144,3584]{1,0:T(8,128)(2,1)S(1)}, u32[]{:S(2)}, u32[]{:S(2)}) collective-permute-start(bf16[144,3584]{1,0:T(8,128)(2,1)} %get-tuple-element.24.own_ref.refs_4_), channel_id=1, source_target_pairs={{0,2},{1,3},{2,0},{3,1},{4,6},{5,7},{6,4},{7,5},{8,10},{9,11},{10,... | collective-permute-start | bytes 3096584 | tf_op jit(solution)/shard_map/ppermute | solution.py:309
  7.9 34.0 %collective-permute-start.4 = (bf16[144,1792]{1,0:T(8,128)(2,1)}, bf16[144,1792]{1,0:T(8,128)(2,1)S(1)}, u32[]{:S(2)}, u32[]{:S(2)}) collective-permute-start(bf16[144,1792]{1,0:T(8,128)(2,1)} %get-tuple-element.26), channel_id=1, source_target_pairs={{0,510},{1,511},{2,4},{3,5},{4,2},{5,3},{6,8},{7,9},{8,6},{9,7},{1... | collective-permute-start | bytes 1548296 | tf_op jit(solution)/shard_map/ppermute | solution.py:309
  19.1 32.2 %collective-permute-start.6 = (bf16[144,3584]{1,0:T(8,128)(2,1)}, bf16[144,3584]{1,0:T(8,128)(2,1)S(1)}, u32[]{:S(2)}, u32[]{:S(2)}) collective-permute-start(bf16[144,3584]{1,0:T(8,128)(2,1)} %get-tuple-element.24.own_ref.refs_4_), channel_id=1, source_target_pairs={{0,1},{1,0},{2,3},{3,2},{4,5},{5,4},{6,7},{7,6},{8,9},{9,8},{10,11... | collective-permute-start | bytes 3096584 | tf_op jit(solution)/shard_map/ppermute | solution.py:309
  21.0 23.5 %copy-start.5 = (s32[1,72]{1,0:T(1,128)S(1)}, s32[1,72]{1,0:T(1,128)}, u32[]{:S(2)}) copy-start(s32[1,72]{1,0:T(1,128)} %param.5) | copy-start | bytes 868
  21.0 23.5 %collective-permute-start.2 = (bf16[144,1792]{1,0:T(8,128)(2,1)}, bf16[144,1792]{1,0:T(8,128)(2,1)S(1)}, u32[]{:S(2)}, u32[]{:S(2)}) collective-permute-start(bf16[144,1792]{1,0:T(8,128)(2,1)} %get-tuple-element.25), channel_id=1, source_target_pairs={{0,510},{1,511},{2,4},{3,5},{4,2},{5,3},{6,8},{7,9},{8,6},{9,7},{1... | collective-permute-start | bytes 1548296 | tf_op jit(solution)/shard_map/ppermute | solution.py:309
  30.9 23.4 %collective-permute-start.1 = (bf16[144,3584]{1,0:T(8,128)(2,1)S(1)}, bf16[144,3584]{1,0:T(8,128)(2,1)S(1)}, u32[]{:S(2)}, u32[]{:S(2)}) collective-permute-start(bf16[144,3584]{1,0:T(8,128)(2,1)S(1)} %collective-permute-done.near_ref.refs_6_), channel_id=1, source_target_pairs={{0,511},{3,4},{4,3},{7,8},{8,7},{11,12},{12,11},{15,16},{16,15},{1... | collective-permute-start | bytes 3096584 | tf_op jit(solution)/shard_map/ppermute | solution.py:309
  41.8 5.8 %collective-permute-start.5 = (bf16[144,1792]{1,0:T(8,128)(2,1)S(1)}, bf16[144,1792]{1,0:T(8,128)(2,1)S(1)}, u32[]{:S(2)}, u32[]{:S(2)}) collective-permute-start(bf16[144,1792]{1,0:T(8,128)(2,1)S(1)} %collective-permute-done.4.next_first.refs_9_), channel_id=1, source_target_pairs={{1,2},{2,1},{5,6},{6,5},{9,10},{10,9},{13,14},{14,13},{17,18},{18,... | collective-permute-start | bytes 1548296 | tf_op jit(solution)/shard_map/ppermute | solution.py:309
  42.5 12.5 %collective-permute-start.7 = (bf16[144,3584]{1,0:T(8,128)(2,1)S(1)}, bf16[144,3584]{1,0:T(8,128)(2,1)S(1)}, u32[]{:S(2)}, u32[]{:S(2)}) collective-permute-start(bf16[144,3584]{1,0:T(8,128)(2,1)S(1)} %collective-permute-done.near_ref.refs_6_), channel_id=1, source_target_pairs={{0,1},{1,0},{2,3},{3,2},{4,5},{5,4},{6,7},{7,6},{8,9},{9,8},{10,11... | collective-permute-start | bytes 3096584 | tf_op jit(solution)/shard_map/ppermute | solution.py:309
  44.6 9.4 %collective-permute-start.3 = (bf16[144,1792]{1,0:T(8,128)(2,1)S(1)}, bf16[144,1792]{1,0:T(8,128)(2,1)S(1)}, u32[]{:S(2)}, u32[]{:S(2)}) collective-permute-start(bf16[144,1792]{1,0:T(8,128)(2,1)S(1)} %collective-permute-done.2.next_second.refs_12_), channel_id=1, source_target_pairs={{1,2},{2,1},{5,6},{6,5},{9,10},{10,9},{13,14},{14,13},{17,18},{18,... | collective-permute-start | bytes 1548296 | tf_op jit(solution)/shard_map/ppermute | solution.py:309
  45.4 1.2 %copy-start = (bf16[144,3584]{1,0:T(8,128)(2,1)S(1)}, bf16[144,3584]{1,0:T(8,128)(2,1)}, u32[]{:S(2)}) copy-start(bf16[144,3584]{1,0:T(8,128)(2,1)} %get-tuple-element.24.own_ref.refs_4_) | copy-start | bytes 3096580
  47.6 7.1 %collective-permute-start.9 = (bf16[144,1792]{1,0:T(8,128)(2,1)S(1)}, bf16[144,1792]{1,0:T(8,128)(2,1)S(1)}, u32[]{:S(2)}, u32[]{:S(2)}) collective-permute-start(bf16[144,1792]{1,0:T(8,128)(2,1)S(1)} %collective-permute-done.2.next_second.refs_12_), channel_id=1, source_target_pairs={{0,1},{1,0},{2,3},{3,2},{4,5},{5,4},{6,7},{7,6},{8,9},{9,8},{10,11... | collective-permute-start | bytes 1548296 | tf_op jit(solution)/shard_map/ppermute | solution.py:309
  51.2 3.8 %collective-permute-start.8 = (bf16[144,1792]{1,0:T(8,128)(2,1)S(1)}, bf16[144,1792]{1,0:T(8,128)(2,1)S(1)}, u32[]{:S(2)}, u32[]{:S(2)}) collective-permute-start(bf16[144,1792]{1,0:T(8,128)(2,1)S(1)} %get-tuple-element.32), channel_id=1, source_target_pairs={{0,1},{1,0},{2,3},{3,2},{4,5},{5,4},{6,7},{7,6},{8,9},{9,8},{10,11... | collective-permute-start | bytes 1548296 | tf_op jit(solution)/shard_map/ppermute | solution.py:309
  55.0 26.5 %copy-start.1 = (bf16[144,3584]{1,0:T(8,128)(2,1)S(1)}, bf16[144,3584]{1,0:T(8,128)(2,1)}, u32[]{:S(2)}) copy-start(bf16[144,3584]{1,0:T(8,128)(2,1)} %get-tuple-element.24.own_ref.refs_4_) | copy-start | bytes 3096580
  55.0 26.5 %copy-start.3 = (bf16[72,3584]{1,0:T(8,128)(2,1)S(1)}, bf16[72,3584]{1,0:T(8,128)(2,1)}, u32[]{:S(2)}) copy-start(bf16[72,3584]{1,0:T(8,128)(2,1)} %refs_16_.1) | copy-start | bytes 1548292
  56.4 25.1 %copy-start.2 = (bf16[72,3584]{1,0:T(8,128)(2,1)S(1)}, bf16[72,3584]{1,0:T(8,128)(2,1)}, u32[]{:S(2)}) copy-start(bf16[72,3584]{1,0:T(8,128)(2,1)} %refs_15_.1) | copy-start | bytes 1548292
  56.4 9.5 %collective-permute-start.10 = (f32[1,144]{1,0:T(1,128)S(1)}, f32[1,144]{1,0:T(1,128)S(1)}, u32[]{:S(2)}, u32[]{:S(2)}) collective-permute-start(f32[1,144]{1,0:T(1,128)S(1)} %get-tuple-element.34.own_row), channel_id=1, source_target_pairs={{0,1},{1,0},{2,3},{3,2},{4,5},{5,4},{6,7},{7,6},{8,9},{9,8},{10,11... | collective-permute-start | bytes 1736 | tf_op jit(solution)/shard_map/ppermute | solution.py:309
  59.7 12.9 %collective-permute-start.11 = (f32[8,144]{1,0:T(8,128)S(1)}, f32[8,144]{1,0:T(8,128)S(1)}, u32[]{:S(2)}, u32[]{:S(2)}) collective-permute-start(f32[8,144]{1,0:T(8,128)S(1)} %get-tuple-element.35), channel_id=1, source_target_pairs={{0,509},{1,4},{2,511},{3,6},{4,1},{5,8},{6,3},{7,10},{8,5},{9,12},... | collective-permute-start | bytes 13832 | tf_op jit(solution)/shard_map/ppermute | solution.py:309
  65.9 15.6 %copy-start.4 = (f32[144,1]{1,0:T(8,128)S(1)}, f32[144,1]{1,0:T(8,128)}, u32[]{:S(2)}) copy-start(f32[144,1]{1,0:T(8,128)} %get-tuple-element.38.scale_ref) | copy-start | bytes 1732
  65.9 6.8 %collective-permute-start.13 = (f32[2,144]{1,0:T(2,128)S(1)}, f32[2,144]{1,0:T(2,128)S(1)}, u32[]{:S(2)}, u32[]{:S(2)}) collective-permute-start(f32[2,144]{1,0:T(2,128)S(1)} %pad_maximum_fusion), channel_id=1, source_target_pairs={{0,2},{1,3},{2,0},{3,1},{4,6},{5,7},{6,4},{7,5},{8,10},{9,11},{10,... | collective-permute-start | bytes 3464 | tf_op jit(solution)/shard_map/ppermute | solution.py:309
  70.6 10.9 %collective-permute-start.12 = (f32[2,144]{1,0:T(2,128)S(1)}, f32[2,144]{1,0:T(2,128)S(1)}, u32[]{:S(2)}, u32[]{:S(2)}) collective-permute-start(f32[2,144]{1,0:T(2,128)S(1)} %pad_maximum_fusion), channel_id=1, source_target_pairs={{0,510},{1,511},{2,4},{3,5},{4,2},{5,3},{6,8},{7,9},{8,6},{9,7},{1... | collective-permute-start | bytes 3464 | tf_op jit(solution)/shard_map/ppermute | solution.py:309

commit v4 on v3

--- a/solution.py
+++ b/solution.py
@@ -169,130 +169,136 @@
     loss_ref[...] = losses[:, : loss_ref.shape[1]]
 
 
-def known_kernel(
-    partner_ref, own_row, mate_row, far_row, own_score, mate_score, far_score, weight_ref, dot_ref
+def weigh(score, recip_col, recip_row):
+    weight = exp_score(score) * (recip_col + recip_row)
+    low = weight.astype(jnp.bfloat16)
+    return low, low.astype(jnp.float32) * score
+
+
+def column_of(row):
+    return jnp.sum(eye_of(row.shape[1]) * row, axis=1, keepdims=True)
+
+
+def part_kernel(
+    partner_ref, own_row, mate_row, far_row, next_rows, own_score, mate_score, far_score, next_score,
+    next_mate_score, own_ref, mate_ref, far_first, far_0, far_1, next_0, next_1, pair_0, pair_1,
+    sum_ref, along_ref,
 ):
     partner = partner_ref[...]
-    eye = eye_of(partner.shape[0])
-    recip_col = jnp.sum(eye * own_row[...], axis=1, keepdims=True)
-    along = jnp.zeros(partner.shape, jnp.float32)
-    for index, (row_ref, score_ref) in enumerate(
-        ((own_row, own_score), (mate_row, mate_score), (far_row, far_score))
+    count = partner.shape[0]
+    recip_row = own_row[...]
+    recip_col = column_of(recip_row)
+    score = own_score[...]
+    weight = exp_score(score) * (recip_col + recip_row)
+    weight = weight * (1.0 - eye_of(count)) * (1.0 - 0.5 * partner) - partner
+    low = weight.astype(jnp.bfloat16)
+    weights = [low]
+    along = low.astype(jnp.float32) * score
+    for score_ref, row in (
+        (mate_score, mate_row[...]),
+        (far_score, far_row[0:1, :]),
+        (next_score, next_rows[0:1, :]),
+        (next_mate_score, next_rows[1:2, :]),
     ):
-        score = score_ref[...]
-        weight = exp_score(score) * (recip_col + row_ref[0:1, :])
-        if index == 0:
-            weight = weight * (1.0 - eye) * (1.0 - 0.5 * partner) - partner
-        low = weight.astype(jnp.bfloat16)
-        along = along + low.astype(jnp.float32) * score
-        weight_ref[index] = low
-    dot_ref[...] = along
-
-
-def known_weights(partner, rows, scores):
-    count = partner.shape[0]
-    return pl.pallas_call(
-        known_kernel,
-        in_specs=[VMEM] * 7,
-        out_specs=(VMEM, VMEM),
-        out_shape=(
-            jax.ShapeDtypeStruct((3, count, count), jnp.bfloat16),
-            jax.ShapeDtypeStruct((count, count), jnp.float32),
-        ),
-        compiler_params=pltpu.CompilerParams(vmem_limit_bytes=16 * 2**20),
-        cost_estimate=pl.CostEstimate(
-            flops=40 * count * count,
-            bytes_accessed=32 * count * count,
-            transcendentals=3 * count * count,
-        ),
-        name="known_weights",
-    )(partner, *rows, *scores)
-
-
-def gradient_kernel(
-    known_ref, along_ref, scale_ref, own_row, next_rows, near_rows, *refs
-):
-    score_refs = refs[:4]
-    own_ref, mate_ref, near_ref, near_mate, far_first = refs[4:9]
-    half_refs = refs[9:12], refs[12:15]
-    query_ref, passage_ref, query_out, passage_out, weight_ref, dot_ref = refs[15:]
-    count = along_ref.shape[0]
-    rows = count // 2
-    step = pl.program_id(0)
-
-    @pl.when(step == 0)
-    def _():
-        recip_col = jnp.sum(eye_of(count) * own_row[...], axis=1, keepdims=True)
-        along = along_ref[...]
-        recip_rows = [near_rows[0:1, :], next_rows[0:1, :], near_rows[1:2, :], next_rows[1:2, :]]
-        weights = [known_ref[0], known_ref[1]]
-        for score_ref, recip_row in zip(score_refs, recip_rows):
-            score = score_ref[...]
-            low = (exp_score(score) * (recip_col + recip_row)).astype(jnp.bfloat16)
-            along = along + low.astype(jnp.float32) * score
-            weights.append(low)
-        weights.append(known_ref[2])
-        weight_ref[...] = jnp.concatenate(weights, axis=1)
-        dot_ref[...] = INV_TEMP * jnp.sum(along, axis=1, keepdims=True)
-
-    half_steps = pl.num_programs(0) // 2
-    whole = pl.ds(pl.multiple_of(step * TILE, TILE), TILE)
-
-    def emit(half):
-        next_ref, next_mate, far_second = half_refs[half]
-        columns = pl.ds(pl.multiple_of((step - half * half_steps) * TILE, TILE), TILE)
+        low, share = weigh(score_ref[...], recip_col, row)
+        weights.append(low)
+        along = along + share
+    along_ref[...] = along
+    weights = jnp.concatenate(weights, axis=1)
+    half = next_0.shape[1]
+    for start in range(0, own_ref.shape[1], TILE):
+        whole = slice(start, start + TILE)
+        columns = slice(start % half, start % half + TILE)
+        far_ref, next_ref, pair_ref = ((far_0, next_0, pair_0), (far_1, next_1, pair_1))[start // half]
         keys = [
             own_ref[:, whole],
             mate_ref[:, whole],
-            near_ref[:, whole],
+            far_first[:, whole] + far_ref[:, columns],
             next_ref[:, columns],
-            near_mate[:, whole],
-            next_mate[:, columns],
-            far_first[:, whole] + far_second[:, columns],
+            pair_ref[:, columns],
         ]
         keys = jnp.concatenate(keys, axis=0)
-        gradient = jnp.dot(weight_ref[...], keys, preferred_element_type=jnp.float32)
-        scale = scale_ref[...]
-        along = dot_ref[...]
-        for part, raw_ref, out_ref in ((0, query_ref, query_out), (1, passage_ref, passage_out)):
+        sum_ref[:, whole] = jnp.dot(weights, keys, preferred_element_type=jnp.float32)
+
+
+def part_gradients(partner, rows, scores, keys):
+    count = partner.shape[0]
+    width = keys[0].shape[1]
+    operands = [partner, *rows, *scores, *keys]
+    return pl.pallas_call(
+        part_kernel,
+        in_specs=[VMEM] * len(operands),
+        out_specs=(VMEM, VMEM),
+        out_shape=(
+            jax.ShapeDtypeStruct((count, width), jnp.float32),
+            jax.ShapeDtypeStruct((count, count), jnp.float32),
+        ),
+        compiler_params=pltpu.CompilerParams(vmem_limit_bytes=24 * 2**20),
+        cost_estimate=pl.CostEstimate(
+            flops=10 * count * count * width,
+            bytes_accessed=16 * count * width,
+            transcendentals=5 * count * count,
+        ),
+        name="part_gradients",
+    )(*operands)
+
+
+def gradient_kernel(
+    sum_ref, along_ref, scale_ref, own_row, near_rows, near_score, pair_score, near_ref, pair_ref,
+    query_ref, passage_ref, query_out, passage_out, query_hold, passage_hold, sems,
+):
+    count = along_ref.shape[0]
+    rows = count // 2
+    recip_col = column_of(own_row[...])
+    near_low, near_share = weigh(near_score[...], recip_col, near_rows[0:1, :])
+    pair_low, pair_share = weigh(pair_score[...], recip_col, near_rows[1:2, :])
+    along = along_ref[...] + near_share + pair_share
+    along = INV_TEMP * jnp.sum(along, axis=1, keepdims=True)
+    weights = jnp.concatenate([near_low, pair_low], axis=1)
+    scale = scale_ref[...]
+    copies = []
+    for start in range(0, near_ref.shape[1], TILE):
+        whole = slice(start, start + TILE)
+        keys = jnp.concatenate([near_ref[:, whole], pair_ref[:, whole]], axis=0)
+        gradient = jnp.dot(weights, keys, preferred_element_type=jnp.float32) + sum_ref[:, whole]
+        for part, raw_ref, hold, out in (
+            (0, query_ref, query_hold, query_out),
+            (1, passage_ref, passage_hold, passage_out),
+        ):
             span = slice(part * rows, (part + 1) * rows)
             unit = raw_ref[:, whole].astype(jnp.float32) * scale[span]
-            out_ref[...] = (INV_TEMP * gradient[span] - unit * along[span]) * scale[span]
-
-    @pl.when(step < half_steps)
-    def _():
-        emit(0)
-
-    @pl.when(step >= half_steps)
-    def _():
-        emit(1)
-
-
-def gradients(known, scale, recip_rows, scores, keys, query_raw, passage_raw):
-    blocks = 7
-    rows, width = query_raw.shape
-    count = 2 * rows
-    out = jax.ShapeDtypeStruct((rows, width), jnp.float32)
-    out_spec = pl.BlockSpec((rows, TILE), lambda step: (0, step))
-
+            hold[:, whole] = (INV_TEMP * gradient[span] - unit * along[span]) * scale[span]
+            copy = pltpu.make_async_copy(
+                hold.at[:, whole], out.at[:, whole], sems.at[len(copies)]
+            )
+            copy.start()
+            copies.append(copy)
+    for copy in copies:
+        copy.wait()
+
+
+def gradients(part_sum, along, scale, rows, scores, keys, query_raw, passage_raw):
+    count, width = part_sum.shape
+    out = jax.ShapeDtypeStruct((count // 2, width), jnp.float32)
+    operands = [part_sum, along, scale, *rows, *scores, *keys, query_raw, passage_raw]
     return pl.pallas_call(
         gradient_kernel,
+        in_specs=[VMEM] * len(operands),
+        out_specs=(HBM, HBM),
         out_shape=(out, out),
-        grid=(width // TILE,),
-        in_specs=[VMEM] * (12 + len(scores) + len(keys) - 4),
-        out_specs=(out_spec, out_spec),
         scratch_shapes=[
-            pltpu.VMEM((count, blocks * count), jnp.bfloat16),
-            pltpu.VMEM((count, 1), jnp.float32),
+            pltpu.VMEM((count // 2, width), jnp.float32),
+            pltpu.VMEM((count // 2, width), jnp.float32),
+            pltpu.SemaphoreType.DMA((2 * width // TILE,)),
         ],
-        compiler_params=pltpu.CompilerParams(vmem_limit_bytes=32 * 2**20),
+        compiler_params=pltpu.CompilerParams(vmem_limit_bytes=24 * 2**20),
         cost_estimate=pl.CostEstimate(
-            flops=2 * blocks * count * count * width,
-            bytes_accessed=2 * blocks * count * width + 12 * rows * width,
-            transcendentals=blocks * count * count,
+            flops=4 * count * count * width,
+            bytes_accessed=12 * count * width,
+            transcendentals=2 * count * count,
         ),
         name="gradients",
-    )(*known, scale, *recip_rows, *scores, *keys, query_raw, passage_raw)
+    )(*operands)
 
 
 def per_device(query_raw, passage_raw, pairing):
@@ -363,19 +369,24 @@
 
     mate_row = swapped(recip, other_core)
     chip_rows = jnp.concatenate([recip, mate_row], axis=0)
+    near_rows = swapped(chip_rows, near_chip)
     next_rows = swapped(chip_rows, next_chip)
-    near_rows = swapped(chip_rows, near_chip)
     far_row = swapped(spread, chip_beyond)
 
-    known = known_weights(partner, [recip, mate_row, far_row], [scores[0], mate_score, far_score])
+    near_score, next_score = scores[1:]
+    part_sum, along = part_gradients(
+        partner,
+        [recip, mate_row, far_row, next_rows],
+        [scores[0], mate_score, far_score, next_score, next_mate_score],
+        [own, mate, far_first, *far_second, *next_halves, *next_mate],
+    )
     query_grad, passage_grad = gradients(
-        known,
+        part_sum,
+        along,
         scale,
-        [recip, next_rows, near_rows],
-        scores[1:] + [near_mate_score, next_mate_score],
-        [own, mate, near, near_mate, far_first]
-        + [next_halves[0], next_mate[0], far_second[0]]
-        + [next_halves[1], next_mate[1], far_second[1]],
+        [recip, near_rows],
+        [near_score, near_mate_score],
+        [near, near_mate],
         query_raw,
         passage_raw,
     )

time: 85.7 us -> 82.8 us (0.966)
  the two profiles are of different devices: /device:TPU:32 before, /device:TPU:1 now
where the time goes in v4:
time: 82.8 us; the launch traced here: 82.3 us
  starting transfers between devices  61.3 us (74%)
  Pallas kernels  10.1 us (12%)
  waiting for transfers between devices  7.84 us (9%)
  local copies, waits for them, and re-layouts  1.24 us (1%)
  between operations  0.95 us (1%)
  other arithmetic  0.91 us (1%)
    ppermute x14, starting transfers between devices, swapped(): return lax.ppermute(value, 'dp', pairs)  61.3 us
    ppermute x14, waiting for transfers between devices, swapped(): return lax.ppermute(value, 'dp', pairs)  7.84 us
    pallas_call x6, Pallas kernels, score_call(): pl.pallas_call(body, in_specs=[VMEM] * len(operands), out_specs=[VMEM] *...  3.81 us
    pallas_call x1, Pallas kernels, unit_rows(): pl.pallas_call(unit_kernel, in_specs=[HBM, HBM], out_specs=(VMEM, VMEM, V...  2.91 us
    pallas_call x1, Pallas kernels, gradients(): pl.pallas_call(gradient_kernel, in_specs=[VMEM] * len(operands), out_spec...  1.95 us
  transfers between devices with their start and end apart: 14, of which 3 were waited for; matrix products, arithmetic and copies ran while one was open for 1% of the time, Pallas kernels for 5%

profile of v4, /device:TPU:1, one launch (start us, length us, event | category | flops | bytes accessed | tf_op | source)
XLA Modules:
  0.0 82.3 jit_solution(13291205892940799677)
XLA Ops:
  0.6 2.9 %unit_rows.1 = (bf16[144,3584]{1,0:T(8,128)(2,1)}, bf16[144,1792]{1,0:T(8,128)(2,1)}, bf16[144,1792]{1,0:T(8,128)(2,1)}, f32[144,1]{1,0:T(8,128)}) custom-call(bf16[72,3584]{1,0:T(8,128)(2,1)} %query_ref.1, bf16[72,3584]{1,0:T(8,128)(2,1)} %passage_ref.1), custom_call_target="tpu_custom_call" | custom-call | flops 1548288 | bytes 2064384 | tf_op jit(solution)/shard_map/unit_rows/pallas_call | solution.py:61
  3.5 4.8 %collective-permute-start = (bf16[144,3584]{1,0:T(8,128)(2,1)}, bf16[144,3584]{1,0:T(8,128)(2,1)S(1)}, u32[]{:S(2)}, u32[]{:S(2)}) collective-permute-start(bf16[144,3584]{1,0:T(8,128)(2,1)} %get-tuple-element.24.own_ref), channel_id=1, source_target_pairs={{0,2},{1,3},{2,0},{3,1},{4,6},{5,7},{6,4},{7,5},{8,10},{9,11},{10,... | collective-permute-start | bytes 3096584 | tf_op jit(solution)/shard_map/ppermute | solution.py:315
  8.4 13.9 %collective-permute-start.4 = (bf16[144,1792]{1,0:T(8,128)(2,1)}, bf16[144,1792]{1,0:T(8,128)(2,1)S(1)}, u32[]{:S(2)}, u32[]{:S(2)}) collective-permute-start(bf16[144,1792]{1,0:T(8,128)(2,1)} %get-tuple-element.26), channel_id=1, source_target_pairs={{0,510},{1,511},{2,4},{3,5},{4,2},{5,3},{6,8},{7,9},{8,6},{9,7},{1... | collective-permute-start | bytes 1548296 | tf_op jit(solution)/shard_map/ppermute | solution.py:315
  22.3 3.1 %collective-permute-start.6 = (bf16[144,3584]{1,0:T(8,128)(2,1)}, bf16[144,3584]{1,0:T(8,128)(2,1)S(1)}, u32[]{:S(2)}, u32[]{:S(2)}) collective-permute-start(bf16[144,3584]{1,0:T(8,128)(2,1)} %get-tuple-element.24.own_ref), channel_id=1, source_target_pairs={{0,1},{1,0},{2,3},{3,2},{4,5},{5,4},{6,7},{7,6},{8,9},{9,8},{10,11... | collective-permute-start | bytes 3096584 | tf_op jit(solution)/shard_map/ppermute | solution.py:315
  25.5 1.9 %collective-permute-start.2 = (bf16[144,1792]{1,0:T(8,128)(2,1)}, bf16[144,1792]{1,0:T(8,128)(2,1)S(1)}, u32[]{:S(2)}, u32[]{:S(2)}) collective-permute-start(bf16[144,1792]{1,0:T(8,128)(2,1)} %get-tuple-element.25), channel_id=1, source_target_pairs={{0,510},{1,511},{2,4},{3,5},{4,2},{5,3},{6,8},{7,9},{8,6},{9,7},{1... | collective-permute-start | bytes 1548296 | tf_op jit(solution)/shard_map/ppermute | solution.py:315
  27.4 0.0 collective-permute-done.near_ref
  27.4 0.7 collective-permute-start.1
  28.2 5.5 %collective-permute-done.4.next_first.next_0 = bf16[144,1792]{1,0:T(8,128)(2,1)S(1)} collective-permute-done((bf16[144,1792]{1,0:T(8,128)(2,1)}, bf16[144,1792]{1,0:T(8,128)(2,1)S(1)}, u32[]{:S(2)}, u32[]{:S(2)}) %collective-permute-start.4) | collective-permute-done | bytes 516128 | tf_op jit(solution)/shard_map/ppermute | solution.py:315
  33.7 2.6 %collective-permute-start.5 = (bf16[144,1792]{1,0:T(8,128)(2,1)S(1)}, bf16[144,1792]{1,0:T(8,128)(2,1)S(1)}, u32[]{:S(2)}, u32[]{:S(2)}) collective-permute-start(bf16[144,1792]{1,0:T(8,128)(2,1)S(1)} %collective-permute-done.4.next_first.next_0), channel_id=1, source_target_pairs={{1,2},{2,1},{5,6},{6,5},{9,10},{10,9},{13,14},{14,13},{17,18},{18,... | collective-permute-start | bytes 1548296 | tf_op jit(solution)/shard_map/ppermute | solution.py:315
  36.3 12.6 %collective-permute-start.7 = (bf16[144,3584]{1,0:T(8,128)(2,1)S(1)}, bf16[144,3584]{1,0:T(8,128)(2,1)S(1)}, u32[]{:S(2)}, u32[]{:S(2)}) collective-permute-start(bf16[144,3584]{1,0:T(8,128)(2,1)S(1)} %collective-permute-done.near_ref), channel_id=1, source_target_pairs={{0,1},{1,0},{2,3},{3,2},{4,5},{5,4},{6,7},{7,6},{8,9},{9,8},{10,11... | collective-permute-start | bytes 3096584 | tf_op jit(solution)/shard_map/ppermute | solution.py:315
  48.9 0.8 iota_compare_fusion.1
  49.8 0.0 collective-permute-done.2.next_second.next_1
  49.8 1.9 %collective-permute-start.3 = (bf16[144,1792]{1,0:T(8,128)(2,1)S(1)}, bf16[144,1792]{1,0:T(8,128)(2,1)S(1)}, u32[]{:S(2)}, u32[]{:S(2)}) collective-permute-start(bf16[144,1792]{1,0:T(8,128)(2,1)S(1)} %collective-permute-done.2.next_second.next_1), channel_id=1, source_target_pairs={{1,2},{2,1},{5,6},{6,5},{9,10},{10,9},{13,14},{14,13},{17,18},{18,... | collective-permute-start | bytes 1548296 | tf_op jit(solution)/shard_map/ppermute | solution.py:315
  51.7 0.1 fusion.partner_ref
  51.8 0.0 copy-start
  51.8 1.2 %copy-done = bf16[144,3584]{1,0:T(8,128)(2,1)S(1)} copy-done((bf16[144,3584]{1,0:T(8,128)(2,1)S(1)}, bf16[144,3584]{1,0:T(8,128)(2,1)}, u32[]{:S(2)}) %copy-start) | copy-done | bytes 1032216
  53.0 1.0 %early_scores.1 = (f32[144,144]{1,0:T(8,128)S(1)}, f32[144,144]{1,0:T(8,128)S(1)}, f32[144,144]{1,0:T(8,128)S(1)}, f32[144,144]{1,0:T(8,128)S(1)}, f32[144,144]{...) custom-call(f32[144,144]{1,0:T(8,128)S(1)} %fusion.partner_ref, bf16[144,3584]{1,0:T(8,128)(2,1)S(1)} %copy-done, ...), custom_call_target="tpu_custom_call" | custom-call | flops 451878912 | bytes 3138048 | tf_op jit(solution)/shard_map/early_scores/pallas_call | solution.py:81
  54.0 0.0 collective-permute-done.5.far_ref.far_0
  54.0 1.9 %collective-permute-start.9 = (bf16[144,1792]{1,0:T(8,128)(2,1)S(1)}, bf16[144,1792]{1,0:T(8,128)(2,1)S(1)}, u32[]{:S(2)}, u32[]{:S(2)}) collective-permute-start(bf16[144,1792]{1,0:T(8,128)(2,1)S(1)} %collective-permute-done.2.next_second.next_1), channel_id=1, source_target_pairs={{0,1},{1,0},{2,3},{3,2},{4,5},{5,4},{6,7},{7,6},{8,9},{9,8},{10,11... | collective-permute-start | bytes 1548296 | tf_op jit(solution)/shard_map/ppermute | solution.py:315
  56.0 0.0 collective-permute-done.6.key_ref.mate_ref
  56.0 2.4 %collective-permute-start.8 = (bf16[144,1792]{1,0:T(8,128)(2,1)S(1)}, bf16[144,1792]{1,0:T(8,128)(2,1)S(1)}, u32[]{:S(2)}, u32[]{:S(2)}) collective-permute-start(bf16[144,1792]{1,0:T(8,128)(2,1)S(1)} %get-tuple-element.32), channel_id=1, source_target_pairs={{0,1},{1,0},{2,3},{3,2},{4,5},{5,4},{6,7},{7,6},{8,9},{9,8},{10,11... | collective-permute-start | bytes 1548296 | tf_op jit(solution)/shard_map/ppermute | solution.py:315
  58.4 0.4 side_scores.1
  58.8 0.3 far_scores.3.sum_ref
  59.1 1.1 %collective-permute-done.3.far_ref.far_1 = bf16[144,1792]{1,0:T(8,128)(2,1)S(1)} collective-permute-done((bf16[144,1792]{1,0:T(8,128)(2,1)S(1)}, bf16[144,1792]{1,0:T(8,128)(2,1)S(1)}, u32[]{:S(2)}, u32[]{:S(2)}) %collective-permute-start.3) | collective-permute-done | bytes 516128 | tf_op jit(solution)/shard_map/ppermute | solution.py:315
  60.2 0.3 far_scores.4.sum_ref
  60.5 0.0 collective-permute-done.1.far_ref.far_first
  60.5 0.4 far_scores.5.far_score_ref.far_score
  61.0 0.0 copy-start.1
  61.0 0.0 collective-permute-done.9.mate_second.pair_1
  61.0 0.0 collective-permute-done.8.mate_first.pair_0
  61.0 0.0 collective-permute-done.7.near_mate_ref.pair_ref
  61.0 1.3 %totals.1 = (f32[144,144]{1,0:T(8,128)S(1)}, f32[144,144]{1,0:T(8,128)S(1)}, f32[1,144]{1,0:T(1,128)S(1)}, f32[8,144]{1,0:T(8,128)S(1)}, f32[1,72]{1,0:T(1,128)}) custom-call(f32[144,144]{1,0:T(8,128)S(1)} %far_scores.5.far_score_ref.far_score, f32[144,144]{1,0:T(8,128)S(1)} %get-tuple-element.29.mass_ref, ...), custom_call_target="tpu_custom_call" | custom-call | flops 475766784 | bytes 3303936 | tf_op jit(solution)/shard_map/totals/pallas_call | solution.py:81
  62.3 1.9 %collective-permute-start.10 = (f32[1,144]{1,0:T(1,128)S(1)}, f32[1,144]{1,0:T(1,128)S(1)}, u32[]{:S(2)}, u32[]{:S(2)}) collective-permute-start(f32[1,144]{1,0:T(1,128)S(1)} %get-tuple-element.34.own_row), channel_id=1, source_target_pairs={{0,1},{1,0},{2,3},{3,2},{4,5},{5,4},{6,7},{7,6},{8,9},{9,8},{10,11... | collective-permute-start | bytes 1736 | tf_op jit(solution)/shard_map/ppermute | solution.py:315
  64.3 1.9 %collective-permute-start.11 = (f32[8,144]{1,0:T(8,128)S(1)}, f32[8,144]{1,0:T(8,128)S(1)}, u32[]{:S(2)}, u32[]{:S(2)}) collective-permute-start(f32[8,144]{1,0:T(8,128)S(1)} %get-tuple-element.35), channel_id=1, source_target_pairs={{0,509},{1,4},{2,511},{3,6},{4,1},{5,8},{6,3},{7,10},{8,5},{9,12},... | collective-permute-start | bytes 13832 | tf_op jit(solution)/shard_map/ppermute | solution.py:315
  66.2 0.0 collective-permute-done.10.mate_row
  66.2 9.5 %collective-permute-start.12 = (f32[2,144]{1,0:T(2,128)S(1)}, f32[2,144]{1,0:T(2,128)S(1)}, u32[]{:S(2)}, u32[]{:S(2)}) collective-permute-start(f32[2,144]{1,0:T(2,128)S(1)} %pad_maximum_fusion), channel_id=1, source_target_pairs={{0,510},{1,511},{2,4},{3,5},{4,2},{5,3},{6,8},{7,9},{8,6},{9,7},{1... | collective-permute-start | bytes 3464 | tf_op jit(solution)/shard_map/ppermute | solution.py:315
  75.7 1.9 %collective-permute-start.13 = (f32[2,144]{1,0:T(2,128)S(1)}, f32[2,144]{1,0:T(2,128)S(1)}, u32[]{:S(2)}, u32[]{:S(2)}) collective-permute-start(f32[2,144]{1,0:T(2,128)S(1)} %pad_maximum_fusion), channel_id=1, source_target_pairs={{0,2},{1,3},{2,0},{3,1},{4,6},{5,7},{6,4},{7,5},{8,10},{9,11},{10,... | collective-permute-start | bytes 3464 | tf_op jit(solution)/shard_map/ppermute | solution.py:315
  77.6 0.0 collective-permute-done.12.next_rows
  77.6 0.0 collective-permute-done.11.far_row
  77.7 0.0 copy-done.1
  77.7 0.0 copy-start.2
  77.7 0.0 copy-start.3
  77.7 0.0 copy-start.4
  77.7 1.4 %part_gradients.1 = (f32[144,3584]{1,0:T(8,128)S(1)}, f32[144,144]{1,0:T(8,128)S(1)}) custom-call(f32[144,144]{1,0:T(8,128)S(1)} %fusion.partner_ref, f32[1,144]{1,0:T(1,128)S(1)} %get-tuple-element.34.own_row, f32[1,144]{1,0:T(1,128)S(1)} %collective-permute-done.10.mate_row, f32[8,144]{1,0:T(8,128)S(1)} %collective-permute-done.11.far_row, ...), custom_call_target="tpu_custom_call" | custom-call | flops 743178240 | bytes 8257536 | tf_op jit(solution)/shard_map/part_gradients/pallas_call | solution.py:228
  79.1 1.2 %collective-permute-done.13.near_rows = f32[2,144]{1,0:T(2,128)S(1)} collective-permute-done((f32[2,144]{1,0:T(2,128)S(1)}, f32[2,144]{1,0:T(2,128)S(1)}, u32[]{:S(2)}, u32[]{:S(2)}) %collective-permute-start.13) | collective-permute-done | bytes 1184 | tf_op jit(solution)/shard_map/ppermute | solution.py:315
  80.3 0.0 copy-done.2
  80.3 0.0 copy-done.4
  80.3 2.0 %gradients.1 = (f32[72,3584]{1,0:T(8,128)}, f32[72,3584]{1,0:T(8,128)}) custom-call(f32[144,3584]{1,0:T(8,128)S(1)} %get-tuple-element.38.sum_ref, f32[144,144]{1,0:T(8,128)S(1)} %get-tuple-element.39.along_ref, f32[144,1]{1,0:T(8,128)S(1)} %copy-done.4, f32[1,144]{1,0:T(1,128)S(1)} %get-tuple-element.34.own_row, ...), custom_call_target="tpu_custom_call" | custom-call | flops 297271296 | bytes 6193152 | tf_op jit(solution)/shard_map/gradients/pallas_call | solution.py:284
  (2 shorter events, 0.0 us)
Async XLA Ops:
  3.5 23.9 %collective-permute-start = (bf16[144,3584]{1,0:T(8,128)(2,1)}, bf16[144,3584]{1,0:T(8,128)(2,1)S(1)}, u32[]{:S(2)}, u32[]{:S(2)}) collective-permute-start(bf16[144,3584]{1,0:T(8,128)(2,1)} %get-tuple-element.24.own_ref), channel_id=1, source_target_pairs={{0,2},{1,3},{2,0},{3,1},{4,6},{5,7},{6,4},{7,5},{8,10},{9,11},{10,... | collective-permute-start | bytes 3096584 | tf_op jit(solution)/shard_map/ppermute | solution.py:315
  8.4 25.3 %collective-permute-start.4 = (bf16[144,1792]{1,0:T(8,128)(2,1)}, bf16[144,1792]{1,0:T(8,128)(2,1)S(1)}, u32[]{:S(2)}, u32[]{:S(2)}) collective-permute-start(bf16[144,1792]{1,0:T(8,128)(2,1)} %get-tuple-element.26), channel_id=1, source_target_pairs={{0,510},{1,511},{2,4},{3,5},{4,2},{5,3},{6,8},{7,9},{8,6},{9,7},{1... | collective-permute-start | bytes 1548296 | tf_op jit(solution)/shard_map/ppermute | solution.py:315
  22.3 33.6 %collective-permute-start.6 = (bf16[144,3584]{1,0:T(8,128)(2,1)}, bf16[144,3584]{1,0:T(8,128)(2,1)S(1)}, u32[]{:S(2)}, u32[]{:S(2)}) collective-permute-start(bf16[144,3584]{1,0:T(8,128)(2,1)} %get-tuple-element.24.own_ref), channel_id=1, source_target_pairs={{0,1},{1,0},{2,3},{3,2},{4,5},{5,4},{6,7},{7,6},{8,9},{9,8},{10,11... | collective-permute-start | bytes 3096584 | tf_op jit(solution)/shard_map/ppermute | solution.py:315
  25.5 24.3 %collective-permute-start.2 = (bf16[144,1792]{1,0:T(8,128)(2,1)}, bf16[144,1792]{1,0:T(8,128)(2,1)S(1)}, u32[]{:S(2)}, u32[]{:S(2)}) collective-permute-start(bf16[144,1792]{1,0:T(8,128)(2,1)} %get-tuple-element.25), channel_id=1, source_target_pairs={{0,510},{1,511},{2,4},{3,5},{4,2},{5,3},{6,8},{7,9},{8,6},{9,7},{1... | collective-permute-start | bytes 1548296 | tf_op jit(solution)/shard_map/ppermute | solution.py:315
  27.4 33.1 %collective-permute-start.1 = (bf16[144,3584]{1,0:T(8,128)(2,1)S(1)}, bf16[144,3584]{1,0:T(8,128)(2,1)S(1)}, u32[]{:S(2)}, u32[]{:S(2)}) collective-permute-start(bf16[144,3584]{1,0:T(8,128)(2,1)S(1)} %collective-permute-done.near_ref), channel_id=1, source_target_pairs={{0,511},{3,4},{4,3},{7,8},{8,7},{11,12},{12,11},{15,16},{16,15},{1... | collective-permute-start | bytes 3096584 | tf_op jit(solution)/shard_map/ppermute | solution.py:315
  33.7 20.3 %collective-permute-start.5 = (bf16[144,1792]{1,0:T(8,128)(2,1)S(1)}, bf16[144,1792]{1,0:T(8,128)(2,1)S(1)}, u32[]{:S(2)}, u32[]{:S(2)}) collective-permute-start(bf16[144,1792]{1,0:T(8,128)(2,1)S(1)} %collective-permute-done.4.next_first.next_0), channel_id=1, source_target_pairs={{1,2},{2,1},{5,6},{6,5},{9,10},{10,9},{13,14},{14,13},{17,18},{18,... | collective-permute-start | bytes 1548296 | tf_op jit(solution)/shard_map/ppermute | solution.py:315
  36.3 24.7 %collective-permute-start.7 = (bf16[144,3584]{1,0:T(8,128)(2,1)S(1)}, bf16[144,3584]{1,0:T(8,128)(2,1)S(1)}, u32[]{:S(2)}, u32[]{:S(2)}) collective-permute-start(bf16[144,3584]{1,0:T(8,128)(2,1)S(1)} %collective-permute-done.near_ref), channel_id=1, source_target_pairs={{0,1},{1,0},{2,3},{3,2},{4,5},{5,4},{6,7},{7,6},{8,9},{9,8},{10,11... | collective-permute-start | bytes 3096584 | tf_op jit(solution)/shard_map/ppermute | solution.py:315
  49.8 10.4 %collective-permute-start.3 = (bf16[144,1792]{1,0:T(8,128)(2,1)S(1)}, bf16[144,1792]{1,0:T(8,128)(2,1)S(1)}, u32[]{:S(2)}, u32[]{:S(2)}) collective-permute-start(bf16[144,1792]{1,0:T(8,128)(2,1)S(1)} %collective-permute-done.2.next_second.next_1), channel_id=1, source_target_pairs={{1,2},{2,1},{5,6},{6,5},{9,10},{10,9},{13,14},{14,13},{17,18},{18,... | collective-permute-start | bytes 1548296 | tf_op jit(solution)/shard_map/ppermute | solution.py:315
  51.8 1.2 %copy-start = (bf16[144,3584]{1,0:T(8,128)(2,1)S(1)}, bf16[144,3584]{1,0:T(8,128)(2,1)}, u32[]{:S(2)}) copy-start(bf16[144,3584]{1,0:T(8,128)(2,1)} %get-tuple-element.24.own_ref) | copy-start | bytes 3096580
  54.0 6.9 %collective-permute-start.9 = (bf16[144,1792]{1,0:T(8,128)(2,1)S(1)}, bf16[144,1792]{1,0:T(8,128)(2,1)S(1)}, u32[]{:S(2)}, u32[]{:S(2)}) collective-permute-start(bf16[144,1792]{1,0:T(8,128)(2,1)S(1)} %collective-permute-done.2.next_second.next_1), channel_id=1, source_target_pairs={{0,1},{1,0},{2,3},{3,2},{4,5},{5,4},{6,7},{7,6},{8,9},{9,8},{10,11... | collective-permute-start | bytes 1548296 | tf_op jit(solution)/shard_map/ppermute | solution.py:315
  56.0 5.0 %collective-permute-start.8 = (bf16[144,1792]{1,0:T(8,128)(2,1)S(1)}, bf16[144,1792]{1,0:T(8,128)(2,1)S(1)}, u32[]{:S(2)}, u32[]{:S(2)}) collective-permute-start(bf16[144,1792]{1,0:T(8,128)(2,1)S(1)} %get-tuple-element.32), channel_id=1, source_target_pairs={{0,1},{1,0},{2,3},{3,2},{4,5},{5,4},{6,7},{7,6},{8,9},{9,8},{10,11... | collective-permute-start | bytes 1548296 | tf_op jit(solution)/shard_map/ppermute | solution.py:315
  61.0 16.7 %copy-start.1 = (bf16[144,3584]{1,0:T(8,128)(2,1)S(1)}, bf16[144,3584]{1,0:T(8,128)(2,1)}, u32[]{:S(2)}) copy-start(bf16[144,3584]{1,0:T(8,128)(2,1)} %get-tuple-element.24.own_ref) | copy-start | bytes 3096580
  62.3 3.8 %collective-permute-start.10 = (f32[1,144]{1,0:T(1,128)S(1)}, f32[1,144]{1,0:T(1,128)S(1)}, u32[]{:S(2)}, u32[]{:S(2)}) collective-permute-start(f32[1,144]{1,0:T(1,128)S(1)} %get-tuple-element.34.own_row), channel_id=1, source_target_pairs={{0,1},{1,0},{2,3},{3,2},{4,5},{5,4},{6,7},{7,6},{8,9},{9,8},{10,11... | collective-permute-start | bytes 1736 | tf_op jit(solution)/shard_map/ppermute | solution.py:315
  64.3 13.4 %collective-permute-start.11 = (f32[8,144]{1,0:T(8,128)S(1)}, f32[8,144]{1,0:T(8,128)S(1)}, u32[]{:S(2)}, u32[]{:S(2)}) collective-permute-start(f32[8,144]{1,0:T(8,128)S(1)} %get-tuple-element.35), channel_id=1, source_target_pairs={{0,509},{1,4},{2,511},{3,6},{4,1},{5,8},{6,3},{7,10},{8,5},{9,12},... | collective-permute-start | bytes 13832 | tf_op jit(solution)/shard_map/ppermute | solution.py:315
  66.2 11.4 %collective-permute-start.12 = (f32[2,144]{1,0:T(2,128)S(1)}, f32[2,144]{1,0:T(2,128)S(1)}, u32[]{:S(2)}, u32[]{:S(2)}) collective-permute-start(f32[2,144]{1,0:T(2,128)S(1)} %pad_maximum_fusion), channel_id=1, source_target_pairs={{0,510},{1,511},{2,4},{3,5},{4,2},{5,3},{6,8},{7,9},{8,6},{9,7},{1... | collective-permute-start | bytes 3464 | tf_op jit(solution)/shard_map/ppermute | solution.py:315
  75.7 4.6 %collective-permute-start.13 = (f32[2,144]{1,0:T(2,128)S(1)}, f32[2,144]{1,0:T(2,128)S(1)}, u32[]{:S(2)}, u32[]{:S(2)}) collective-permute-start(f32[2,144]{1,0:T(2,128)S(1)} %pad_maximum_fusion), channel_id=1, source_target_pairs={{0,2},{1,3},{2,0},{3,1},{4,6},{5,7},{6,4},{7,5},{8,10},{9,11},{10,... | collective-permute-start | bytes 3464 | tf_op jit(solution)/shard_map/ppermute | solution.py:315
  77.7 2.7 %copy-start.2 = (bf16[72,3584]{1,0:T(8,128)(2,1)S(1)}, bf16[72,3584]{1,0:T(8,128)(2,1)}, u32[]{:S(2)}) copy-start(bf16[72,3584]{1,0:T(8,128)(2,1)} %query_ref.1) | copy-start | bytes 1548292
  77.7 2.7 %copy-start.3 = (bf16[72,3584]{1,0:T(8,128)(2,1)S(1)}, bf16[72,3584]{1,0:T(8,128)(2,1)}, u32[]{:S(2)}) copy-start(bf16[72,3584]{1,0:T(8,128)(2,1)} %passage_ref.1) | copy-start | bytes 1548292
  77.7 2.6 %copy-start.4 = (f32[144,1]{1,0:T(8,128)S(1)}, f32[144,1]{1,0:T(8,128)}, u32[]{:S(2)}) copy-start(f32[144,1]{1,0:T(8,128)} %get-tuple-element.40.scale_ref) | copy-start | bytes 1732

commit v5 on v4

--- a/solution.py
+++ b/solution.py
@@ -10,7 +10,6 @@
 INV_TEMP = 20.0
 EPS = 1e-06
 TILE = 896
-SPREAD = 8
 VMEM = pl.BlockSpec(memory_space=pltpu.VMEM)
 HBM = pl.BlockSpec(memory_space=pl.ANY)
 
@@ -147,7 +146,7 @@
 
 def total_kernel(
     far_score_ref, mass_ref, score_ref, partner_ref, own_ref, own_mate_score, near_mate_ref, mate_first, mate_second,
-    near_mate_out, next_mate_out, recip_ref, spread_ref, loss_ref,
+    near_mate_out, next_mate_out, recip_ref, loss_ref,
 ):
     partner = partner_ref[...]
     own = own_ref[...]
@@ -163,7 +162,6 @@
     eye = eye_of(partner.shape[0])
     norm_row = jnp.sum((eye + partner) * total_col, axis=0, keepdims=True)
     recip_ref[...] = 1.0 / norm_row
-    spread_ref[...] = jnp.broadcast_to(1.0 / norm_row, spread_ref.shape)
     positive = jnp.sum(partner * score_ref[...], axis=0, keepdims=True)
     losses = jnp.log(norm_row) + INV_TEMP - INV_TEMP * positive
     loss_ref[...] = losses[:, : loss_ref.shape[1]]
@@ -180,9 +178,8 @@
 
 
 def part_kernel(
-    partner_ref, own_row, mate_row, far_row, next_rows, own_score, mate_score, far_score, next_score,
-    next_mate_score, own_ref, mate_ref, far_first, far_0, far_1, next_0, next_1, pair_0, pair_1,
-    sum_ref, along_ref,
+    partner_ref, own_row, mate_row, next_rows, own_score, mate_score, next_score, next_mate_score,
+    own_ref, mate_ref, next_0, next_1, pair_0, pair_1, sum_ref, along_ref,
 ):
     partner = partner_ref[...]
     count = partner.shape[0]
@@ -196,7 +193,6 @@
     along = low.astype(jnp.float32) * score
     for score_ref, row in (
         (mate_score, mate_row[...]),
-        (far_score, far_row[0:1, :]),
         (next_score, next_rows[0:1, :]),
         (next_mate_score, next_rows[1:2, :]),
     ):
@@ -209,11 +205,10 @@
     for start in range(0, own_ref.shape[1], TILE):
         whole = slice(start, start + TILE)
         columns = slice(start % half, start % half + TILE)
-        far_ref, next_ref, pair_ref = ((far_0, next_0, pair_0), (far_1, next_1, pair_1))[start // half]
+        next_ref, pair_ref = ((next_0, pair_0), (next_1, pair_1))[start // half]
         keys = [
             own_ref[:, whole],
             mate_ref[:, whole],
-            far_first[:, whole] + far_ref[:, columns],
             next_ref[:, columns],
             pair_ref[:, columns],
         ]
@@ -235,31 +230,36 @@
         ),
         compiler_params=pltpu.CompilerParams(vmem_limit_bytes=24 * 2**20),
         cost_estimate=pl.CostEstimate(
-            flops=10 * count * count * width,
-            bytes_accessed=16 * count * width,
-            transcendentals=5 * count * count,
+            flops=8 * count * count * width,
+            bytes_accessed=12 * count * width,
+            transcendentals=4 * count * count,
         ),
         name="part_gradients",
     )(*operands)
 
 
 def gradient_kernel(
-    sum_ref, along_ref, scale_ref, own_row, near_rows, near_score, pair_score, near_ref, pair_ref,
-    query_ref, passage_ref, query_out, passage_out, query_hold, passage_hold, sems,
+    sum_ref, along_ref, scale_ref, own_row, near_rows, far_row, near_score, pair_score, far_score,
+    near_ref, pair_ref, far_first, far_0, far_1, query_ref, passage_ref,
+    query_out, passage_out, query_hold, passage_hold, sems,
 ):
     count = along_ref.shape[0]
     rows = count // 2
     recip_col = column_of(own_row[...])
     near_low, near_share = weigh(near_score[...], recip_col, near_rows[0:1, :])
     pair_low, pair_share = weigh(pair_score[...], recip_col, near_rows[1:2, :])
-    along = along_ref[...] + near_share + pair_share
+    far_low, far_share = weigh(far_score[...], recip_col, far_row[...])
+    along = along_ref[...] + near_share + pair_share + far_share
     along = INV_TEMP * jnp.sum(along, axis=1, keepdims=True)
-    weights = jnp.concatenate([near_low, pair_low], axis=1)
+    weights = jnp.concatenate([near_low, pair_low, far_low], axis=1)
+    half = far_0.shape[1]
     scale = scale_ref[...]
     copies = []
     for start in range(0, near_ref.shape[1], TILE):
         whole = slice(start, start + TILE)
-        keys = jnp.concatenate([near_ref[:, whole], pair_ref[:, whole]], axis=0)
+        far_ref = (far_0, far_1)[start // half]
+        far = far_first[:, whole] + far_ref[:, start % half : start % half + TILE]
+        keys = jnp.concatenate([near_ref[:, whole], pair_ref[:, whole], far], axis=0)
         gradient = jnp.dot(weights, keys, preferred_element_type=jnp.float32) + sum_ref[:, whole]
         for part, raw_ref, hold, out in (
             (0, query_ref, query_hold, query_out),
@@ -293,9 +293,9 @@
         ],
         compiler_params=pltpu.CompilerParams(vmem_limit_bytes=24 * 2**20),
         cost_estimate=pl.CostEstimate(
-            flops=4 * count * count * width,
-            bytes_accessed=12 * count * width,
-            transcendentals=2 * count * count,
+            flops=6 * count * count * width,
+            bytes_accessed=16 * count * width,
+            transcendentals=3 * count * count,
         ),
         name="gradients",
     )(*operands)
@@ -359,11 +359,11 @@
     far_score = far_scores(own, far_second[0], far_score, 0)
     far_score = far_scores(own, far_second[1], far_score, 1)
     far_score = far_scores(own, far_first, far_score, 0)
-    near_mate_score, next_mate_score, recip, spread, losses = score_call(
+    near_mate_score, next_mate_score, recip, losses = score_call(
         total_kernel,
         "totals",
         count,
-        [square, square, (1, count), (SPREAD, count), (1, rows)],
+        [square, square, (1, count), (1, rows)],
         [far_score, mass, scores[0], partner, own, mate_score, near_mate, *next_mate],
     )
 
@@ -371,22 +371,22 @@
     chip_rows = jnp.concatenate([recip, mate_row], axis=0)
     near_rows = swapped(chip_rows, near_chip)
     next_rows = swapped(chip_rows, next_chip)
-    far_row = swapped(spread, chip_beyond)
+    far_row = swapped(recip, chip_beyond)
 
     near_score, next_score = scores[1:]
     part_sum, along = part_gradients(
         partner,
-        [recip, mate_row, far_row, next_rows],
-        [scores[0], mate_score, far_score, next_score, next_mate_score],
-        [own, mate, far_first, *far_second, *next_halves, *next_mate],
+        [recip, mate_row, next_rows],
+        [scores[0], mate_score, next_score, next_mate_score],
+        [own, mate, *next_halves, *next_mate],
     )
     query_grad, passage_grad = gradients(
         part_sum,
         along,
         scale,
-        [recip, near_rows],
-        [near_score, near_mate_score],
-        [near, near_mate],
+        [recip, near_rows, far_row],
+        [near_score, near_mate_score, far_score],
+        [near, near_mate, far_first, *far_second],
         query_raw,
         passage_raw,
     )

time: 82.8 us -> 83.2 us (level); the launches traced: 82.3 us -> 81.6 us
  starting transfers between devices: 61.3 us -> 55.6 us
  waiting for transfers between devices: 7.84 us -> 12.9 us
    ppermute x14, starting transfers between devices: 61.3 us -> 55.6 us  [swapped(): return lax.ppermute(value, 'dp', pairs)]
    ppermute x14, waiting for transfers between devices: 7.84 us -> 12.9 us  [swapped(): return lax.ppermute(value, 'dp', pairs)]
  transfers between devices with their start and end apart: 14 -> 14, of which waited for: 3 -> 5; matrix products, arithmetic and copies ran while one was open for 1% -> 1% of each run, Pallas kernels for 5% -> 5%
where the time goes in v5:
time: 83.2 us; the launch traced here: 81.6 us
  starting transfers between devices  55.6 us (67%)
  waiting for transfers between devices  12.9 us (16%)
  Pallas kernels  10.1 us (12%)
  local copies, waits for them, and re-layouts  1.24 us (1%)
  between operations  0.93 us (1%)
  other arithmetic  0.91 us (1%)
    ppermute x14, starting transfers between devices, swapped(): return lax.ppermute(value, 'dp', pairs)  55.6 us
    ppermute x14, waiting for transfers between devices, swapped(): return lax.ppermute(value, 'dp', pairs)  12.9 us
    pallas_call x6, Pallas kernels, score_call(): pl.pallas_call(body, in_specs=[VMEM] * len(operands), out_specs=[VMEM] *...  3.82 us
    pallas_call x1, Pallas kernels, unit_rows(): pl.pallas_call(unit_kernel, in_specs=[HBM, HBM], out_specs=(VMEM, VMEM, V...  2.91 us
    pallas_call x1, Pallas kernels, gradients(): pl.pallas_call(gradient_kernel, in_specs=[VMEM] * len(operands), out_spec...  2.11 us
  transfers between devices with their start and end apart: 14, of which 5 were waited for; matrix products, arithmetic and copies ran while one was open for 1% of the time, Pallas kernels for 5%

profile of v5, /device:TPU:1, one launch (start us, length us, event | category | flops | bytes accessed | tf_op | source)
XLA Modules:
  0.0 81.6 jit_solution(16782059505936528629)
XLA Ops:
  0.6 2.9 %unit_rows.1 = (bf16[144,3584]{1,0:T(8,128)(2,1)}, bf16[144,1792]{1,0:T(8,128)(2,1)}, bf16[144,1792]{1,0:T(8,128)(2,1)}, f32[144,1]{1,0:T(8,128)}) custom-call(bf16[72,3584]{1,0:T(8,128)(2,1)} %query_ref.1, bf16[72,3584]{1,0:T(8,128)(2,1)} %passage_ref.1), custom_call_target="tpu_custom_call" | custom-call | flops 1548288 | bytes 2064384 | tf_op jit(solution)/shard_map/unit_rows/pallas_call | solution.py:60
  3.5 4.8 %collective-permute-start = (bf16[144,3584]{1,0:T(8,128)(2,1)}, bf16[144,3584]{1,0:T(8,128)(2,1)S(1)}, u32[]{:S(2)}, u32[]{:S(2)}) collective-permute-start(bf16[144,3584]{1,0:T(8,128)(2,1)} %get-tuple-element.23.own_ref), channel_id=1, source_target_pairs={{0,2},{1,3},{2,0},{3,1},{4,6},{5,7},{6,4},{7,5},{8,10},{9,11},{10,... | collective-permute-start | bytes 3096584 | tf_op jit(solution)/shard_map/ppermute | solution.py:315
  8.4 5.9 %collective-permute-start.6 = (bf16[144,3584]{1,0:T(8,128)(2,1)}, bf16[144,3584]{1,0:T(8,128)(2,1)S(1)}, u32[]{:S(2)}, u32[]{:S(2)}) collective-permute-start(bf16[144,3584]{1,0:T(8,128)(2,1)} %get-tuple-element.23.own_ref), channel_id=1, source_target_pairs={{0,1},{1,0},{2,3},{3,2},{4,5},{5,4},{6,7},{7,6},{8,9},{9,8},{10,11... | collective-permute-start | bytes 3096584 | tf_op jit(solution)/shard_map/ppermute | solution.py:315
  14.3 10.9 %collective-permute-start.4 = (bf16[144,1792]{1,0:T(8,128)(2,1)}, bf16[144,1792]{1,0:T(8,128)(2,1)S(1)}, u32[]{:S(2)}, u32[]{:S(2)}) collective-permute-start(bf16[144,1792]{1,0:T(8,128)(2,1)} %get-tuple-element.25), channel_id=1, source_target_pairs={{0,510},{1,511},{2,4},{3,5},{4,2},{5,3},{6,8},{7,9},{8,6},{9,7},{1... | collective-permute-start | bytes 1548296 | tf_op jit(solution)/shard_map/ppermute | solution.py:315
  25.2 1.9 %collective-permute-start.2 = (bf16[144,1792]{1,0:T(8,128)(2,1)}, bf16[144,1792]{1,0:T(8,128)(2,1)S(1)}, u32[]{:S(2)}, u32[]{:S(2)}) collective-permute-start(bf16[144,1792]{1,0:T(8,128)(2,1)} %get-tuple-element.24), channel_id=1, source_target_pairs={{0,510},{1,511},{2,4},{3,5},{4,2},{5,3},{6,8},{7,9},{8,6},{9,7},{1... | collective-permute-start | bytes 1548296 | tf_op jit(solution)/shard_map/ppermute | solution.py:315
  27.1 0.0 collective-permute-done.near_ref
  27.2 0.7 collective-permute-start.1
  27.9 9.6 %collective-permute-done.4.next_first.next_0 = bf16[144,1792]{1,0:T(8,128)(2,1)S(1)} collective-permute-done((bf16[144,1792]{1,0:T(8,128)(2,1)}, bf16[144,1792]{1,0:T(8,128)(2,1)S(1)}, u32[]{:S(2)}, u32[]{:S(2)}) %collective-permute-start.4) | collective-permute-done | bytes 516128 | tf_op jit(solution)/shard_map/ppermute | solution.py:315
  37.5 1.9 %collective-permute-start.5 = (bf16[144,1792]{1,0:T(8,128)(2,1)S(1)}, bf16[144,1792]{1,0:T(8,128)(2,1)S(1)}, u32[]{:S(2)}, u32[]{:S(2)}) collective-permute-start(bf16[144,1792]{1,0:T(8,128)(2,1)S(1)} %collective-permute-done.4.next_first.next_0), channel_id=1, source_target_pairs={{1,2},{2,1},{5,6},{6,5},{9,10},{10,9},{13,14},{14,13},{17,18},{18,... | collective-permute-start | bytes 1548296 | tf_op jit(solution)/shard_map/ppermute | solution.py:315
  39.4 9.5 %collective-permute-start.7 = (bf16[144,3584]{1,0:T(8,128)(2,1)S(1)}, bf16[144,3584]{1,0:T(8,128)(2,1)S(1)}, u32[]{:S(2)}, u32[]{:S(2)}) collective-permute-start(bf16[144,3584]{1,0:T(8,128)(2,1)S(1)} %collective-permute-done.near_ref), channel_id=1, source_target_pairs={{0,1},{1,0},{2,3},{3,2},{4,5},{5,4},{6,7},{7,6},{8,9},{9,8},{10,11... | collective-permute-start | bytes 3096584 | tf_op jit(solution)/shard_map/ppermute | solution.py:315
  48.9 0.8 iota_compare_fusion.1
  49.8 0.0 collective-permute-done.2.next_second.next_1
  49.8 1.9 %collective-permute-start.3 = (bf16[144,1792]{1,0:T(8,128)(2,1)S(1)}, bf16[144,1792]{1,0:T(8,128)(2,1)S(1)}, u32[]{:S(2)}, u32[]{:S(2)}) collective-permute-start(bf16[144,1792]{1,0:T(8,128)(2,1)S(1)} %collective-permute-done.2.next_second.next_1), channel_id=1, source_target_pairs={{1,2},{2,1},{5,6},{6,5},{9,10},{10,9},{13,14},{14,13},{17,18},{18,... | collective-permute-start | bytes 1548296 | tf_op jit(solution)/shard_map/ppermute | solution.py:315
  51.7 0.1 fusion.partner_ref
  51.8 0.0 copy-start
  51.8 1.2 %copy-done = bf16[144,3584]{1,0:T(8,128)(2,1)S(1)} copy-done((bf16[144,3584]{1,0:T(8,128)(2,1)S(1)}, bf16[144,3584]{1,0:T(8,128)(2,1)}, u32[]{:S(2)}) %copy-start) | copy-done | bytes 1032216
  53.0 1.0 %early_scores.1 = (f32[144,144]{1,0:T(8,128)S(1)}, f32[144,144]{1,0:T(8,128)S(1)}, f32[144,144]{1,0:T(8,128)S(1)}, f32[144,144]{1,0:T(8,128)S(1)}, f32[144,144]{...) custom-call(f32[144,144]{1,0:T(8,128)S(1)} %fusion.partner_ref, bf16[144,3584]{1,0:T(8,128)(2,1)S(1)} %copy-done, ...), custom_call_target="tpu_custom_call" | custom-call | flops 451878912 | bytes 3138048 | tf_op jit(solution)/shard_map/early_scores/pallas_call | solution.py:80
  54.0 0.0 collective-permute-done.6.key_ref.mate_ref
  54.0 1.9 %collective-permute-start.9 = (bf16[144,1792]{1,0:T(8,128)(2,1)S(1)}, bf16[144,1792]{1,0:T(8,128)(2,1)S(1)}, u32[]{:S(2)}, u32[]{:S(2)}) collective-permute-start(bf16[144,1792]{1,0:T(8,128)(2,1)S(1)} %collective-permute-done.2.next_second.next_1), channel_id=1, source_target_pairs={{0,1},{1,0},{2,3},{3,2},{4,5},{5,4},{6,7},{7,6},{8,9},{9,8},{10,11... | collective-permute-start | bytes 1548296 | tf_op jit(solution)/shard_map/ppermute | solution.py:315
  56.0 0.0 collective-permute-done.5.far_ref.far_0
  56.0 2.4 %collective-permute-start.8 = (bf16[144,1792]{1,0:T(8,128)(2,1)S(1)}, bf16[144,1792]{1,0:T(8,128)(2,1)S(1)}, u32[]{:S(2)}, u32[]{:S(2)}) collective-permute-start(bf16[144,1792]{1,0:T(8,128)(2,1)S(1)} %get-tuple-element.31), channel_id=1, source_target_pairs={{0,1},{1,0},{2,3},{3,2},{4,5},{5,4},{6,7},{7,6},{8,9},{9,8},{10,11... | collective-permute-start | bytes 1548296 | tf_op jit(solution)/shard_map/ppermute | solution.py:315
  58.4 0.4 side_scores.1
  58.8 0.3 far_scores.3.sum_ref
  59.1 1.0 %collective-permute-done.3.far_ref.far_1 = bf16[144,1792]{1,0:T(8,128)(2,1)S(1)} collective-permute-done((bf16[144,1792]{1,0:T(8,128)(2,1)S(1)}, bf16[144,1792]{1,0:T(8,128)(2,1)S(1)}, u32[]{:S(2)}, u32[]{:S(2)}) %collective-permute-start.3) | collective-permute-done | bytes 516128 | tf_op jit(solution)/shard_map/ppermute | solution.py:315
  60.2 0.3 far_scores.4.sum_ref
  60.5 0.0 collective-permute-done.1.far_ref.far_first
  60.5 0.4 far_scores.5.far_score_ref.far_score
  61.0 0.0 copy-start.1
  61.0 0.0 collective-permute-done.9.mate_second.pair_1
  61.0 0.0 collective-permute-done.8.mate_first.pair_0
  61.0 0.0 collective-permute-done.7.near_mate_ref.pair_ref
  61.0 1.3 %totals.1 = (f32[144,144]{1,0:T(8,128)S(1)}, f32[144,144]{1,0:T(8,128)S(1)}, f32[1,144]{1,0:T(1,128)S(1)}, f32[1,72]{1,0:T(1,128)}) custom-call(f32[144,144]{1,0:T(8,128)S(1)} %far_scores.5.far_score_ref.far_score, f32[144,144]{1,0:T(8,128)S(1)} %get-tuple-element.28.mass_ref, f32[144,144]{1,0:T(8,128)S(1)} %get-tuple-element.29.score_ref.own_score, ...), custom_call_target="tpu_custom_call" | custom-call | flops 475766784 | bytes 3303936 | tf_op jit(solution)/shard_map/totals/pallas_call | solution.py:80
  62.3 1.9 %collective-permute-start.10 = (f32[1,144]{1,0:T(1,128)S(1)}, f32[1,144]{1,0:T(1,128)S(1)}, u32[]{:S(2)}, u32[]{:S(2)}) collective-permute-start(f32[1,144]{1,0:T(1,128)S(1)} %get-tuple-element.33.own_row), channel_id=1, source_target_pairs={{0,1},{1,0},{2,3},{3,2},{4,5},{5,4},{6,7},{7,6},{8,9},{9,8},{10,11... | collective-permute-start | bytes 1736 | tf_op jit(solution)/shard_map/ppermute | solution.py:315
  64.3 1.1 %collective-permute-done.10.mate_row = f32[1,144]{1,0:T(1,128)S(1)} collective-permute-done((f32[1,144]{1,0:T(1,128)S(1)}, f32[1,144]{1,0:T(1,128)S(1)}, u32[]{:S(2)}, u32[]{:S(2)}) %collective-permute-start.10) | collective-permute-done | bytes 608 | tf_op jit(solution)/shard_map/ppermute | solution.py:315
  65.4 7.9 %collective-permute-start.11 = (f32[2,144]{1,0:T(2,128)S(1)}, f32[2,144]{1,0:T(2,128)S(1)}, u32[]{:S(2)}, u32[]{:S(2)}) collective-permute-start(f32[2,144]{1,0:T(2,128)S(1)} %pad_maximum_fusion), channel_id=1, source_target_pairs={{0,510},{1,511},{2,4},{3,5},{4,2},{5,3},{6,8},{7,9},{8,6},{9,7},{1... | collective-permute-start | bytes 3464 | tf_op jit(solution)/shard_map/ppermute | solution.py:315
  73.2 1.9 %collective-permute-start.13 = (f32[1,144]{1,0:T(1,128)S(1)}, f32[1,144]{1,0:T(1,128)S(1)}, u32[]{:S(2)}, u32[]{:S(2)}) collective-permute-start(f32[1,144]{1,0:T(1,128)S(1)} %get-tuple-element.33.own_row), channel_id=1, source_target_pairs={{0,509},{1,4},{2,511},{3,6},{4,1},{5,8},{6,3},{7,10},{8,5},{9,12},... | collective-permute-start | bytes 1736 | tf_op jit(solution)/shard_map/ppermute | solution.py:315
  75.2 1.9 %collective-permute-start.12 = (f32[2,144]{1,0:T(2,128)S(1)}, f32[2,144]{1,0:T(2,128)S(1)}, u32[]{:S(2)}, u32[]{:S(2)}) collective-permute-start(f32[2,144]{1,0:T(2,128)S(1)} %pad_maximum_fusion), channel_id=1, source_target_pairs={{0,2},{1,3},{2,0},{3,1},{4,6},{5,7},{6,4},{7,5},{8,10},{9,11},{10,... | collective-permute-start | bytes 3464 | tf_op jit(solution)/shard_map/ppermute | solution.py:315
  77.1 0.0 collective-permute-done.11.next_rows
  77.1 0.0 copy-done.1
  77.1 0.0 copy-start.2
  77.1 0.0 copy-start.3
  77.1 0.0 copy-start.4
  77.1 1.3 %part_gradients.1 = (f32[144,3584]{1,0:T(8,128)S(1)}, f32[144,144]{1,0:T(8,128)S(1)}) custom-call(f32[144,144]{1,0:T(8,128)S(1)} %fusion.partner_ref, f32[1,144]{1,0:T(1,128)S(1)} %get-tuple-element.33.own_row, f32[1,144]{1,0:T(1,128)S(1)} %collective-permute-done.10.mate_row, f32[2,144]{1,0:T(2,128)S(1)} %collective-permute-done.11.next_rows, ...), custom_call_target="tpu_custom_call" | custom-call | flops 594542592 | bytes 6193152 | tf_op jit(solution)/shard_map/part_gradients/pallas_call | solution.py:223
  78.4 0.6 collective-permute-done.13.far_row
  79.0 0.5 collective-permute-done.12.near_rows
  79.5 0.0 copy-done.2
  79.5 0.0 copy-done.3
  79.5 2.1 %gradients.1 = (f32[72,3584]{1,0:T(8,128)}, f32[72,3584]{1,0:T(8,128)}) custom-call(f32[144,3584]{1,0:T(8,128)S(1)} %get-tuple-element.36.sum_ref, f32[144,144]{1,0:T(8,128)S(1)} %get-tuple-element.37.along_ref, f32[144,1]{1,0:T(8,128)S(1)} %copy-done.4, f32[1,144]{1,0:T(1,128)S(1)} %get-tuple-element.33.own_row, ...), custom_call_target="tpu_custom_call" | custom-call | flops 445906944 | bytes 8257536 | tf_op jit(solution)/shard_map/gradients/pallas_call | solution.py:284
  (2 shorter events, 0.0 us)
Async XLA Ops:
  3.5 23.6 %collective-permute-start = (bf16[144,3584]{1,0:T(8,128)(2,1)}, bf16[144,3584]{1,0:T(8,128)(2,1)S(1)}, u32[]{:S(2)}, u32[]{:S(2)}) collective-permute-start(bf16[144,3584]{1,0:T(8,128)(2,1)} %get-tuple-element.23.own_ref), channel_id=1, source_target_pairs={{0,2},{1,3},{2,0},{3,1},{4,6},{5,7},{6,4},{7,5},{8,10},{9,11},{10,... | collective-permute-start | bytes 3096584 | tf_op jit(solution)/shard_map/ppermute | solution.py:315
  8.4 45.6 %collective-permute-start.6 = (bf16[144,3584]{1,0:T(8,128)(2,1)}, bf16[144,3584]{1,0:T(8,128)(2,1)S(1)}, u32[]{:S(2)}, u32[]{:S(2)}) collective-permute-start(bf16[144,3584]{1,0:T(8,128)(2,1)} %get-tuple-element.23.own_ref), channel_id=1, source_target_pairs={{0,1},{1,0},{2,3},{3,2},{4,5},{5,4},{6,7},{7,6},{8,9},{9,8},{10,11... | collective-permute-start | bytes 3096584 | tf_op jit(solution)/shard_map/ppermute | solution.py:315
  14.3 23.2 %collective-permute-start.4 = (bf16[144,1792]{1,0:T(8,128)(2,1)}, bf16[144,1792]{1,0:T(8,128)(2,1)S(1)}, u32[]{:S(2)}, u32[]{:S(2)}) collective-permute-start(bf16[144,1792]{1,0:T(8,128)(2,1)} %get-tuple-element.25), channel_id=1, source_target_pairs={{0,510},{1,511},{2,4},{3,5},{4,2},{5,3},{6,8},{7,9},{8,6},{9,7},{1... | collective-permute-start | bytes 1548296 | tf_op jit(solution)/shard_map/ppermute | solution.py:315
  25.2 24.6 %collective-permute-start.2 = (bf16[144,1792]{1,0:T(8,128)(2,1)}, bf16[144,1792]{1,0:T(8,128)(2,1)S(1)}, u32[]{:S(2)}, u32[]{:S(2)}) collective-permute-start(bf16[144,1792]{1,0:T(8,128)(2,1)} %get-tuple-element.24), channel_id=1, source_target_pairs={{0,510},{1,511},{2,4},{3,5},{4,2},{5,3},{6,8},{7,9},{8,6},{9,7},{1... | collective-permute-start | bytes 1548296 | tf_op jit(solution)/shard_map/ppermute | solution.py:315
  27.2 33.3 %collective-permute-start.1 = (bf16[144,3584]{1,0:T(8,128)(2,1)S(1)}, bf16[144,3584]{1,0:T(8,128)(2,1)S(1)}, u32[]{:S(2)}, u32[]{:S(2)}) collective-permute-start(bf16[144,3584]{1,0:T(8,128)(2,1)S(1)} %collective-permute-done.near_ref), channel_id=1, source_target_pairs={{0,511},{3,4},{4,3},{7,8},{8,7},{11,12},{12,11},{15,16},{16,15},{1... | collective-permute-start | bytes 3096584 | tf_op jit(solution)/shard_map/ppermute | solution.py:315
  37.5 18.4 %collective-permute-start.5 = (bf16[144,1792]{1,0:T(8,128)(2,1)S(1)}, bf16[144,1792]{1,0:T(8,128)(2,1)S(1)}, u32[]{:S(2)}, u32[]{:S(2)}) collective-permute-start(bf16[144,1792]{1,0:T(8,128)(2,1)S(1)} %collective-permute-done.4.next_first.next_0), channel_id=1, source_target_pairs={{1,2},{2,1},{5,6},{6,5},{9,10},{10,9},{13,14},{14,13},{17,18},{18,... | collective-permute-start | bytes 1548296 | tf_op jit(solution)/shard_map/ppermute | solution.py:315
  39.4 21.6 %collective-permute-start.7 = (bf16[144,3584]{1,0:T(8,128)(2,1)S(1)}, bf16[144,3584]{1,0:T(8,128)(2,1)S(1)}, u32[]{:S(2)}, u32[]{:S(2)}) collective-permute-start(bf16[144,3584]{1,0:T(8,128)(2,1)S(1)} %collective-permute-done.near_ref), channel_id=1, source_target_pairs={{0,1},{1,0},{2,3},{3,2},{4,5},{5,4},{6,7},{7,6},{8,9},{9,8},{10,11... | collective-permute-start | bytes 3096584 | tf_op jit(solution)/shard_map/ppermute | solution.py:315
  49.8 10.4 %collective-permute-start.3 = (bf16[144,1792]{1,0:T(8,128)(2,1)S(1)}, bf16[144,1792]{1,0:T(8,128)(2,1)S(1)}, u32[]{:S(2)}, u32[]{:S(2)}) collective-permute-start(bf16[144,1792]{1,0:T(8,128)(2,1)S(1)} %collective-permute-done.2.next_second.next_1), channel_id=1, source_target_pairs={{1,2},{2,1},{5,6},{6,5},{9,10},{10,9},{13,14},{14,13},{17,18},{18,... | collective-permute-start | bytes 1548296 | tf_op jit(solution)/shard_map/ppermute | solution.py:315
  51.8 1.2 %copy-start = (bf16[144,3584]{1,0:T(8,128)(2,1)S(1)}, bf16[144,3584]{1,0:T(8,128)(2,1)}, u32[]{:S(2)}) copy-start(bf16[144,3584]{1,0:T(8,128)(2,1)} %get-tuple-element.23.own_ref) | copy-start | bytes 3096580
  54.0 6.9 %collective-permute-start.9 = (bf16[144,1792]{1,0:T(8,128)(2,1)S(1)}, bf16[144,1792]{1,0:T(8,128)(2,1)S(1)}, u32[]{:S(2)}, u32[]{:S(2)}) collective-permute-start(bf16[144,1792]{1,0:T(8,128)(2,1)S(1)} %collective-permute-done.2.next_second.next_1), channel_id=1, source_target_pairs={{0,1},{1,0},{2,3},{3,2},{4,5},{5,4},{6,7},{7,6},{8,9},{9,8},{10,11... | collective-permute-start | bytes 1548296 | tf_op jit(solution)/shard_map/ppermute | solution.py:315
  56.0 5.0 %collective-permute-start.8 = (bf16[144,1792]{1,0:T(8,128)(2,1)S(1)}, bf16[144,1792]{1,0:T(8,128)(2,1)S(1)}, u32[]{:S(2)}, u32[]{:S(2)}) collective-permute-start(bf16[144,1792]{1,0:T(8,128)(2,1)S(1)} %get-tuple-element.31), channel_id=1, source_target_pairs={{0,1},{1,0},{2,3},{3,2},{4,5},{5,4},{6,7},{7,6},{8,9},{9,8},{10,11... | collective-permute-start | bytes 1548296 | tf_op jit(solution)/shard_map/ppermute | solution.py:315
  61.0 16.1 %copy-start.1 = (bf16[144,3584]{1,0:T(8,128)(2,1)S(1)}, bf16[144,3584]{1,0:T(8,128)(2,1)}, u32[]{:S(2)}) copy-start(bf16[144,3584]{1,0:T(8,128)(2,1)} %get-tuple-element.23.own_ref) | copy-start | bytes 3096580
  62.3 3.0 %collective-permute-start.10 = (f32[1,144]{1,0:T(1,128)S(1)}, f32[1,144]{1,0:T(1,128)S(1)}, u32[]{:S(2)}, u32[]{:S(2)}) collective-permute-start(f32[1,144]{1,0:T(1,128)S(1)} %get-tuple-element.33.own_row), channel_id=1, source_target_pairs={{0,1},{1,0},{2,3},{3,2},{4,5},{5,4},{6,7},{7,6},{8,9},{9,8},{10,11... | collective-permute-start | bytes 1736 | tf_op jit(solution)/shard_map/ppermute | solution.py:315
  65.4 11.7 %collective-permute-start.11 = (f32[2,144]{1,0:T(2,128)S(1)}, f32[2,144]{1,0:T(2,128)S(1)}, u32[]{:S(2)}, u32[]{:S(2)}) collective-permute-start(f32[2,144]{1,0:T(2,128)S(1)} %pad_maximum_fusion), channel_id=1, source_target_pairs={{0,510},{1,511},{2,4},{3,5},{4,2},{5,3},{6,8},{7,9},{8,6},{9,7},{1... | collective-permute-start | bytes 3464 | tf_op jit(solution)/shard_map/ppermute | solution.py:315
  73.2 5.8 %collective-permute-start.13 = (f32[1,144]{1,0:T(1,128)S(1)}, f32[1,144]{1,0:T(1,128)S(1)}, u32[]{:S(2)}, u32[]{:S(2)}) collective-permute-start(f32[1,144]{1,0:T(1,128)S(1)} %get-tuple-element.33.own_row), channel_id=1, source_target_pairs={{0,509},{1,4},{2,511},{3,6},{4,1},{5,8},{6,3},{7,10},{8,5},{9,12},... | collective-permute-start | bytes 1736 | tf_op jit(solution)/shard_map/ppermute | solution.py:315
  75.2 4.3 %collective-permute-start.12 = (f32[2,144]{1,0:T(2,128)S(1)}, f32[2,144]{1,0:T(2,128)S(1)}, u32[]{:S(2)}, u32[]{:S(2)}) collective-permute-start(f32[2,144]{1,0:T(2,128)S(1)} %pad_maximum_fusion), channel_id=1, source_target_pairs={{0,2},{1,3},{2,0},{3,1},{4,6},{5,7},{6,4},{7,5},{8,10},{9,11},{10,... | collective-permute-start | bytes 3464 | tf_op jit(solution)/shard_map/ppermute | solution.py:315
  77.1 2.4 %copy-start.2 = (bf16[72,3584]{1,0:T(8,128)(2,1)S(1)}, bf16[72,3584]{1,0:T(8,128)(2,1)}, u32[]{:S(2)}) copy-start(bf16[72,3584]{1,0:T(8,128)(2,1)} %query_ref.1) | copy-start | bytes 1548292
  77.1 2.4 %copy-start.3 = (bf16[72,3584]{1,0:T(8,128)(2,1)S(1)}, bf16[72,3584]{1,0:T(8,128)(2,1)}, u32[]{:S(2)}) copy-start(bf16[72,3584]{1,0:T(8,128)(2,1)} %passage_ref.1) | copy-start | bytes 1548292
  77.1 2.4 %copy-start.4 = (f32[144,1]{1,0:T(8,128)S(1)}, f32[144,1]{1,0:T(8,128)}, u32[]{:S(2)}) copy-start(f32[144,1]{1,0:T(8,128)} %get-tuple-element.38.scale_ref) | copy-start | bytes 1732

commit v6 on v5

--- a/solution.py
+++ b/solution.py
@@ -10,6 +10,8 @@
 INV_TEMP = 20.0
 EPS = 1e-06
 TILE = 896
+SPREAD = 8
+CHUNK = 48
 VMEM = pl.BlockSpec(memory_space=pltpu.VMEM)
 HBM = pl.BlockSpec(memory_space=pl.ANY)
 
@@ -31,26 +33,41 @@
 
 
 def unit_kernel(
-    query_any, passage_any, own_ref, first_ref, second_ref, scale_ref, query_ref, passage_ref, sems
+    query_any, passage_any, own_out, first_out, second_out, scale_ref,
+    query_ref, passage_ref, hold_ref, in_sems, out_sems,
 ):
-    copies = [
-        pltpu.make_async_copy(query_any, query_ref, sems.at[0]),
-        pltpu.make_async_copy(passage_any, passage_ref, sems.at[1]),
+    reads = [
+        pltpu.make_async_copy(query_any, query_ref, in_sems.at[0]),
+        pltpu.make_async_copy(passage_any, passage_ref, in_sems.at[1]),
     ]
-    for copy in copies:
+    for copy in reads:
         copy.start()
-    for copy in copies:
+    for copy in reads:
         copy.wait()
     raw_rows = jnp.concatenate(
         [query_ref[...].astype(jnp.float32), passage_ref[...].astype(jnp.float32)], axis=0
     )
-    scale_rows = lax.rsqrt(jnp.sum(raw_rows * raw_rows, axis=1, keepdims=True) + EPS)
-    low_rows = (raw_rows * scale_rows).astype(jnp.bfloat16)
-    width = first_ref.shape[1]
-    own_ref[...] = low_rows
-    first_ref[...] = low_rows[:, :width]
-    second_ref[...] = low_rows[:, width:]
-    scale_ref[...] = scale_rows
+    count, width = hold_ref.shape
+    half = width // 2
+    writes = []
+    for start in range(0, count, CHUNK):
+        rows = slice(start, start + CHUNK)
+        chunk = raw_rows[rows]
+        scale_rows = lax.rsqrt(jnp.sum(chunk * chunk, axis=1, keepdims=True) + EPS)
+        hold_ref[rows, :] = (chunk * scale_rows).astype(jnp.bfloat16)
+        scale_ref[rows, :] = scale_rows
+        for columns, out in (
+            (slice(0, width), own_out),
+            (slice(0, half), first_out),
+            (slice(half, width), second_out),
+        ):
+            copy = pltpu.make_async_copy(
+                hold_ref.at[rows, columns], out.at[rows, :], out_sems.at[len(writes)]
+            )
+            copy.start()
+            writes.append(copy)
+    for copy in writes:
+        copy.wait()
 
 
 def unit_rows(query_raw, passage_raw):
@@ -60,12 +77,14 @@
     return pl.pallas_call(
         unit_kernel,
         in_specs=[HBM, HBM],
-        out_specs=(VMEM, VMEM, VMEM, VMEM),
+        out_specs=(HBM, HBM, HBM, VMEM),
         out_shape=(whole, half, half, jax.ShapeDtypeStruct((2 * rows, 1), jnp.float32)),
         scratch_shapes=[
             pltpu.VMEM((rows, width), jnp.bfloat16),
             pltpu.VMEM((rows, width), jnp.bfloat16),
+            pltpu.VMEM((2 * rows, width), jnp.bfloat16),
             pltpu.SemaphoreType.DMA((2,)),
+            pltpu.SemaphoreType.DMA((3 * 2 * rows // CHUNK,)),
         ],
         compiler_params=pltpu.CompilerParams(vmem_limit_bytes=121 * 2**19),
         cost_estimate=pl.CostEstimate(
@@ -146,7 +165,7 @@
 
 def total_kernel(
     far_score_ref, mass_ref, score_ref, partner_ref, own_ref, own_mate_score, near_mate_ref, mate_first, mate_second,
-    near_mate_out, next_mate_out, recip_ref, loss_ref,
+    near_mate_out, next_mate_out, recip_ref, spread_ref, loss_ref,
 ):
     partner = partner_ref[...]
     own = own_ref[...]
@@ -162,6 +181,7 @@
     eye = eye_of(partner.shape[0])
     norm_row = jnp.sum((eye + partner) * total_col, axis=0, keepdims=True)
     recip_ref[...] = 1.0 / norm_row
+    spread_ref[...] = jnp.broadcast_to(1.0 / norm_row, spread_ref.shape)
     positive = jnp.sum(partner * score_ref[...], axis=0, keepdims=True)
     losses = jnp.log(norm_row) + INV_TEMP - INV_TEMP * positive
     loss_ref[...] = losses[:, : loss_ref.shape[1]]
@@ -178,8 +198,8 @@
 
 
 def part_kernel(
-    partner_ref, own_row, mate_row, next_rows, own_score, mate_score, next_score, next_mate_score,
-    own_ref, mate_ref, next_0, next_1, pair_0, pair_1, sum_ref, along_ref,
+    partner_ref, own_row, mate_row, even_row, next_rows, own_score, mate_score, next_score, next_mate_score,
+    own_ref, mate_ref, next_0, next_1, pair_0, pair_1, sum_ref, along_ref, passed_ref,
 ):
     partner = partner_ref[...]
     count = partner.shape[0]
@@ -200,6 +220,7 @@
         weights.append(low)
         along = along + share
     along_ref[...] = along
+    passed_ref[...] = even_row[0:1, :]
     weights = jnp.concatenate(weights, axis=1)
     half = next_0.shape[1]
     for start in range(0, own_ref.shape[1], TILE):
@@ -223,10 +244,11 @@
     return pl.pallas_call(
         part_kernel,
         in_specs=[VMEM] * len(operands),
-        out_specs=(VMEM, VMEM),
+        out_specs=(VMEM, VMEM, VMEM),
         out_shape=(
             jax.ShapeDtypeStruct((count, width), jnp.float32),
             jax.ShapeDtypeStruct((count, count), jnp.float32),
+            jax.ShapeDtypeStruct((1, count), jnp.float32),
         ),
         compiler_params=pltpu.CompilerParams(vmem_limit_bytes=24 * 2**20),
         cost_estimate=pl.CostEstimate(
@@ -239,7 +261,7 @@
 
 
 def gradient_kernel(
-    sum_ref, along_ref, scale_ref, own_row, near_rows, far_row, near_score, pair_score, far_score,
+    sum_ref, along_ref, scale_ref, own_row, near_rows, even_row, odd_row, near_score, pair_score, far_score,
     near_ref, pair_ref, far_first, far_0, far_1, query_ref, passage_ref,
     query_out, passage_out, query_hold, passage_hold, sems,
 ):
@@ -248,7 +270,7 @@
     recip_col = column_of(own_row[...])
     near_low, near_share = weigh(near_score[...], recip_col, near_rows[0:1, :])
     pair_low, pair_share = weigh(pair_score[...], recip_col, near_rows[1:2, :])
-    far_low, far_share = weigh(far_score[...], recip_col, far_row[...])
+    far_low, far_share = weigh(far_score[...], recip_col, even_row[...] + odd_row[...])
     along = along_ref[...] + near_share + pair_share + far_share
     along = INV_TEMP * jnp.sum(along, axis=1, keepdims=True)
     weights = jnp.concatenate([near_low, pair_low, far_low], axis=1)
@@ -329,8 +351,8 @@
     def far_over_near(chip, core):
         return (chip + 1 if core else chip - 1, 1 - core) if chip % 2 != core else None
 
-    def chip_beyond(chip, core):
-        return (chip + 2 if core else chip - 2, 1 - core)
+    def beyond_of(parity, chip, core):
+        return (chip + 2 if core else chip - 2, 1 - core) if chip % 2 == parity else None
 
     own, first, second, scale = unit_rows(query_raw, passage_raw)
     paired = (pairing[0][:, None] == jnp.arange(rows, dtype=jnp.int32)[None, :]).astype(jnp.float32)
@@ -355,15 +377,15 @@
         [next_halves[0]],
     )
     next_mate = [swapped(half, other_core) for half in (passed, next_halves[1])]
+    far_score = far_scores(own, far_second[0], far_score, 0)
     far_score, mate_score = side_scores(own, mate, far_score, 0)
-    far_score = far_scores(own, far_second[0], far_score, 0)
     far_score = far_scores(own, far_second[1], far_score, 1)
     far_score = far_scores(own, far_first, far_score, 0)
-    near_mate_score, next_mate_score, recip, losses = score_call(
+    near_mate_score, next_mate_score, recip, spread, losses = score_call(
         total_kernel,
         "totals",
         count,
-        [square, square, (1, count), (1, rows)],
+        [square, square, (1, count), (SPREAD, count), (1, rows)],
         [far_score, mass, scores[0], partner, own, mate_score, near_mate, *next_mate],
     )
 
@@ -371,12 +393,13 @@
     chip_rows = jnp.concatenate([recip, mate_row], axis=0)
     near_rows = swapped(chip_rows, near_chip)
     next_rows = swapped(chip_rows, next_chip)
-    far_row = swapped(recip, chip_beyond)
+    even_row = swapped(spread, functools.partial(beyond_of, 0))
+    odd_row = swapped(recip, functools.partial(beyond_of, 1))
 
     near_score, next_score = scores[1:]
-    part_sum, along = part_gradients(
+    part_sum, along, even_row = part_gradients(
         partner,
-        [recip, mate_row, next_rows],
+        [recip, mate_row, even_row, next_rows],
         [scores[0], mate_score, next_score, next_mate_score],
         [own, mate, *next_halves, *next_mate],
     )
@@ -384,7 +407,7 @@
         part_sum,
         along,
         scale,
-        [recip, near_rows, far_row],
+        [recip, near_rows, even_row, odd_row],
         [near_score, near_mate_score, far_score],
         [near, near_mate, far_first, *far_second],
         query_raw,

time: 83.2 us -> 83.6 us (level)
  the two profiles are of different devices: /device:TPU:1 before, /device:TPU:64 now
where the time goes in v6:
time: 83.6 us; the launch traced here: 83.1 us
  starting transfers between devices  55 us (66%)
  waiting for transfers between devices  14.3 us (17%)
  Pallas kernels  10.7 us (13%)
  local copies, waits for them, and re-layouts  1.24 us (1%)
  between operations  0.95 us (1%)
  other arithmetic  0.91 us (1%)
    ppermute x15, starting transfers between devices, swapped(): return lax.ppermute(value, 'dp', pairs)  55 us
    ppermute x15, waiting for transfers between devices, swapped(): return lax.ppermute(value, 'dp', pairs)  14.3 us
    pallas_call x6, Pallas kernels, score_call(): pl.pallas_call(body, in_specs=[VMEM] * len(operands), out_specs=[VMEM] *...  3.81 us
    pallas_call x1, Pallas kernels, unit_rows(): pl.pallas_call(unit_kernel, in_specs=[HBM, HBM], out_specs=(HBM, HBM, HBM...  3.55 us
    pallas_call x1, Pallas kernels, gradients(): pl.pallas_call(gradient_kernel, in_specs=[VMEM] * len(operands), out_spec...  2.07 us
  transfers between devices with their start and end apart: 15, of which 4 were waited for; matrix products, arithmetic and copies ran while one was open for 1% of the time, Pallas kernels for 5%

profile of v6, /device:TPU:64, one launch (start us, length us, event | category | flops | bytes accessed | tf_op | source)
XLA Modules:
  0.0 83.1 jit_solution(5587603907436202366)
XLA Ops:
  0.6 3.6 %unit_rows.1 = (bf16[144,3584]{1,0:T(8,128)(2,1)}, bf16[144,1792]{1,0:T(8,128)(2,1)}, bf16[144,1792]{1,0:T(8,128)(2,1)}, f32[144,1]{1,0:T(8,128)}) custom-call(bf16[72,3584]{1,0:T(8,128)(2,1)} %query_ref.1, bf16[72,3584]{1,0:T(8,128)(2,1)} %passage_ref.1), custom_call_target="tpu_custom_call" | custom-call | flops 1548288 | bytes 2064384 | tf_op jit(solution)/shard_map/unit_rows/pallas_call | solution.py:77
  4.2 6.9 %collective-permute-start = (bf16[144,3584]{1,0:T(8,128)(2,1)}, bf16[144,3584]{1,0:T(8,128)(2,1)S(1)}, u32[]{:S(2)}, u32[]{:S(2)}) collective-permute-start(bf16[144,3584]{1,0:T(8,128)(2,1)} %get-tuple-element.25.own_ref), channel_id=1, source_target_pairs={{0,2},{1,3},{2,0},{3,1},{4,6},{5,7},{6,4},{7,5},{8,10},{9,11},{10,... | collective-permute-start | bytes 3096584 | tf_op jit(solution)/shard_map/ppermute | solution.py:337
  11.1 1.9 %collective-permute-start.4 = (bf16[144,1792]{1,0:T(8,128)(2,1)}, bf16[144,1792]{1,0:T(8,128)(2,1)S(1)}, u32[]{:S(2)}, u32[]{:S(2)}) collective-permute-start(bf16[144,1792]{1,0:T(8,128)(2,1)} %get-tuple-element.27), channel_id=1, source_target_pairs={{0,510},{1,511},{2,4},{3,5},{4,2},{5,3},{6,8},{7,9},{8,6},{9,7},{1... | collective-permute-start | bytes 1548296 | tf_op jit(solution)/shard_map/ppermute | solution.py:337
  13.1 1.9 %collective-permute-start.6 = (bf16[144,3584]{1,0:T(8,128)(2,1)}, bf16[144,3584]{1,0:T(8,128)(2,1)S(1)}, u32[]{:S(2)}, u32[]{:S(2)}) collective-permute-start(bf16[144,3584]{1,0:T(8,128)(2,1)} %get-tuple-element.25.own_ref), channel_id=1, source_target_pairs={{0,1},{1,0},{2,3},{3,2},{4,5},{5,4},{6,7},{7,6},{8,9},{9,8},{10,11... | collective-permute-start | bytes 3096584 | tf_op jit(solution)/shard_map/ppermute | solution.py:337
  15.0 3.9 %collective-permute-start.2 = (bf16[144,1792]{1,0:T(8,128)(2,1)}, bf16[144,1792]{1,0:T(8,128)(2,1)S(1)}, u32[]{:S(2)}, u32[]{:S(2)}) collective-permute-start(bf16[144,1792]{1,0:T(8,128)(2,1)} %get-tuple-element.26), channel_id=1, source_target_pairs={{0,510},{1,511},{2,4},{3,5},{4,2},{5,3},{6,8},{7,9},{8,6},{9,7},{1... | collective-permute-start | bytes 1548296 | tf_op jit(solution)/shard_map/ppermute | solution.py:337
  18.9 11.9 %collective-permute-done.near_ref = bf16[144,3584]{1,0:T(8,128)(2,1)S(1)} collective-permute-done((bf16[144,3584]{1,0:T(8,128)(2,1)}, bf16[144,3584]{1,0:T(8,128)(2,1)S(1)}, u32[]{:S(2)}, u32[]{:S(2)}) %collective-permute-start) | collective-permute-done | bytes 1032224 | tf_op jit(solution)/shard_map/ppermute | solution.py:337
  30.8 0.7 collective-permute-start.1
  31.6 0.0 collective-permute-done.4.next_first.next_0
  31.6 2.9 %collective-permute-start.5 = (bf16[144,1792]{1,0:T(8,128)(2,1)S(1)}, bf16[144,1792]{1,0:T(8,128)(2,1)S(1)}, u32[]{:S(2)}, u32[]{:S(2)}) collective-permute-start(bf16[144,1792]{1,0:T(8,128)(2,1)S(1)} %collective-permute-done.4.next_first.next_0), channel_id=1, source_target_pairs={{1,2},{2,1},{5,6},{6,5},{9,10},{10,9},{13,14},{14,13},{17,18},{18,... | collective-permute-start | bytes 1548296 | tf_op jit(solution)/shard_map/ppermute | solution.py:337
  34.5 4.0 %collective-permute-start.7 = (bf16[144,3584]{1,0:T(8,128)(2,1)S(1)}, bf16[144,3584]{1,0:T(8,128)(2,1)S(1)}, u32[]{:S(2)}, u32[]{:S(2)}) collective-permute-start(bf16[144,3584]{1,0:T(8,128)(2,1)S(1)} %collective-permute-done.near_ref), channel_id=1, source_target_pairs={{0,1},{1,0},{2,3},{3,2},{4,5},{5,4},{6,7},{7,6},{8,9},{9,8},{10,11... | collective-permute-start | bytes 3096584 | tf_op jit(solution)/shard_map/ppermute | solution.py:337
  38.5 0.8 iota_compare_fusion.1
  39.3 0.0 collective-permute-done.2.next_second.next_1
  39.3 11.3 %collective-permute-start.3 = (bf16[144,1792]{1,0:T(8,128)(2,1)S(1)}, bf16[144,1792]{1,0:T(8,128)(2,1)S(1)}, u32[]{:S(2)}, u32[]{:S(2)}) collective-permute-start(bf16[144,1792]{1,0:T(8,128)(2,1)S(1)} %collective-permute-done.2.next_second.next_1), channel_id=1, source_target_pairs={{1,2},{2,1},{5,6},{6,5},{9,10},{10,9},{13,14},{14,13},{17,18},{18,... | collective-permute-start | bytes 1548296 | tf_op jit(solution)/shard_map/ppermute | solution.py:337
  50.6 0.1 fusion.partner_ref
  50.7 0.0 copy-start
  50.7 1.2 %copy-done = bf16[144,3584]{1,0:T(8,128)(2,1)S(1)} copy-done((bf16[144,3584]{1,0:T(8,128)(2,1)S(1)}, bf16[144,3584]{1,0:T(8,128)(2,1)}, u32[]{:S(2)}) %copy-start) | copy-done | bytes 1032216
  51.9 1.0 %early_scores.1 = (f32[144,144]{1,0:T(8,128)S(1)}, f32[144,144]{1,0:T(8,128)S(1)}, f32[144,144]{1,0:T(8,128)S(1)}, f32[144,144]{1,0:T(8,128)S(1)}, f32[144,144]{...) custom-call(f32[144,144]{1,0:T(8,128)S(1)} %fusion.partner_ref, bf16[144,3584]{1,0:T(8,128)(2,1)S(1)} %copy-done, ...), custom_call_target="tpu_custom_call" | custom-call | flops 451878912 | bytes 3138048 | tf_op jit(solution)/shard_map/early_scores/pallas_call | solution.py:99
  52.9 0.0 collective-permute-done.5.far_ref.far_0
  52.9 1.9 %collective-permute-start.9 = (bf16[144,1792]{1,0:T(8,128)(2,1)S(1)}, bf16[144,1792]{1,0:T(8,128)(2,1)S(1)}, u32[]{:S(2)}, u32[]{:S(2)}) collective-permute-start(bf16[144,1792]{1,0:T(8,128)(2,1)S(1)} %collective-permute-done.2.next_second.next_1), channel_id=1, source_target_pairs={{0,1},{1,0},{2,3},{3,2},{4,5},{5,4},{6,7},{7,6},{8,9},{9,8},{10,11... | collective-permute-start | bytes 1548296 | tf_op jit(solution)/shard_map/ppermute | solution.py:337
  54.8 0.0 collective-permute-done.6.key_ref.mate_ref
  54.9 2.4 %collective-permute-start.8 = (bf16[144,1792]{1,0:T(8,128)(2,1)S(1)}, bf16[144,1792]{1,0:T(8,128)(2,1)S(1)}, u32[]{:S(2)}, u32[]{:S(2)}) collective-permute-start(bf16[144,1792]{1,0:T(8,128)(2,1)S(1)} %get-tuple-element.33), channel_id=1, source_target_pairs={{0,1},{1,0},{2,3},{3,2},{4,5},{5,4},{6,7},{7,6},{8,9},{9,8},{10,11... | collective-permute-start | bytes 1548296 | tf_op jit(solution)/shard_map/ppermute | solution.py:337
  57.3 0.3 far_scores.3.sum_ref
  57.6 0.4 side_scores.1
  58.0 0.0 collective-permute-done.3.far_ref.far_1
  58.0 0.3 far_scores.4.sum_ref
  58.3 0.0 collective-permute-done.1.far_ref.far_first
  58.4 0.4 far_scores.5.far_score_ref.far_score
  58.8 0.0 copy-start.1
  58.8 0.0 collective-permute-done.9.mate_second.pair_1
  58.8 0.0 collective-permute-done.8.mate_first.pair_0
  58.8 0.0 collective-permute-done.7.near_mate_ref.pair_ref
  58.8 1.3 %totals.1 = (f32[144,144]{1,0:T(8,128)S(1)}, f32[144,144]{1,0:T(8,128)S(1)}, f32[1,144]{1,0:T(1,128)S(1)}, f32[8,144]{1,0:T(8,128)S(1)}, f32[1,72]{1,0:T(1,128)}) custom-call(f32[144,144]{1,0:T(8,128)S(1)} %far_scores.5.far_score_ref.far_score, f32[144,144]{1,0:T(8,128)S(1)} %get-tuple-element.30.mass_ref, ...), custom_call_target="tpu_custom_call" | custom-call | flops 475766784 | bytes 3303936 | tf_op jit(solution)/shard_map/totals/pallas_call | solution.py:99
  60.2 2.2 %collective-permute-start.10 = (f32[1,144]{1,0:T(1,128)S(1)}, f32[1,144]{1,0:T(1,128)S(1)}, u32[]{:S(2)}, u32[]{:S(2)}) collective-permute-start(f32[1,144]{1,0:T(1,128)S(1)} %get-tuple-element.35.own_row), channel_id=1, source_target_pairs={{0,1},{1,0},{2,3},{3,2},{4,5},{5,4},{6,7},{7,6},{8,9},{9,8},{10,11... | collective-permute-start | bytes 1736 | tf_op jit(solution)/shard_map/ppermute | solution.py:337
  62.4 0.7 collective-permute-start.11
  63.1 0.1 collective-permute-done.10.mate_row
  63.2 5.3 %collective-permute-start.12 = (f32[2,144]{1,0:T(2,128)S(1)}, f32[2,144]{1,0:T(2,128)S(1)}, u32[]{:S(2)}, u32[]{:S(2)}) collective-permute-start(f32[2,144]{1,0:T(2,128)S(1)} %pad_maximum_fusion), channel_id=1, source_target_pairs={{0,510},{1,511},{2,4},{3,5},{4,2},{5,3},{6,8},{7,9},{8,6},{9,7},{1... | collective-permute-start | bytes 3464 | tf_op jit(solution)/shard_map/ppermute | solution.py:337
  68.5 7.1 %collective-permute-start.14 = (f32[1,144]{1,0:T(1,128)S(1)}, f32[1,144]{1,0:T(1,128)S(1)}, u32[]{:S(2)}, u32[]{:S(2)}) collective-permute-start(f32[1,144]{1,0:T(1,128)S(1)} %get-tuple-element.35.own_row), channel_id=1, source_target_pairs={{2,511},{3,6},{6,3},{7,10},{10,7},{11,14},{14,11},{15,18},{18,15},... | collective-permute-start | bytes 1736 | tf_op jit(solution)/shard_map/ppermute | solution.py:337
  75.5 1.9 %collective-permute-start.13 = (f32[2,144]{1,0:T(2,128)S(1)}, f32[2,144]{1,0:T(2,128)S(1)}, u32[]{:S(2)}, u32[]{:S(2)}) collective-permute-start(f32[2,144]{1,0:T(2,128)S(1)} %pad_maximum_fusion), channel_id=1, source_target_pairs={{0,2},{1,3},{2,0},{3,1},{4,6},{5,7},{6,4},{7,5},{8,10},{9,11},{10,... | collective-permute-start | bytes 3464 | tf_op jit(solution)/shard_map/ppermute | solution.py:337
  77.5 0.0 collective-permute-done.12.next_rows
  77.5 0.0 collective-permute-done.11.even_row
  77.5 0.0 copy-done.1
  77.5 0.0 copy-start.2
  77.5 0.0 copy-start.3
  77.5 1.3 %part_gradients.1 = (f32[144,3584]{1,0:T(8,128)S(1)}, f32[144,144]{1,0:T(8,128)S(1)}, f32[1,144]{1,0:T(1,128)S(1)}) custom-call(f32[144,144]{1,0:T(8,128)S(1)} %fusion.partner_ref, f32[1,144]{1,0:T(1,128)S(1)} %get-tuple-element.35.own_row, f32[1,144]{1,0:T(1,128)S(1)} %collective-permute-done.10.mate_row, f32[8,144]{1,0:T(8,128)S(1)} %collective-permute-done.11.even_row, ...), custom_call_target="tpu_custom_call" | custom-call | flops 594542592 | bytes 6193152 | tf_op jit(solution)/shard_map/part_gradients/pallas_call | solution.py:244
  78.8 0.9 %collective-permute-done.14.odd_row = f32[1,144]{1,0:T(1,128)S(1)} collective-permute-done((f32[1,144]{1,0:T(1,128)S(1)}, f32[1,144]{1,0:T(1,128)S(1)}, u32[]{:S(2)}, u32[]{:S(2)}) %collective-permute-start.14) | collective-permute-done | bytes 608 | tf_op jit(solution)/shard_map/ppermute | solution.py:337
  79.7 1.3 %collective-permute-done.13.near_rows = f32[2,144]{1,0:T(2,128)S(1)} collective-permute-done((f32[2,144]{1,0:T(2,128)S(1)}, f32[2,144]{1,0:T(2,128)S(1)}, u32[]{:S(2)}, u32[]{:S(2)}) %collective-permute-start.13) | collective-permute-done | bytes 1184 | tf_op jit(solution)/shard_map/ppermute | solution.py:337
  81.0 0.0 copy-done.4
  81.0 2.1 %gradients.1 = (f32[72,3584]{1,0:T(8,128)}, f32[72,3584]{1,0:T(8,128)}) custom-call(f32[144,3584]{1,0:T(8,128)S(1)} %get-tuple-element.39.sum_ref, f32[144,144]{1,0:T(8,128)S(1)} %get-tuple-element.40.along_ref, f32[144,1]{1,0:T(8,128)S(1)} %copy-done.4, f32[1,144]{1,0:T(1,128)S(1)} %get-tuple-element.35.own_row, ...), custom_call_target="tpu_custom_call" | custom-call | flops 445906944 | bytes 8257536 | tf_op jit(solution)/shard_map/gradients/pallas_call | solution.py:306
  (4 shorter events, 0.0 us)
Async XLA Ops:
  4.2 26.7 %collective-permute-start = (bf16[144,3584]{1,0:T(8,128)(2,1)}, bf16[144,3584]{1,0:T(8,128)(2,1)S(1)}, u32[]{:S(2)}, u32[]{:S(2)}) collective-permute-start(bf16[144,3584]{1,0:T(8,128)(2,1)} %get-tuple-element.25.own_ref), channel_id=1, source_target_pairs={{0,2},{1,3},{2,0},{3,1},{4,6},{5,7},{6,4},{7,5},{8,10},{9,11},{10,... | collective-permute-start | bytes 3096584 | tf_op jit(solution)/shard_map/ppermute | solution.py:337
  11.1 20.4 %collective-permute-start.4 = (bf16[144,1792]{1,0:T(8,128)(2,1)}, bf16[144,1792]{1,0:T(8,128)(2,1)S(1)}, u32[]{:S(2)}, u32[]{:S(2)}) collective-permute-start(bf16[144,1792]{1,0:T(8,128)(2,1)} %get-tuple-element.27), channel_id=1, source_target_pairs={{0,510},{1,511},{2,4},{3,5},{4,2},{5,3},{6,8},{7,9},{8,6},{9,7},{1... | collective-permute-start | bytes 1548296 | tf_op jit(solution)/shard_map/ppermute | solution.py:337
  13.1 41.8 %collective-permute-start.6 = (bf16[144,3584]{1,0:T(8,128)(2,1)}, bf16[144,3584]{1,0:T(8,128)(2,1)S(1)}, u32[]{:S(2)}, u32[]{:S(2)}) collective-permute-start(bf16[144,3584]{1,0:T(8,128)(2,1)} %get-tuple-element.25.own_ref), channel_id=1, source_target_pairs={{0,1},{1,0},{2,3},{3,2},{4,5},{5,4},{6,7},{7,6},{8,9},{9,8},{10,11... | collective-permute-start | bytes 3096584 | tf_op jit(solution)/shard_map/ppermute | solution.py:337
  15.0 24.3 %collective-permute-start.2 = (bf16[144,1792]{1,0:T(8,128)(2,1)}, bf16[144,1792]{1,0:T(8,128)(2,1)S(1)}, u32[]{:S(2)}, u32[]{:S(2)}) collective-permute-start(bf16[144,1792]{1,0:T(8,128)(2,1)} %get-tuple-element.26), channel_id=1, source_target_pairs={{0,510},{1,511},{2,4},{3,5},{4,2},{5,3},{6,8},{7,9},{8,6},{9,7},{1... | collective-permute-start | bytes 1548296 | tf_op jit(solution)/shard_map/ppermute | solution.py:337
  30.8 27.5 %collective-permute-start.1 = (bf16[144,3584]{1,0:T(8,128)(2,1)S(1)}, bf16[144,3584]{1,0:T(8,128)(2,1)S(1)}, u32[]{:S(2)}, u32[]{:S(2)}) collective-permute-start(bf16[144,3584]{1,0:T(8,128)(2,1)S(1)} %collective-permute-done.near_ref), channel_id=1, source_target_pairs={{0,511},{3,4},{4,3},{7,8},{8,7},{11,12},{12,11},{15,16},{16,15},{1... | collective-permute-start | bytes 3096584 | tf_op jit(solution)/shard_map/ppermute | solution.py:337
  31.6 21.3 %collective-permute-start.5 = (bf16[144,1792]{1,0:T(8,128)(2,1)S(1)}, bf16[144,1792]{1,0:T(8,128)(2,1)S(1)}, u32[]{:S(2)}, u32[]{:S(2)}) collective-permute-start(bf16[144,1792]{1,0:T(8,128)(2,1)S(1)} %collective-permute-done.4.next_first.next_0), channel_id=1, source_target_pairs={{1,2},{2,1},{5,6},{6,5},{9,10},{10,9},{13,14},{14,13},{17,18},{18,... | collective-permute-start | bytes 1548296 | tf_op jit(solution)/shard_map/ppermute | solution.py:337
  34.5 24.3 %collective-permute-start.7 = (bf16[144,3584]{1,0:T(8,128)(2,1)S(1)}, bf16[144,3584]{1,0:T(8,128)(2,1)S(1)}, u32[]{:S(2)}, u32[]{:S(2)}) collective-permute-start(bf16[144,3584]{1,0:T(8,128)(2,1)S(1)} %collective-permute-done.near_ref), channel_id=1, source_target_pairs={{0,1},{1,0},{2,3},{3,2},{4,5},{5,4},{6,7},{7,6},{8,9},{9,8},{10,11... | collective-permute-start | bytes 3096584 | tf_op jit(solution)/shard_map/ppermute | solution.py:337
  39.3 18.7 %collective-permute-start.3 = (bf16[144,1792]{1,0:T(8,128)(2,1)S(1)}, bf16[144,1792]{1,0:T(8,128)(2,1)S(1)}, u32[]{:S(2)}, u32[]{:S(2)}) collective-permute-start(bf16[144,1792]{1,0:T(8,128)(2,1)S(1)} %collective-permute-done.2.next_second.next_1), channel_id=1, source_target_pairs={{1,2},{2,1},{5,6},{6,5},{9,10},{10,9},{13,14},{14,13},{17,18},{18,... | collective-permute-start | bytes 1548296 | tf_op jit(solution)/shard_map/ppermute | solution.py:337
  50.7 1.2 %copy-start = (bf16[144,3584]{1,0:T(8,128)(2,1)S(1)}, bf16[144,3584]{1,0:T(8,128)(2,1)}, u32[]{:S(2)}) copy-start(bf16[144,3584]{1,0:T(8,128)(2,1)} %get-tuple-element.25.own_ref) | copy-start | bytes 3096580
  52.9 5.9 %collective-permute-start.9 = (bf16[144,1792]{1,0:T(8,128)(2,1)S(1)}, bf16[144,1792]{1,0:T(8,128)(2,1)S(1)}, u32[]{:S(2)}, u32[]{:S(2)}) collective-permute-start(bf16[144,1792]{1,0:T(8,128)(2,1)S(1)} %collective-permute-done.2.next_second.next_1), channel_id=1, source_target_pairs={{0,1},{1,0},{2,3},{3,2},{4,5},{5,4},{6,7},{7,6},{8,9},{9,8},{10,11... | collective-permute-start | bytes 1548296 | tf_op jit(solution)/shard_map/ppermute | solution.py:337
  54.9 4.0 %collective-permute-start.8 = (bf16[144,1792]{1,0:T(8,128)(2,1)S(1)}, bf16[144,1792]{1,0:T(8,128)(2,1)S(1)}, u32[]{:S(2)}, u32[]{:S(2)}) collective-permute-start(bf16[144,1792]{1,0:T(8,128)(2,1)S(1)} %get-tuple-element.33), channel_id=1, source_target_pairs={{0,1},{1,0},{2,3},{3,2},{4,5},{5,4},{6,7},{7,6},{8,9},{9,8},{10,11... | collective-permute-start | bytes 1548296 | tf_op jit(solution)/shard_map/ppermute | solution.py:337
  58.8 18.7 %copy-start.1 = (bf16[144,3584]{1,0:T(8,128)(2,1)S(1)}, bf16[144,3584]{1,0:T(8,128)(2,1)}, u32[]{:S(2)}) copy-start(bf16[144,3584]{1,0:T(8,128)(2,1)} %get-tuple-element.25.own_ref) | copy-start | bytes 3096580
  60.2 3.0 %collective-permute-start.10 = (f32[1,144]{1,0:T(1,128)S(1)}, f32[1,144]{1,0:T(1,128)S(1)}, u32[]{:S(2)}, u32[]{:S(2)}) collective-permute-start(f32[1,144]{1,0:T(1,128)S(1)} %get-tuple-element.35.own_row), channel_id=1, source_target_pairs={{0,1},{1,0},{2,3},{3,2},{4,5},{5,4},{6,7},{7,6},{8,9},{9,8},{10,11... | collective-permute-start | bytes 1736 | tf_op jit(solution)/shard_map/ppermute | solution.py:337
  62.4 15.1 %collective-permute-start.11 = (f32[8,144]{1,0:T(8,128)S(1)}, f32[8,144]{1,0:T(8,128)S(1)}, u32[]{:S(2)}, u32[]{:S(2)}) collective-permute-start(f32[8,144]{1,0:T(8,128)S(1)} %get-tuple-element.36), channel_id=1, source_target_pairs={{0,509},{1,4},{4,1},{5,8},{8,5},{9,12},{12,9},{13,16},{16,13},{17,... | collective-permute-start | bytes 13832 | tf_op jit(solution)/shard_map/ppermute | solution.py:337
  63.2 14.3 %collective-permute-start.12 = (f32[2,144]{1,0:T(2,128)S(1)}, f32[2,144]{1,0:T(2,128)S(1)}, u32[]{:S(2)}, u32[]{:S(2)}) collective-permute-start(f32[2,144]{1,0:T(2,128)S(1)} %pad_maximum_fusion), channel_id=1, source_target_pairs={{0,510},{1,511},{2,4},{3,5},{4,2},{5,3},{6,8},{7,9},{8,6},{9,7},{1... | collective-permute-start | bytes 3464 | tf_op jit(solution)/shard_map/ppermute | solution.py:337
  68.5 11.2 %collective-permute-start.14 = (f32[1,144]{1,0:T(1,128)S(1)}, f32[1,144]{1,0:T(1,128)S(1)}, u32[]{:S(2)}, u32[]{:S(2)}) collective-permute-start(f32[1,144]{1,0:T(1,128)S(1)} %get-tuple-element.35.own_row), channel_id=1, source_target_pairs={{2,511},{3,6},{6,3},{7,10},{10,7},{11,14},{14,11},{15,18},{18,15},... | collective-permute-start | bytes 1736 | tf_op jit(solution)/shard_map/ppermute | solution.py:337
  75.5 5.5 %collective-permute-start.13 = (f32[2,144]{1,0:T(2,128)S(1)}, f32[2,144]{1,0:T(2,128)S(1)}, u32[]{:S(2)}, u32[]{:S(2)}) collective-permute-start(f32[2,144]{1,0:T(2,128)S(1)} %pad_maximum_fusion), channel_id=1, source_target_pairs={{0,2},{1,3},{2,0},{3,1},{4,6},{5,7},{6,4},{7,5},{8,10},{9,11},{10,... | collective-permute-start | bytes 3464 | tf_op jit(solution)/shard_map/ppermute | solution.py:337
  77.5 3.5 %copy-start.2 = (bf16[72,3584]{1,0:T(8,128)(2,1)S(1)}, bf16[72,3584]{1,0:T(8,128)(2,1)}, u32[]{:S(2)}) copy-start(bf16[72,3584]{1,0:T(8,128)(2,1)} %query_ref.1) | copy-start | bytes 1548292
  77.5 3.5 %copy-start.3 = (bf16[72,3584]{1,0:T(8,128)(2,1)S(1)}, bf16[72,3584]{1,0:T(8,128)(2,1)}, u32[]{:S(2)}) copy-start(bf16[72,3584]{1,0:T(8,128)(2,1)} %passage_ref.1) | copy-start | bytes 1548292
  77.5 3.5 %copy-start.4 = (f32[144,1]{1,0:T(8,128)S(1)}, f32[144,1]{1,0:T(8,128)}, u32[]{:S(2)}) copy-start(f32[144,1]{1,0:T(8,128)} %get-tuple-element.41.scale_ref) | copy-start | bytes 1732

commit v7 on v5

--- a/solution.py
+++ b/solution.py
@@ -10,6 +10,7 @@
 INV_TEMP = 20.0
 EPS = 1e-06
 TILE = 896
+SPREAD = 8
 VMEM = pl.BlockSpec(memory_space=pltpu.VMEM)
 HBM = pl.BlockSpec(memory_space=pl.ANY)
 
@@ -146,7 +147,7 @@
 
 def total_kernel(
     far_score_ref, mass_ref, score_ref, partner_ref, own_ref, own_mate_score, near_mate_ref, mate_first, mate_second,
-    near_mate_out, next_mate_out, recip_ref, loss_ref,
+    near_mate_out, next_mate_out, recip_ref, spread_ref, loss_ref,
 ):
     partner = partner_ref[...]
     own = own_ref[...]
@@ -162,6 +163,7 @@
     eye = eye_of(partner.shape[0])
     norm_row = jnp.sum((eye + partner) * total_col, axis=0, keepdims=True)
     recip_ref[...] = 1.0 / norm_row
+    spread_ref[...] = jnp.broadcast_to(1.0 / norm_row, spread_ref.shape)
     positive = jnp.sum(partner * score_ref[...], axis=0, keepdims=True)
     losses = jnp.log(norm_row) + INV_TEMP - INV_TEMP * positive
     loss_ref[...] = losses[:, : loss_ref.shape[1]]
@@ -178,8 +180,8 @@
 
 
 def part_kernel(
-    partner_ref, own_row, mate_row, next_rows, own_score, mate_score, next_score, next_mate_score,
-    own_ref, mate_ref, next_0, next_1, pair_0, pair_1, sum_ref, along_ref,
+    partner_ref, own_row, mate_row, even_row, near_rows, own_score, mate_score, near_score, pair_score,
+    own_ref, mate_ref, near_ref, pair_ref, sum_ref, along_ref, passed_ref,
 ):
     partner = partner_ref[...]
     count = partner.shape[0]
@@ -193,25 +195,18 @@
     along = low.astype(jnp.float32) * score
     for score_ref, row in (
         (mate_score, mate_row[...]),
-        (next_score, next_rows[0:1, :]),
-        (next_mate_score, next_rows[1:2, :]),
+        (near_score, near_rows[0:1, :]),
+        (pair_score, near_rows[1:2, :]),
     ):
         low, share = weigh(score_ref[...], recip_col, row)
         weights.append(low)
         along = along + share
     along_ref[...] = along
+    passed_ref[...] = even_row[0:1, :]
     weights = jnp.concatenate(weights, axis=1)
-    half = next_0.shape[1]
     for start in range(0, own_ref.shape[1], TILE):
         whole = slice(start, start + TILE)
-        columns = slice(start % half, start % half + TILE)
-        next_ref, pair_ref = ((next_0, pair_0), (next_1, pair_1))[start // half]
-        keys = [
-            own_ref[:, whole],
-            mate_ref[:, whole],
-            next_ref[:, columns],
-            pair_ref[:, columns],
-        ]
+        keys = [own_ref[:, whole], mate_ref[:, whole], near_ref[:, whole], pair_ref[:, whole]]
         keys = jnp.concatenate(keys, axis=0)
         sum_ref[:, whole] = jnp.dot(weights, keys, preferred_element_type=jnp.float32)
 
@@ -223,10 +218,11 @@
     return pl.pallas_call(
         part_kernel,
         in_specs=[VMEM] * len(operands),
-        out_specs=(VMEM, VMEM),
+        out_specs=(VMEM, VMEM, VMEM),
         out_shape=(
             jax.ShapeDtypeStruct((count, width), jnp.float32),
             jax.ShapeDtypeStruct((count, count), jnp.float32),
+            jax.ShapeDtypeStruct((1, count), jnp.float32),
         ),
         compiler_params=pltpu.CompilerParams(vmem_limit_bytes=24 * 2**20),
         cost_estimate=pl.CostEstimate(
@@ -239,27 +235,28 @@
 
 
 def gradient_kernel(
-    sum_ref, along_ref, scale_ref, own_row, near_rows, far_row, near_score, pair_score, far_score,
-    near_ref, pair_ref, far_first, far_0, far_1, query_ref, passage_ref,
+    sum_ref, along_ref, scale_ref, own_row, next_rows, even_row, odd_row, next_score, pair_score, far_score,
+    next_0, next_1, pair_0, pair_1, far_first, far_0, far_1, query_ref, passage_ref,
     query_out, passage_out, query_hold, passage_hold, sems,
 ):
     count = along_ref.shape[0]
     rows = count // 2
     recip_col = column_of(own_row[...])
-    near_low, near_share = weigh(near_score[...], recip_col, near_rows[0:1, :])
-    pair_low, pair_share = weigh(pair_score[...], recip_col, near_rows[1:2, :])
-    far_low, far_share = weigh(far_score[...], recip_col, far_row[...])
-    along = along_ref[...] + near_share + pair_share + far_share
+    next_low, next_share = weigh(next_score[...], recip_col, next_rows[0:1, :])
+    pair_low, pair_share = weigh(pair_score[...], recip_col, next_rows[1:2, :])
+    far_low, far_share = weigh(far_score[...], recip_col, even_row[...] + odd_row[...])
+    along = along_ref[...] + next_share + pair_share + far_share
     along = INV_TEMP * jnp.sum(along, axis=1, keepdims=True)
-    weights = jnp.concatenate([near_low, pair_low, far_low], axis=1)
+    weights = jnp.concatenate([next_low, pair_low, far_low], axis=1)
     half = far_0.shape[1]
     scale = scale_ref[...]
     copies = []
-    for start in range(0, near_ref.shape[1], TILE):
+    for start in range(0, far_first.shape[1], TILE):
         whole = slice(start, start + TILE)
-        far_ref = (far_0, far_1)[start // half]
-        far = far_first[:, whole] + far_ref[:, start % half : start % half + TILE]
-        keys = jnp.concatenate([near_ref[:, whole], pair_ref[:, whole], far], axis=0)
+        columns = slice(start % half, start % half + TILE)
+        next_ref, pair_ref, far_ref = ((next_0, pair_0, far_0), (next_1, pair_1, far_1))[start // half]
+        far = far_first[:, whole] + far_ref[:, columns]
+        keys = jnp.concatenate([next_ref[:, columns], pair_ref[:, columns], far], axis=0)
         gradient = jnp.dot(weights, keys, preferred_element_type=jnp.float32) + sum_ref[:, whole]
         for part, raw_ref, hold, out in (
             (0, query_ref, query_hold, query_out),
@@ -329,8 +326,8 @@
     def far_over_near(chip, core):
         return (chip + 1 if core else chip - 1, 1 - core) if chip % 2 != core else None
 
-    def chip_beyond(chip, core):
-        return (chip + 2 if core else chip - 2, 1 - core)
+    def beyond_of(parity, chip, core):
+        return (chip + 2 if core else chip - 2, 1 - core) if chip % 2 == parity else None
 
     own, first, second, scale = unit_rows(query_raw, passage_raw)
     paired = (pairing[0][:, None] == jnp.arange(rows, dtype=jnp.int32)[None, :]).astype(jnp.float32)
@@ -355,15 +352,15 @@
         [next_halves[0]],
     )
     next_mate = [swapped(half, other_core) for half in (passed, next_halves[1])]
+    far_score = far_scores(own, far_second[0], far_score, 0)
     far_score, mate_score = side_scores(own, mate, far_score, 0)
-    far_score = far_scores(own, far_second[0], far_score, 0)
     far_score = far_scores(own, far_second[1], far_score, 1)
     far_score = far_scores(own, far_first, far_score, 0)
-    near_mate_score, next_mate_score, recip, losses = score_call(
+    near_mate_score, next_mate_score, recip, spread, losses = score_call(
         total_kernel,
         "totals",
         count,
-        [square, square, (1, count), (1, rows)],
+        [square, square, (1, count), (SPREAD, count), (1, rows)],
         [far_score, mass, scores[0], partner, own, mate_score, near_mate, *next_mate],
     )
 
@@ -371,22 +368,23 @@
     chip_rows = jnp.concatenate([recip, mate_row], axis=0)
     near_rows = swapped(chip_rows, near_chip)
     next_rows = swapped(chip_rows, next_chip)
-    far_row = swapped(recip, chip_beyond)
+    even_row = swapped(spread, functools.partial(beyond_of, 0))
+    odd_row = swapped(recip, functools.partial(beyond_of, 1))
 
     near_score, next_score = scores[1:]
-    part_sum, along = part_gradients(
+    part_sum, along, even_row = part_gradients(
         partner,
-        [recip, mate_row, next_rows],
-        [scores[0], mate_score, next_score, next_mate_score],
-        [own, mate, *next_halves, *next_mate],
+        [recip, mate_row, even_row, near_rows],
+        [scores[0], mate_score, near_score, near_mate_score],
+        [own, mate, near, near_mate],
     )
     query_grad, passage_grad = gradients(
         part_sum,
         along,
         scale,
-        [recip, near_rows, far_row],
-        [near_score, near_mate_score, far_score],
-        [near, near_mate, far_first, *far_second],
+        [recip, next_rows, even_row, odd_row],
+        [next_score, next_mate_score, far_score],
+        [*next_halves, *next_mate, far_first, *far_second],
         query_raw,
         passage_raw,
     )

time: 83.2 us -> 88.3 us (1.061); the launches traced: 81.6 us -> 87.7 us
  starting transfers between devices: 55.6 us -> 67.9 us
  waiting for transfers between devices: 12.9 us -> 6.61 us
    ppermute x14 -> x15, starting transfers between devices: 55.6 us -> 67.9 us  [swapped(): return lax.ppermute(value, 'dp', pairs)]
    ppermute x14 -> x15, waiting for transfers between devices: 12.9 us -> 6.61 us  [swapped(): return lax.ppermute(value, 'dp', pairs)]
  transfers between devices with their start and end apart: 14 -> 15, of which waited for: 5 -> 2; matrix products, arithmetic and copies ran while one was open for 1% -> 1% of each run, Pallas kernels for 5% -> 4%
where the time goes in v7:
time: 88.3 us; the launch traced here: 87.7 us
  starting transfers between devices  67.9 us (77%)
  Pallas kernels  10.1 us (11%)
  waiting for transfers between devices  6.61 us (7%)
  local copies, waits for them, and re-layouts  1.24 us (1%)
  between operations  0.99 us (1%)
  other arithmetic  0.91 us (1%)
    ppermute x15, starting transfers between devices, swapped(): return lax.ppermute(value, 'dp', pairs)  67.9 us
    ppermute x15, waiting for transfers between devices, swapped(): return lax.ppermute(value, 'dp', pairs)  6.61 us
    pallas_call x6, Pallas kernels, score_call(): pl.pallas_call(body, in_specs=[VMEM] * len(operands), out_specs=[VMEM] *...  3.8 us
    pallas_call x1, Pallas kernels, unit_rows(): pl.pallas_call(unit_kernel, in_specs=[HBM, HBM], out_specs=(VMEM, VMEM, V...  2.93 us
    pallas_call x1, Pallas kernels, gradients(): pl.pallas_call(gradient_kernel, in_specs=[VMEM] * len(operands), out_spec...  2.06 us
  transfers between devices with their start and end apart: 15, of which 2 were waited for; matrix products, arithmetic and copies ran while one was open for 1% of the time, Pallas kernels for 4%

profile of v7, /device:TPU:1, one launch (start us, length us, event | category | flops | bytes accessed | tf_op | source)
XLA Modules:
  0.0 87.7 jit_solution(2772077945989275088)
XLA Ops:
  0.6 2.9 %unit_rows.1 = (bf16[144,3584]{1,0:T(8,128)(2,1)}, bf16[144,1792]{1,0:T(8,128)(2,1)}, bf16[144,1792]{1,0:T(8,128)(2,1)}, f32[144,1]{1,0:T(8,128)}) custom-call(bf16[72,3584]{1,0:T(8,128)(2,1)} %query_ref.1, bf16[72,3584]{1,0:T(8,128)(2,1)} %passage_ref.1), custom_call_target="tpu_custom_call" | custom-call | flops 1548288 | bytes 2064384 | tf_op jit(solution)/shard_map/unit_rows/pallas_call | solution.py:61
  3.6 4.8 %collective-permute-start = (bf16[144,3584]{1,0:T(8,128)(2,1)}, bf16[144,3584]{1,0:T(8,128)(2,1)S(1)}, u32[]{:S(2)}, u32[]{:S(2)}) collective-permute-start(bf16[144,3584]{1,0:T(8,128)(2,1)} %get-tuple-element.25.own_ref), channel_id=1, source_target_pairs={{0,2},{1,3},{2,0},{3,1},{4,6},{5,7},{6,4},{7,5},{8,10},{9,11},{10,... | collective-permute-start | bytes 3096584 | tf_op jit(solution)/shard_map/ppermute | solution.py:312
  8.4 13.9 %collective-permute-start.4 = (bf16[144,1792]{1,0:T(8,128)(2,1)}, bf16[144,1792]{1,0:T(8,128)(2,1)S(1)}, u32[]{:S(2)}, u32[]{:S(2)}) collective-permute-start(bf16[144,1792]{1,0:T(8,128)(2,1)} %get-tuple-element.27), channel_id=1, source_target_pairs={{0,510},{1,511},{2,4},{3,5},{4,2},{5,3},{6,8},{7,9},{8,6},{9,7},{1... | collective-permute-start | bytes 1548296 | tf_op jit(solution)/shard_map/ppermute | solution.py:312
  22.4 3.1 %collective-permute-start.6 = (bf16[144,3584]{1,0:T(8,128)(2,1)}, bf16[144,3584]{1,0:T(8,128)(2,1)S(1)}, u32[]{:S(2)}, u32[]{:S(2)}) collective-permute-start(bf16[144,3584]{1,0:T(8,128)(2,1)} %get-tuple-element.25.own_ref), channel_id=1, source_target_pairs={{0,1},{1,0},{2,3},{3,2},{4,5},{5,4},{6,7},{7,6},{8,9},{9,8},{10,11... | collective-permute-start | bytes 3096584 | tf_op jit(solution)/shard_map/ppermute | solution.py:312
  25.5 1.9 %collective-permute-start.2 = (bf16[144,1792]{1,0:T(8,128)(2,1)}, bf16[144,1792]{1,0:T(8,128)(2,1)S(1)}, u32[]{:S(2)}, u32[]{:S(2)}) collective-permute-start(bf16[144,1792]{1,0:T(8,128)(2,1)} %get-tuple-element.26), channel_id=1, source_target_pairs={{0,510},{1,511},{2,4},{3,5},{4,2},{5,3},{6,8},{7,9},{8,6},{9,7},{1... | collective-permute-start | bytes 1548296 | tf_op jit(solution)/shard_map/ppermute | solution.py:312
  27.4 0.0 collective-permute-done.near_ref
  27.4 0.7 collective-permute-start.1
  28.2 5.5 %collective-permute-done.4.next_first.next_0 = bf16[144,1792]{1,0:T(8,128)(2,1)S(1)} collective-permute-done((bf16[144,1792]{1,0:T(8,128)(2,1)}, bf16[144,1792]{1,0:T(8,128)(2,1)S(1)}, u32[]{:S(2)}, u32[]{:S(2)}) %collective-permute-start.4) | collective-permute-done | bytes 516128 | tf_op jit(solution)/shard_map/ppermute | solution.py:312
  33.7 2.6 %collective-permute-start.5 = (bf16[144,1792]{1,0:T(8,128)(2,1)S(1)}, bf16[144,1792]{1,0:T(8,128)(2,1)S(1)}, u32[]{:S(2)}, u32[]{:S(2)}) collective-permute-start(bf16[144,1792]{1,0:T(8,128)(2,1)S(1)} %collective-permute-done.4.next_first.next_0), channel_id=1, source_target_pairs={{1,2},{2,1},{5,6},{6,5},{9,10},{10,9},{13,14},{14,13},{17,18},{18,... | collective-permute-start | bytes 1548296 | tf_op jit(solution)/shard_map/ppermute | solution.py:312
  36.3 12.6 %collective-permute-start.7 = (bf16[144,3584]{1,0:T(8,128)(2,1)S(1)}, bf16[144,3584]{1,0:T(8,128)(2,1)S(1)}, u32[]{:S(2)}, u32[]{:S(2)}) collective-permute-start(bf16[144,3584]{1,0:T(8,128)(2,1)S(1)} %collective-permute-done.near_ref), channel_id=1, source_target_pairs={{0,1},{1,0},{2,3},{3,2},{4,5},{5,4},{6,7},{7,6},{8,9},{9,8},{10,11... | collective-permute-start | bytes 3096584 | tf_op jit(solution)/shard_map/ppermute | solution.py:312
  49.0 0.8 iota_compare_fusion.1
  49.8 0.0 collective-permute-done.2.next_second.next_1
  49.8 1.9 %collective-permute-start.3 = (bf16[144,1792]{1,0:T(8,128)(2,1)S(1)}, bf16[144,1792]{1,0:T(8,128)(2,1)S(1)}, u32[]{:S(2)}, u32[]{:S(2)}) collective-permute-start(bf16[144,1792]{1,0:T(8,128)(2,1)S(1)} %collective-permute-done.2.next_second.next_1), channel_id=1, source_target_pairs={{1,2},{2,1},{5,6},{6,5},{9,10},{10,9},{13,14},{14,13},{17,18},{18,... | collective-permute-start | bytes 1548296 | tf_op jit(solution)/shard_map/ppermute | solution.py:312
  51.7 0.1 fusion.partner_ref
  51.8 0.0 copy-start
  51.8 1.2 %copy-done = bf16[144,3584]{1,0:T(8,128)(2,1)S(1)} copy-done((bf16[144,3584]{1,0:T(8,128)(2,1)S(1)}, bf16[144,3584]{1,0:T(8,128)(2,1)}, u32[]{:S(2)}) %copy-start) | copy-done | bytes 1032216
  53.0 1.0 %early_scores.1 = (f32[144,144]{1,0:T(8,128)S(1)}, f32[144,144]{1,0:T(8,128)S(1)}, f32[144,144]{1,0:T(8,128)S(1)}, f32[144,144]{1,0:T(8,128)S(1)}, f32[144,144]{...) custom-call(f32[144,144]{1,0:T(8,128)S(1)} %fusion.partner_ref, bf16[144,3584]{1,0:T(8,128)(2,1)S(1)} %copy-done, ...), custom_call_target="tpu_custom_call" | custom-call | flops 451878912 | bytes 3138048 | tf_op jit(solution)/shard_map/early_scores/pallas_call | solution.py:81
  54.0 0.0 collective-permute-done.5.far_ref.far_0
  54.0 1.9 %collective-permute-start.9 = (bf16[144,1792]{1,0:T(8,128)(2,1)S(1)}, bf16[144,1792]{1,0:T(8,128)(2,1)S(1)}, u32[]{:S(2)}, u32[]{:S(2)}) collective-permute-start(bf16[144,1792]{1,0:T(8,128)(2,1)S(1)} %collective-permute-done.2.next_second.next_1), channel_id=1, source_target_pairs={{0,1},{1,0},{2,3},{3,2},{4,5},{5,4},{6,7},{7,6},{8,9},{9,8},{10,11... | collective-permute-start | bytes 1548296 | tf_op jit(solution)/shard_map/ppermute | solution.py:312
  56.0 0.0 collective-permute-done.6.key_ref.mate_ref
  56.0 2.4 %collective-permute-start.8 = (bf16[144,1792]{1,0:T(8,128)(2,1)S(1)}, bf16[144,1792]{1,0:T(8,128)(2,1)S(1)}, u32[]{:S(2)}, u32[]{:S(2)}) collective-permute-start(bf16[144,1792]{1,0:T(8,128)(2,1)S(1)} %get-tuple-element.33), channel_id=1, source_target_pairs={{0,1},{1,0},{2,3},{3,2},{4,5},{5,4},{6,7},{7,6},{8,9},{9,8},{10,11... | collective-permute-start | bytes 1548296 | tf_op jit(solution)/shard_map/ppermute | solution.py:312
  58.4 0.3 far_scores.3.sum_ref
  58.7 0.4 side_scores.1
  59.1 1.1 %collective-permute-done.3.far_ref.far_1 = bf16[144,1792]{1,0:T(8,128)(2,1)S(1)} collective-permute-done((bf16[144,1792]{1,0:T(8,128)(2,1)S(1)}, bf16[144,1792]{1,0:T(8,128)(2,1)S(1)}, u32[]{:S(2)}, u32[]{:S(2)}) %collective-permute-start.3) | collective-permute-done | bytes 516128 | tf_op jit(solution)/shard_map/ppermute | solution.py:312
  60.2 0.3 far_scores.4.sum_ref
  60.5 0.0 collective-permute-done.1.far_ref.far_first
  60.5 0.4 far_scores.5.far_score_ref.far_score
  61.0 0.0 copy-start.1
  61.0 0.0 collective-permute-done.9.mate_second.pair_1
  61.0 0.0 collective-permute-done.8.mate_first.pair_0
  61.0 0.0 collective-permute-done.7.near_mate_ref.pair_ref
  61.0 1.3 %totals.1 = (f32[144,144]{1,0:T(8,128)S(1)}, f32[144,144]{1,0:T(8,128)S(1)}, f32[1,144]{1,0:T(1,128)S(1)}, f32[8,144]{1,0:T(8,128)S(1)}, f32[1,72]{1,0:T(1,128)}) custom-call(f32[144,144]{1,0:T(8,128)S(1)} %far_scores.5.far_score_ref.far_score, f32[144,144]{1,0:T(8,128)S(1)} %get-tuple-element.30.mass_ref, ...), custom_call_target="tpu_custom_call" | custom-call | flops 475766784 | bytes 3303936 | tf_op jit(solution)/shard_map/totals/pallas_call | solution.py:81
  62.3 1.9 %collective-permute-start.10 = (f32[1,144]{1,0:T(1,128)S(1)}, f32[1,144]{1,0:T(1,128)S(1)}, u32[]{:S(2)}, u32[]{:S(2)}) collective-permute-start(f32[1,144]{1,0:T(1,128)S(1)} %get-tuple-element.35.own_row), channel_id=1, source_target_pairs={{0,1},{1,0},{2,3},{3,2},{4,5},{5,4},{6,7},{7,6},{8,9},{9,8},{10,11... | collective-permute-start | bytes 1736 | tf_op jit(solution)/shard_map/ppermute | solution.py:312
  64.3 1.9 %collective-permute-start.11 = (f32[8,144]{1,0:T(8,128)S(1)}, f32[8,144]{1,0:T(8,128)S(1)}, u32[]{:S(2)}, u32[]{:S(2)}) collective-permute-start(f32[8,144]{1,0:T(8,128)S(1)} %get-tuple-element.36), channel_id=1, source_target_pairs={{0,509},{1,4},{4,1},{5,8},{8,5},{9,12},{12,9},{13,16},{16,13},{17,... | collective-permute-start | bytes 13832 | tf_op jit(solution)/shard_map/ppermute | solution.py:312
  66.2 0.0 collective-permute-done.10.mate_row
  66.2 1.9 %collective-permute-start.12 = (f32[2,144]{1,0:T(2,128)S(1)}, f32[2,144]{1,0:T(2,128)S(1)}, u32[]{:S(2)}, u32[]{:S(2)}) collective-permute-start(f32[2,144]{1,0:T(2,128)S(1)} %pad_maximum_fusion), channel_id=1, source_target_pairs={{0,2},{1,3},{2,0},{3,1},{4,6},{5,7},{6,4},{7,5},{8,10},{9,11},{10,... | collective-permute-start | bytes 3464 | tf_op jit(solution)/shard_map/ppermute | solution.py:312
  68.1 0.7 collective-permute-start.14
  68.8 15.5 %collective-permute-start.13 = (f32[2,144]{1,0:T(2,128)S(1)}, f32[2,144]{1,0:T(2,128)S(1)}, u32[]{:S(2)}, u32[]{:S(2)}) collective-permute-start(f32[2,144]{1,0:T(2,128)S(1)} %pad_maximum_fusion), channel_id=1, source_target_pairs={{0,510},{1,511},{2,4},{3,5},{4,2},{5,3},{6,8},{7,9},{8,6},{9,7},{1... | collective-permute-start | bytes 3464 | tf_op jit(solution)/shard_map/ppermute | solution.py:312
  84.3 0.0 collective-permute-done.12.near_rows
  84.3 0.0 collective-permute-done.11.even_row
  84.3 0.0 copy-done.1
  84.3 0.0 copy-start.2
  84.3 0.0 copy-start.3
  84.4 0.0 copy-start.4
  84.4 1.3 %part_gradients.1 = (f32[144,3584]{1,0:T(8,128)S(1)}, f32[144,144]{1,0:T(8,128)S(1)}, f32[1,144]{1,0:T(1,128)S(1)}) custom-call(f32[144,144]{1,0:T(8,128)S(1)} %fusion.partner_ref, f32[1,144]{1,0:T(1,128)S(1)} %get-tuple-element.35.own_row, f32[1,144]{1,0:T(1,128)S(1)} %collective-permute-done.10.mate_row, f32[8,144]{1,0:T(8,128)S(1)} %collective-permute-done.11.even_row, ...), custom_call_target="tpu_custom_call" | custom-call | flops 594542592 | bytes 6193152 | tf_op jit(solution)/shard_map/part_gradients/pallas_call | solution.py:218
  85.6 0.0 collective-permute-done.14.odd_row
  85.6 0.0 collective-permute-done.13.next_rows
  85.7 2.1 %gradients.1 = (f32[72,3584]{1,0:T(8,128)}, f32[72,3584]{1,0:T(8,128)}) custom-call(f32[144,3584]{1,0:T(8,128)S(1)} %get-tuple-element.39.sum_ref, f32[144,144]{1,0:T(8,128)S(1)} %get-tuple-element.40.along_ref, f32[144,1]{1,0:T(8,128)S(1)} %copy-done.4, f32[1,144]{1,0:T(1,128)S(1)} %get-tuple-element.35.own_row, ...), custom_call_target="tpu_custom_call" | custom-call | flops 445906944 | bytes 8257536 | tf_op jit(solution)/shard_map/gradients/pallas_call | solution.py:281
  (4 shorter events, 0.0 us)
Async XLA Ops:
  3.6 23.9 %collective-permute-start = (bf16[144,3584]{1,0:T(8,128)(2,1)}, bf16[144,3584]{1,0:T(8,128)(2,1)S(1)}, u32[]{:S(2)}, u32[]{:S(2)}) collective-permute-start(bf16[144,3584]{1,0:T(8,128)(2,1)} %get-tuple-element.25.own_ref), channel_id=1, source_target_pairs={{0,2},{1,3},{2,0},{3,1},{4,6},{5,7},{6,4},{7,5},{8,10},{9,11},{10,... | collective-permute-start | bytes 3096584 | tf_op jit(solution)/shard_map/ppermute | solution.py:312
  8.4 25.3 %collective-permute-start.4 = (bf16[144,1792]{1,0:T(8,128)(2,1)}, bf16[144,1792]{1,0:T(8,128)(2,1)S(1)}, u32[]{:S(2)}, u32[]{:S(2)}) collective-permute-start(bf16[144,1792]{1,0:T(8,128)(2,1)} %get-tuple-element.27), channel_id=1, source_target_pairs={{0,510},{1,511},{2,4},{3,5},{4,2},{5,3},{6,8},{7,9},{8,6},{9,7},{1... | collective-permute-start | bytes 1548296 | tf_op jit(solution)/shard_map/ppermute | solution.py:312
  22.4 33.6 %collective-permute-start.6 = (bf16[144,3584]{1,0:T(8,128)(2,1)}, bf16[144,3584]{1,0:T(8,128)(2,1)S(1)}, u32[]{:S(2)}, u32[]{:S(2)}) collective-permute-start(bf16[144,3584]{1,0:T(8,128)(2,1)} %get-tuple-element.25.own_ref), channel_id=1, source_target_pairs={{0,1},{1,0},{2,3},{3,2},{4,5},{5,4},{6,7},{7,6},{8,9},{9,8},{10,11... | collective-permute-start | bytes 3096584 | tf_op jit(solution)/shard_map/ppermute | solution.py:312
  25.5 24.3 %collective-permute-start.2 = (bf16[144,1792]{1,0:T(8,128)(2,1)}, bf16[144,1792]{1,0:T(8,128)(2,1)S(1)}, u32[]{:S(2)}, u32[]{:S(2)}) collective-permute-start(bf16[144,1792]{1,0:T(8,128)(2,1)} %get-tuple-element.26), channel_id=1, source_target_pairs={{0,510},{1,511},{2,4},{3,5},{4,2},{5,3},{6,8},{7,9},{8,6},{9,7},{1... | collective-permute-start | bytes 1548296 | tf_op jit(solution)/shard_map/ppermute | solution.py:312
  27.4 33.1 %collective-permute-start.1 = (bf16[144,3584]{1,0:T(8,128)(2,1)S(1)}, bf16[144,3584]{1,0:T(8,128)(2,1)S(1)}, u32[]{:S(2)}, u32[]{:S(2)}) collective-permute-start(bf16[144,3584]{1,0:T(8,128)(2,1)S(1)} %collective-permute-done.near_ref), channel_id=1, source_target_pairs={{0,511},{3,4},{4,3},{7,8},{8,7},{11,12},{12,11},{15,16},{16,15},{1... | collective-permute-start | bytes 3096584 | tf_op jit(solution)/shard_map/ppermute | solution.py:312
  33.7 20.3 %collective-permute-start.5 = (bf16[144,1792]{1,0:T(8,128)(2,1)S(1)}, bf16[144,1792]{1,0:T(8,128)(2,1)S(1)}, u32[]{:S(2)}, u32[]{:S(2)}) collective-permute-start(bf16[144,1792]{1,0:T(8,128)(2,1)S(1)} %collective-permute-done.4.next_first.next_0), channel_id=1, source_target_pairs={{1,2},{2,1},{5,6},{6,5},{9,10},{10,9},{13,14},{14,13},{17,18},{18,... | collective-permute-start | bytes 1548296 | tf_op jit(solution)/shard_map/ppermute | solution.py:312
  36.3 24.7 %collective-permute-start.7 = (bf16[144,3584]{1,0:T(8,128)(2,1)S(1)}, bf16[144,3584]{1,0:T(8,128)(2,1)S(1)}, u32[]{:S(2)}, u32[]{:S(2)}) collective-permute-start(bf16[144,3584]{1,0:T(8,128)(2,1)S(1)} %collective-permute-done.near_ref), channel_id=1, source_target_pairs={{0,1},{1,0},{2,3},{3,2},{4,5},{5,4},{6,7},{7,6},{8,9},{9,8},{10,11... | collective-permute-start | bytes 3096584 | tf_op jit(solution)/shard_map/ppermute | solution.py:312
  49.8 10.4 %collective-permute-start.3 = (bf16[144,1792]{1,0:T(8,128)(2,1)S(1)}, bf16[144,1792]{1,0:T(8,128)(2,1)S(1)}, u32[]{:S(2)}, u32[]{:S(2)}) collective-permute-start(bf16[144,1792]{1,0:T(8,128)(2,1)S(1)} %collective-permute-done.2.next_second.next_1), channel_id=1, source_target_pairs={{1,2},{2,1},{5,6},{6,5},{9,10},{10,9},{13,14},{14,13},{17,18},{18,... | collective-permute-start | bytes 1548296 | tf_op jit(solution)/shard_map/ppermute | solution.py:312
  51.8 1.2 %copy-start = (bf16[144,3584]{1,0:T(8,128)(2,1)S(1)}, bf16[144,3584]{1,0:T(8,128)(2,1)}, u32[]{:S(2)}) copy-start(bf16[144,3584]{1,0:T(8,128)(2,1)} %get-tuple-element.25.own_ref) | copy-start | bytes 3096580
  54.0 6.9 %collective-permute-start.9 = (bf16[144,1792]{1,0:T(8,128)(2,1)S(1)}, bf16[144,1792]{1,0:T(8,128)(2,1)S(1)}, u32[]{:S(2)}, u32[]{:S(2)}) collective-permute-start(bf16[144,1792]{1,0:T(8,128)(2,1)S(1)} %collective-permute-done.2.next_second.next_1), channel_id=1, source_target_pairs={{0,1},{1,0},{2,3},{3,2},{4,5},{5,4},{6,7},{7,6},{8,9},{9,8},{10,11... | collective-permute-start | bytes 1548296 | tf_op jit(solution)/shard_map/ppermute | solution.py:312
  56.0 5.0 %collective-permute-start.8 = (bf16[144,1792]{1,0:T(8,128)(2,1)S(1)}, bf16[144,1792]{1,0:T(8,128)(2,1)S(1)}, u32[]{:S(2)}, u32[]{:S(2)}) collective-permute-start(bf16[144,1792]{1,0:T(8,128)(2,1)S(1)} %get-tuple-element.33), channel_id=1, source_target_pairs={{0,1},{1,0},{2,3},{3,2},{4,5},{5,4},{6,7},{7,6},{8,9},{9,8},{10,11... | collective-permute-start | bytes 1548296 | tf_op jit(solution)/shard_map/ppermute | solution.py:312
  61.0 23.4 %copy-start.1 = (bf16[144,3584]{1,0:T(8,128)(2,1)S(1)}, bf16[144,3584]{1,0:T(8,128)(2,1)}, u32[]{:S(2)}) copy-start(bf16[144,3584]{1,0:T(8,128)(2,1)} %get-tuple-element.25.own_ref) | copy-start | bytes 3096580
  62.3 3.8 %collective-permute-start.10 = (f32[1,144]{1,0:T(1,128)S(1)}, f32[1,144]{1,0:T(1,128)S(1)}, u32[]{:S(2)}, u32[]{:S(2)}) collective-permute-start(f32[1,144]{1,0:T(1,128)S(1)} %get-tuple-element.35.own_row), channel_id=1, source_target_pairs={{0,1},{1,0},{2,3},{3,2},{4,5},{5,4},{6,7},{7,6},{8,9},{9,8},{10,11... | collective-permute-start | bytes 1736 | tf_op jit(solution)/shard_map/ppermute | solution.py:312
  64.3 20.0 %collective-permute-start.11 = (f32[8,144]{1,0:T(8,128)S(1)}, f32[8,144]{1,0:T(8,128)S(1)}, u32[]{:S(2)}, u32[]{:S(2)}) collective-permute-start(f32[8,144]{1,0:T(8,128)S(1)} %get-tuple-element.36), channel_id=1, source_target_pairs={{0,509},{1,4},{4,1},{5,8},{8,5},{9,12},{12,9},{13,16},{16,13},{17,... | collective-permute-start | bytes 13832 | tf_op jit(solution)/shard_map/ppermute | solution.py:312
  66.2 18.1 %collective-permute-start.12 = (f32[2,144]{1,0:T(2,128)S(1)}, f32[2,144]{1,0:T(2,128)S(1)}, u32[]{:S(2)}, u32[]{:S(2)}) collective-permute-start(f32[2,144]{1,0:T(2,128)S(1)} %pad_maximum_fusion), channel_id=1, source_target_pairs={{0,2},{1,3},{2,0},{3,1},{4,6},{5,7},{6,4},{7,5},{8,10},{9,11},{10,... | collective-permute-start | bytes 3464 | tf_op jit(solution)/shard_map/ppermute | solution.py:312
  68.1 17.5 %collective-permute-start.14 = (f32[1,144]{1,0:T(1,128)S(1)}, f32[1,144]{1,0:T(1,128)S(1)}, u32[]{:S(2)}, u32[]{:S(2)}) collective-permute-start(f32[1,144]{1,0:T(1,128)S(1)} %get-tuple-element.35.own_row), channel_id=1, source_target_pairs={{2,511},{3,6},{6,3},{7,10},{10,7},{11,14},{14,11},{15,18},{18,15},... | collective-permute-start | bytes 1736 | tf_op jit(solution)/shard_map/ppermute | solution.py:312
  68.8 16.8 %collective-permute-start.13 = (f32[2,144]{1,0:T(2,128)S(1)}, f32[2,144]{1,0:T(2,128)S(1)}, u32[]{:S(2)}, u32[]{:S(2)}) collective-permute-start(f32[2,144]{1,0:T(2,128)S(1)} %pad_maximum_fusion), channel_id=1, source_target_pairs={{0,510},{1,511},{2,4},{3,5},{4,2},{5,3},{6,8},{7,9},{8,6},{9,7},{1... | collective-permute-start | bytes 3464 | tf_op jit(solution)/shard_map/ppermute | solution.py:312
  84.3 1.3 %copy-start.2 = (bf16[72,3584]{1,0:T(8,128)(2,1)S(1)}, bf16[72,3584]{1,0:T(8,128)(2,1)}, u32[]{:S(2)}) copy-start(bf16[72,3584]{1,0:T(8,128)(2,1)} %query_ref.1) | copy-start | bytes 1548292
  84.3 1.3 %copy-start.3 = (bf16[72,3584]{1,0:T(8,128)(2,1)S(1)}, bf16[72,3584]{1,0:T(8,128)(2,1)}, u32[]{:S(2)}) copy-start(bf16[72,3584]{1,0:T(8,128)(2,1)} %passage_ref.1) | copy-start | bytes 1548292
  84.4 1.3 %copy-start.4 = (f32[144,1]{1,0:T(8,128)S(1)}, f32[144,1]{1,0:T(8,128)}, u32[]{:S(2)}) copy-start(f32[144,1]{1,0:T(8,128)} %get-tuple-element.41.scale_ref) | copy-start | bytes 1732

commit v8 on v5

--- a/solution.py
+++ b/solution.py
@@ -10,6 +10,7 @@
 INV_TEMP = 20.0
 EPS = 1e-06
 TILE = 896
+SPREAD = 8
 VMEM = pl.BlockSpec(memory_space=pltpu.VMEM)
 HBM = pl.BlockSpec(memory_space=pl.ANY)
 
@@ -146,7 +147,7 @@
 
 def total_kernel(
     far_score_ref, mass_ref, score_ref, partner_ref, own_ref, own_mate_score, near_mate_ref, mate_first, mate_second,
-    near_mate_out, next_mate_out, recip_ref, loss_ref,
+    near_mate_out, next_mate_out, recip_ref, spread_ref, loss_ref,
 ):
     partner = partner_ref[...]
     own = own_ref[...]
@@ -162,6 +163,7 @@
     eye = eye_of(partner.shape[0])
     norm_row = jnp.sum((eye + partner) * total_col, axis=0, keepdims=True)
     recip_ref[...] = 1.0 / norm_row
+    spread_ref[...] = jnp.broadcast_to(1.0 / norm_row, spread_ref.shape)
     positive = jnp.sum(partner * score_ref[...], axis=0, keepdims=True)
     losses = jnp.log(norm_row) + INV_TEMP - INV_TEMP * positive
     loss_ref[...] = losses[:, : loss_ref.shape[1]]
@@ -178,8 +180,8 @@
 
 
 def part_kernel(
-    partner_ref, own_row, mate_row, next_rows, own_score, mate_score, next_score, next_mate_score,
-    own_ref, mate_ref, next_0, next_1, pair_0, pair_1, sum_ref, along_ref,
+    partner_ref, own_row, mate_row, even_row, next_rows, own_score, mate_score, next_score, next_mate_score,
+    own_ref, mate_ref, next_0, next_1, pair_0, pair_1, sum_ref, along_ref, passed_ref,
 ):
     partner = partner_ref[...]
     count = partner.shape[0]
@@ -200,6 +202,7 @@
         weights.append(low)
         along = along + share
     along_ref[...] = along
+    passed_ref[...] = even_row[0:1, :]
     weights = jnp.concatenate(weights, axis=1)
     half = next_0.shape[1]
     for start in range(0, own_ref.shape[1], TILE):
@@ -223,10 +226,11 @@
     return pl.pallas_call(
         part_kernel,
         in_specs=[VMEM] * len(operands),
-        out_specs=(VMEM, VMEM),
+        out_specs=(VMEM, VMEM, VMEM),
         out_shape=(
             jax.ShapeDtypeStruct((count, width), jnp.float32),
             jax.ShapeDtypeStruct((count, count), jnp.float32),
+            jax.ShapeDtypeStruct((1, count), jnp.float32),
         ),
         compiler_params=pltpu.CompilerParams(vmem_limit_bytes=24 * 2**20),
         cost_estimate=pl.CostEstimate(
@@ -239,7 +243,7 @@
 
 
 def gradient_kernel(
-    sum_ref, along_ref, scale_ref, own_row, near_rows, far_row, near_score, pair_score, far_score,
+    sum_ref, along_ref, scale_ref, own_row, near_rows, even_row, odd_row, near_score, pair_score, far_score,
     near_ref, pair_ref, far_first, far_0, far_1, query_ref, passage_ref,
     query_out, passage_out, query_hold, passage_hold, sems,
 ):
@@ -248,7 +252,7 @@
     recip_col = column_of(own_row[...])
     near_low, near_share = weigh(near_score[...], recip_col, near_rows[0:1, :])
     pair_low, pair_share = weigh(pair_score[...], recip_col, near_rows[1:2, :])
-    far_low, far_share = weigh(far_score[...], recip_col, far_row[...])
+    far_low, far_share = weigh(far_score[...], recip_col, even_row[...] + odd_row[...])
     along = along_ref[...] + near_share + pair_share + far_share
     along = INV_TEMP * jnp.sum(along, axis=1, keepdims=True)
     weights = jnp.concatenate([near_low, pair_low, far_low], axis=1)
@@ -329,8 +333,8 @@
     def far_over_near(chip, core):
         return (chip + 1 if core else chip - 1, 1 - core) if chip % 2 != core else None
 
-    def chip_beyond(chip, core):
-        return (chip + 2 if core else chip - 2, 1 - core)
+    def beyond_of(parity, chip, core):
+        return (chip + 2 if core else chip - 2, 1 - core) if chip % 2 == parity else None
 
     own, first, second, scale = unit_rows(query_raw, passage_raw)
     paired = (pairing[0][:, None] == jnp.arange(rows, dtype=jnp.int32)[None, :]).astype(jnp.float32)
@@ -355,15 +359,15 @@
         [next_halves[0]],
     )
     next_mate = [swapped(half, other_core) for half in (passed, next_halves[1])]
+    far_score = far_scores(own, far_second[0], far_score, 0)
     far_score, mate_score = side_scores(own, mate, far_score, 0)
-    far_score = far_scores(own, far_second[0], far_score, 0)
     far_score = far_scores(own, far_second[1], far_score, 1)
     far_score = far_scores(own, far_first, far_score, 0)
-    near_mate_score, next_mate_score, recip, losses = score_call(
+    near_mate_score, next_mate_score, recip, spread, losses = score_call(
         total_kernel,
         "totals",
         count,
-        [square, square, (1, count), (1, rows)],
+        [square, square, (1, count), (SPREAD, count), (1, rows)],
         [far_score, mass, scores[0], partner, own, mate_score, near_mate, *next_mate],
     )
 
@@ -371,12 +375,13 @@
     chip_rows = jnp.concatenate([recip, mate_row], axis=0)
     near_rows = swapped(chip_rows, near_chip)
     next_rows = swapped(chip_rows, next_chip)
-    far_row = swapped(recip, chip_beyond)
+    even_row = swapped(spread, functools.partial(beyond_of, 0))
+    odd_row = swapped(recip, functools.partial(beyond_of, 1))
 
     near_score, next_score = scores[1:]
-    part_sum, along = part_gradients(
+    part_sum, along, even_row = part_gradients(
         partner,
-        [recip, mate_row, next_rows],
+        [recip, mate_row, even_row, next_rows],
         [scores[0], mate_score, next_score, next_mate_score],
         [own, mate, *next_halves, *next_mate],
     )
@@ -384,7 +389,7 @@
         part_sum,
         along,
         scale,
-        [recip, near_rows, far_row],
+        [recip, near_rows, even_row, odd_row],
         [near_score, near_mate_score, far_score],
         [near, near_mate, far_first, *far_second],
         query_raw,

time: 83.2 us -> 83 us (level)
  the two profiles are of different devices: /device:TPU:1 before, /device:TPU:64 now
where the time goes in v8:
time: 83 us; the launch traced here: 82.5 us
  starting transfers between devices  55 us (66%)
  waiting for transfers between devices  14.3 us (17%)
  Pallas kernels  10.1 us (12%)
  local copies, waits for them, and re-layouts  1.24 us (1%)
  between operations  0.95 us (1%)
  other arithmetic  0.91 us (1%)
    ppermute x15, starting transfers between devices, swapped(): return lax.ppermute(value, 'dp', pairs)  55 us
    ppermute x15, waiting for transfers between devices, swapped(): return lax.ppermute(value, 'dp', pairs)  14.3 us
    pallas_call x6, Pallas kernels, score_call(): pl.pallas_call(body, in_specs=[VMEM] * len(operands), out_specs=[VMEM] *...  3.81 us
    pallas_call x1, Pallas kernels, unit_rows(): pl.pallas_call(unit_kernel, in_specs=[HBM, HBM], out_specs=(VMEM, VMEM, V...  2.93 us
    pallas_call x1, Pallas kernels, gradients(): pl.pallas_call(gradient_kernel, in_specs=[VMEM] * len(operands), out_spec...  2.07 us
  transfers between devices with their start and end apart: 15, of which 4 were waited for; matrix products, arithmetic and copies ran while one was open for 1% of the time, Pallas kernels for 5%

profile of v8, /device:TPU:64, one launch (start us, length us, event | category | flops | bytes accessed | tf_op | source)
XLA Modules:
  0.0 82.5 jit_solution(14829721894719638677)
XLA Ops:
  0.6 2.9 %unit_rows.1 = (bf16[144,3584]{1,0:T(8,128)(2,1)}, bf16[144,1792]{1,0:T(8,128)(2,1)}, bf16[144,1792]{1,0:T(8,128)(2,1)}, f32[144,1]{1,0:T(8,128)}) custom-call(bf16[72,3584]{1,0:T(8,128)(2,1)} %query_ref.1, bf16[72,3584]{1,0:T(8,128)(2,1)} %passage_ref.1), custom_call_target="tpu_custom_call" | custom-call | flops 1548288 | bytes 2064384 | tf_op jit(solution)/shard_map/unit_rows/pallas_call | solution.py:61
  3.6 6.9 %collective-permute-start = (bf16[144,3584]{1,0:T(8,128)(2,1)}, bf16[144,3584]{1,0:T(8,128)(2,1)S(1)}, u32[]{:S(2)}, u32[]{:S(2)}) collective-permute-start(bf16[144,3584]{1,0:T(8,128)(2,1)} %get-tuple-element.25.own_ref), channel_id=1, source_target_pairs={{0,2},{1,3},{2,0},{3,1},{4,6},{5,7},{6,4},{7,5},{8,10},{9,11},{10,... | collective-permute-start | bytes 3096584 | tf_op jit(solution)/shard_map/ppermute | solution.py:319
  10.5 1.9 %collective-permute-start.4 = (bf16[144,1792]{1,0:T(8,128)(2,1)}, bf16[144,1792]{1,0:T(8,128)(2,1)S(1)}, u32[]{:S(2)}, u32[]{:S(2)}) collective-permute-start(bf16[144,1792]{1,0:T(8,128)(2,1)} %get-tuple-element.27), channel_id=1, source_target_pairs={{0,510},{1,511},{2,4},{3,5},{4,2},{5,3},{6,8},{7,9},{8,6},{9,7},{1... | collective-permute-start | bytes 1548296 | tf_op jit(solution)/shard_map/ppermute | solution.py:319
  12.4 1.9 %collective-permute-start.6 = (bf16[144,3584]{1,0:T(8,128)(2,1)}, bf16[144,3584]{1,0:T(8,128)(2,1)S(1)}, u32[]{:S(2)}, u32[]{:S(2)}) collective-permute-start(bf16[144,3584]{1,0:T(8,128)(2,1)} %get-tuple-element.25.own_ref), channel_id=1, source_target_pairs={{0,1},{1,0},{2,3},{3,2},{4,5},{5,4},{6,7},{7,6},{8,9},{9,8},{10,11... | collective-permute-start | bytes 3096584 | tf_op jit(solution)/shard_map/ppermute | solution.py:319
  14.4 3.9 %collective-permute-start.2 = (bf16[144,1792]{1,0:T(8,128)(2,1)}, bf16[144,1792]{1,0:T(8,128)(2,1)S(1)}, u32[]{:S(2)}, u32[]{:S(2)}) collective-permute-start(bf16[144,1792]{1,0:T(8,128)(2,1)} %get-tuple-element.26), channel_id=1, source_target_pairs={{0,510},{1,511},{2,4},{3,5},{4,2},{5,3},{6,8},{7,9},{8,6},{9,7},{1... | collective-permute-start | bytes 1548296 | tf_op jit(solution)/shard_map/ppermute | solution.py:319
  18.3 11.9 %collective-permute-done.near_ref = bf16[144,3584]{1,0:T(8,128)(2,1)S(1)} collective-permute-done((bf16[144,3584]{1,0:T(8,128)(2,1)}, bf16[144,3584]{1,0:T(8,128)(2,1)S(1)}, u32[]{:S(2)}, u32[]{:S(2)}) %collective-permute-start) | collective-permute-done | bytes 1032224 | tf_op jit(solution)/shard_map/ppermute | solution.py:319
  30.2 0.7 collective-permute-start.1
  30.9 0.0 collective-permute-done.4.next_first.next_0
  31.0 2.9 %collective-permute-start.5 = (bf16[144,1792]{1,0:T(8,128)(2,1)S(1)}, bf16[144,1792]{1,0:T(8,128)(2,1)S(1)}, u32[]{:S(2)}, u32[]{:S(2)}) collective-permute-start(bf16[144,1792]{1,0:T(8,128)(2,1)S(1)} %collective-permute-done.4.next_first.next_0), channel_id=1, source_target_pairs={{1,2},{2,1},{5,6},{6,5},{9,10},{10,9},{13,14},{14,13},{17,18},{18,... | collective-permute-start | bytes 1548296 | tf_op jit(solution)/shard_map/ppermute | solution.py:319
  33.9 4.0 %collective-permute-start.7 = (bf16[144,3584]{1,0:T(8,128)(2,1)S(1)}, bf16[144,3584]{1,0:T(8,128)(2,1)S(1)}, u32[]{:S(2)}, u32[]{:S(2)}) collective-permute-start(bf16[144,3584]{1,0:T(8,128)(2,1)S(1)} %collective-permute-done.near_ref), channel_id=1, source_target_pairs={{0,1},{1,0},{2,3},{3,2},{4,5},{5,4},{6,7},{7,6},{8,9},{9,8},{10,11... | collective-permute-start | bytes 3096584 | tf_op jit(solution)/shard_map/ppermute | solution.py:319
  37.9 0.8 iota_compare_fusion.1
  38.7 0.0 collective-permute-done.2.next_second.next_1
  38.7 11.3 %collective-permute-start.3 = (bf16[144,1792]{1,0:T(8,128)(2,1)S(1)}, bf16[144,1792]{1,0:T(8,128)(2,1)S(1)}, u32[]{:S(2)}, u32[]{:S(2)}) collective-permute-start(bf16[144,1792]{1,0:T(8,128)(2,1)S(1)} %collective-permute-done.2.next_second.next_1), channel_id=1, source_target_pairs={{1,2},{2,1},{5,6},{6,5},{9,10},{10,9},{13,14},{14,13},{17,18},{18,... | collective-permute-start | bytes 1548296 | tf_op jit(solution)/shard_map/ppermute | solution.py:319
  50.0 0.1 fusion.partner_ref
  50.1 0.0 copy-start
  50.1 1.2 %copy-done = bf16[144,3584]{1,0:T(8,128)(2,1)S(1)} copy-done((bf16[144,3584]{1,0:T(8,128)(2,1)S(1)}, bf16[144,3584]{1,0:T(8,128)(2,1)}, u32[]{:S(2)}) %copy-start) | copy-done | bytes 1032216
  51.3 1.0 %early_scores.1 = (f32[144,144]{1,0:T(8,128)S(1)}, f32[144,144]{1,0:T(8,128)S(1)}, f32[144,144]{1,0:T(8,128)S(1)}, f32[144,144]{1,0:T(8,128)S(1)}, f32[144,144]{...) custom-call(f32[144,144]{1,0:T(8,128)S(1)} %fusion.partner_ref, bf16[144,3584]{1,0:T(8,128)(2,1)S(1)} %copy-done, ...), custom_call_target="tpu_custom_call" | custom-call | flops 451878912 | bytes 3138048 | tf_op jit(solution)/shard_map/early_scores/pallas_call | solution.py:81
  52.3 0.0 collective-permute-done.5.far_ref.far_0
  52.3 1.9 %collective-permute-start.9 = (bf16[144,1792]{1,0:T(8,128)(2,1)S(1)}, bf16[144,1792]{1,0:T(8,128)(2,1)S(1)}, u32[]{:S(2)}, u32[]{:S(2)}) collective-permute-start(bf16[144,1792]{1,0:T(8,128)(2,1)S(1)} %collective-permute-done.2.next_second.next_1), channel_id=1, source_target_pairs={{0,1},{1,0},{2,3},{3,2},{4,5},{5,4},{6,7},{7,6},{8,9},{9,8},{10,11... | collective-permute-start | bytes 1548296 | tf_op jit(solution)/shard_map/ppermute | solution.py:319
  54.2 0.0 collective-permute-done.6.key_ref.mate_ref
  54.2 2.4 %collective-permute-start.8 = (bf16[144,1792]{1,0:T(8,128)(2,1)S(1)}, bf16[144,1792]{1,0:T(8,128)(2,1)S(1)}, u32[]{:S(2)}, u32[]{:S(2)}) collective-permute-start(bf16[144,1792]{1,0:T(8,128)(2,1)S(1)} %get-tuple-element.33), channel_id=1, source_target_pairs={{0,1},{1,0},{2,3},{3,2},{4,5},{5,4},{6,7},{7,6},{8,9},{9,8},{10,11... | collective-permute-start | bytes 1548296 | tf_op jit(solution)/shard_map/ppermute | solution.py:319
  56.6 0.3 far_scores.3.sum_ref
  57.0 0.4 side_scores.1
  57.4 0.0 collective-permute-done.3.far_ref.far_1
  57.4 0.3 far_scores.4.sum_ref
  57.7 0.0 collective-permute-done.1.far_ref.far_first
  57.7 0.4 far_scores.5.far_score_ref.far_score
  58.2 0.0 copy-start.1
  58.2 0.0 collective-permute-done.9.mate_second.pair_1
  58.2 0.0 collective-permute-done.8.mate_first.pair_0
  58.2 0.0 collective-permute-done.7.near_mate_ref.pair_ref
  58.2 1.3 %totals.1 = (f32[144,144]{1,0:T(8,128)S(1)}, f32[144,144]{1,0:T(8,128)S(1)}, f32[1,144]{1,0:T(1,128)S(1)}, f32[8,144]{1,0:T(8,128)S(1)}, f32[1,72]{1,0:T(1,128)}) custom-call(f32[144,144]{1,0:T(8,128)S(1)} %far_scores.5.far_score_ref.far_score, f32[144,144]{1,0:T(8,128)S(1)} %get-tuple-element.30.mass_ref, ...), custom_call_target="tpu_custom_call" | custom-call | flops 475766784 | bytes 3303936 | tf_op jit(solution)/shard_map/totals/pallas_call | solution.py:81
  59.6 2.2 %collective-permute-start.10 = (f32[1,144]{1,0:T(1,128)S(1)}, f32[1,144]{1,0:T(1,128)S(1)}, u32[]{:S(2)}, u32[]{:S(2)}) collective-permute-start(f32[1,144]{1,0:T(1,128)S(1)} %get-tuple-element.35.own_row), channel_id=1, source_target_pairs={{0,1},{1,0},{2,3},{3,2},{4,5},{5,4},{6,7},{7,6},{8,9},{9,8},{10,11... | collective-permute-start | bytes 1736 | tf_op jit(solution)/shard_map/ppermute | solution.py:319
  61.8 0.7 collective-permute-start.11
  62.4 0.1 collective-permute-done.10.mate_row
  62.6 5.3 %collective-permute-start.12 = (f32[2,144]{1,0:T(2,128)S(1)}, f32[2,144]{1,0:T(2,128)S(1)}, u32[]{:S(2)}, u32[]{:S(2)}) collective-permute-start(f32[2,144]{1,0:T(2,128)S(1)} %pad_maximum_fusion), channel_id=1, source_target_pairs={{0,510},{1,511},{2,4},{3,5},{4,2},{5,3},{6,8},{7,9},{8,6},{9,7},{1... | collective-permute-start | bytes 3464 | tf_op jit(solution)/shard_map/ppermute | solution.py:319
  67.8 7.1 %collective-permute-start.14 = (f32[1,144]{1,0:T(1,128)S(1)}, f32[1,144]{1,0:T(1,128)S(1)}, u32[]{:S(2)}, u32[]{:S(2)}) collective-permute-start(f32[1,144]{1,0:T(1,128)S(1)} %get-tuple-element.35.own_row), channel_id=1, source_target_pairs={{2,511},{3,6},{6,3},{7,10},{10,7},{11,14},{14,11},{15,18},{18,15},... | collective-permute-start | bytes 1736 | tf_op jit(solution)/shard_map/ppermute | solution.py:319
  74.9 1.9 %collective-permute-start.13 = (f32[2,144]{1,0:T(2,128)S(1)}, f32[2,144]{1,0:T(2,128)S(1)}, u32[]{:S(2)}, u32[]{:S(2)}) collective-permute-start(f32[2,144]{1,0:T(2,128)S(1)} %pad_maximum_fusion), channel_id=1, source_target_pairs={{0,2},{1,3},{2,0},{3,1},{4,6},{5,7},{6,4},{7,5},{8,10},{9,11},{10,... | collective-permute-start | bytes 3464 | tf_op jit(solution)/shard_map/ppermute | solution.py:319
  76.9 0.0 collective-permute-done.12.next_rows
  76.9 0.0 collective-permute-done.11.even_row
  76.9 0.0 copy-done.1
  76.9 0.0 copy-start.2
  76.9 0.0 copy-start.3
  76.9 1.3 %part_gradients.1 = (f32[144,3584]{1,0:T(8,128)S(1)}, f32[144,144]{1,0:T(8,128)S(1)}, f32[1,144]{1,0:T(1,128)S(1)}) custom-call(f32[144,144]{1,0:T(8,128)S(1)} %fusion.partner_ref, f32[1,144]{1,0:T(1,128)S(1)} %get-tuple-element.35.own_row, f32[1,144]{1,0:T(1,128)S(1)} %collective-permute-done.10.mate_row, f32[8,144]{1,0:T(8,128)S(1)} %collective-permute-done.11.even_row, ...), custom_call_target="tpu_custom_call" | custom-call | flops 594542592 | bytes 6193152 | tf_op jit(solution)/shard_map/part_gradients/pallas_call | solution.py:226
  78.2 0.9 %collective-permute-done.14.odd_row = f32[1,144]{1,0:T(1,128)S(1)} collective-permute-done((f32[1,144]{1,0:T(1,128)S(1)}, f32[1,144]{1,0:T(1,128)S(1)}, u32[]{:S(2)}, u32[]{:S(2)}) %collective-permute-start.14) | collective-permute-done | bytes 608 | tf_op jit(solution)/shard_map/ppermute | solution.py:319
  79.1 1.3 %collective-permute-done.13.near_rows = f32[2,144]{1,0:T(2,128)S(1)} collective-permute-done((f32[2,144]{1,0:T(2,128)S(1)}, f32[2,144]{1,0:T(2,128)S(1)}, u32[]{:S(2)}, u32[]{:S(2)}) %collective-permute-start.13) | collective-permute-done | bytes 1184 | tf_op jit(solution)/shard_map/ppermute | solution.py:319
  80.4 0.0 copy-done.2
  80.4 2.1 %gradients.1 = (f32[72,3584]{1,0:T(8,128)}, f32[72,3584]{1,0:T(8,128)}) custom-call(f32[144,3584]{1,0:T(8,128)S(1)} %get-tuple-element.39.sum_ref, f32[144,144]{1,0:T(8,128)S(1)} %get-tuple-element.40.along_ref, f32[144,1]{1,0:T(8,128)S(1)} %copy-done.4, f32[1,144]{1,0:T(1,128)S(1)} %get-tuple-element.35.own_row, ...), custom_call_target="tpu_custom_call" | custom-call | flops 445906944 | bytes 8257536 | tf_op jit(solution)/shard_map/gradients/pallas_call | solution.py:288
  (4 shorter events, 0.0 us)
Async XLA Ops:
  3.6 26.7 %collective-permute-start = (bf16[144,3584]{1,0:T(8,128)(2,1)}, bf16[144,3584]{1,0:T(8,128)(2,1)S(1)}, u32[]{:S(2)}, u32[]{:S(2)}) collective-permute-start(bf16[144,3584]{1,0:T(8,128)(2,1)} %get-tuple-element.25.own_ref), channel_id=1, source_target_pairs={{0,2},{1,3},{2,0},{3,1},{4,6},{5,7},{6,4},{7,5},{8,10},{9,11},{10,... | collective-permute-start | bytes 3096584 | tf_op jit(solution)/shard_map/ppermute | solution.py:319
  10.5 20.4 %collective-permute-start.4 = (bf16[144,1792]{1,0:T(8,128)(2,1)}, bf16[144,1792]{1,0:T(8,128)(2,1)S(1)}, u32[]{:S(2)}, u32[]{:S(2)}) collective-permute-start(bf16[144,1792]{1,0:T(8,128)(2,1)} %get-tuple-element.27), channel_id=1, source_target_pairs={{0,510},{1,511},{2,4},{3,5},{4,2},{5,3},{6,8},{7,9},{8,6},{9,7},{1... | collective-permute-start | bytes 1548296 | tf_op jit(solution)/shard_map/ppermute | solution.py:319
  12.4 41.8 %collective-permute-start.6 = (bf16[144,3584]{1,0:T(8,128)(2,1)}, bf16[144,3584]{1,0:T(8,128)(2,1)S(1)}, u32[]{:S(2)}, u32[]{:S(2)}) collective-permute-start(bf16[144,3584]{1,0:T(8,128)(2,1)} %get-tuple-element.25.own_ref), channel_id=1, source_target_pairs={{0,1},{1,0},{2,3},{3,2},{4,5},{5,4},{6,7},{7,6},{8,9},{9,8},{10,11... | collective-permute-start | bytes 3096584 | tf_op jit(solution)/shard_map/ppermute | solution.py:319
  14.4 24.3 %collective-permute-start.2 = (bf16[144,1792]{1,0:T(8,128)(2,1)}, bf16[144,1792]{1,0:T(8,128)(2,1)S(1)}, u32[]{:S(2)}, u32[]{:S(2)}) collective-permute-start(bf16[144,1792]{1,0:T(8,128)(2,1)} %get-tuple-element.26), channel_id=1, source_target_pairs={{0,510},{1,511},{2,4},{3,5},{4,2},{5,3},{6,8},{7,9},{8,6},{9,7},{1... | collective-permute-start | bytes 1548296 | tf_op jit(solution)/shard_map/ppermute | solution.py:319
  30.2 27.5 %collective-permute-start.1 = (bf16[144,3584]{1,0:T(8,128)(2,1)S(1)}, bf16[144,3584]{1,0:T(8,128)(2,1)S(1)}, u32[]{:S(2)}, u32[]{:S(2)}) collective-permute-start(bf16[144,3584]{1,0:T(8,128)(2,1)S(1)} %collective-permute-done.near_ref), channel_id=1, source_target_pairs={{0,511},{3,4},{4,3},{7,8},{8,7},{11,12},{12,11},{15,16},{16,15},{1... | collective-permute-start | bytes 3096584 | tf_op jit(solution)/shard_map/ppermute | solution.py:319
  31.0 21.3 %collective-permute-start.5 = (bf16[144,1792]{1,0:T(8,128)(2,1)S(1)}, bf16[144,1792]{1,0:T(8,128)(2,1)S(1)}, u32[]{:S(2)}, u32[]{:S(2)}) collective-permute-start(bf16[144,1792]{1,0:T(8,128)(2,1)S(1)} %collective-permute-done.4.next_first.next_0), channel_id=1, source_target_pairs={{1,2},{2,1},{5,6},{6,5},{9,10},{10,9},{13,14},{14,13},{17,18},{18,... | collective-permute-start | bytes 1548296 | tf_op jit(solution)/shard_map/ppermute | solution.py:319
  33.9 24.3 %collective-permute-start.7 = (bf16[144,3584]{1,0:T(8,128)(2,1)S(1)}, bf16[144,3584]{1,0:T(8,128)(2,1)S(1)}, u32[]{:S(2)}, u32[]{:S(2)}) collective-permute-start(bf16[144,3584]{1,0:T(8,128)(2,1)S(1)} %collective-permute-done.near_ref), channel_id=1, source_target_pairs={{0,1},{1,0},{2,3},{3,2},{4,5},{5,4},{6,7},{7,6},{8,9},{9,8},{10,11... | collective-permute-start | bytes 3096584 | tf_op jit(solution)/shard_map/ppermute | solution.py:319
  38.7 18.7 %collective-permute-start.3 = (bf16[144,1792]{1,0:T(8,128)(2,1)S(1)}, bf16[144,1792]{1,0:T(8,128)(2,1)S(1)}, u32[]{:S(2)}, u32[]{:S(2)}) collective-permute-start(bf16[144,1792]{1,0:T(8,128)(2,1)S(1)} %collective-permute-done.2.next_second.next_1), channel_id=1, source_target_pairs={{1,2},{2,1},{5,6},{6,5},{9,10},{10,9},{13,14},{14,13},{17,18},{18,... | collective-permute-start | bytes 1548296 | tf_op jit(solution)/shard_map/ppermute | solution.py:319
  50.1 1.2 %copy-start = (bf16[144,3584]{1,0:T(8,128)(2,1)S(1)}, bf16[144,3584]{1,0:T(8,128)(2,1)}, u32[]{:S(2)}) copy-start(bf16[144,3584]{1,0:T(8,128)(2,1)} %get-tuple-element.25.own_ref) | copy-start | bytes 3096580
  52.3 5.9 %collective-permute-start.9 = (bf16[144,1792]{1,0:T(8,128)(2,1)S(1)}, bf16[144,1792]{1,0:T(8,128)(2,1)S(1)}, u32[]{:S(2)}, u32[]{:S(2)}) collective-permute-start(bf16[144,1792]{1,0:T(8,128)(2,1)S(1)} %collective-permute-done.2.next_second.next_1), channel_id=1, source_target_pairs={{0,1},{1,0},{2,3},{3,2},{4,5},{5,4},{6,7},{7,6},{8,9},{9,8},{10,11... | collective-permute-start | bytes 1548296 | tf_op jit(solution)/shard_map/ppermute | solution.py:319
  54.2 4.0 %collective-permute-start.8 = (bf16[144,1792]{1,0:T(8,128)(2,1)S(1)}, bf16[144,1792]{1,0:T(8,128)(2,1)S(1)}, u32[]{:S(2)}, u32[]{:S(2)}) collective-permute-start(bf16[144,1792]{1,0:T(8,128)(2,1)S(1)} %get-tuple-element.33), channel_id=1, source_target_pairs={{0,1},{1,0},{2,3},{3,2},{4,5},{5,4},{6,7},{7,6},{8,9},{9,8},{10,11... | collective-permute-start | bytes 1548296 | tf_op jit(solution)/shard_map/ppermute | solution.py:319
  58.2 18.7 %copy-start.1 = (bf16[144,3584]{1,0:T(8,128)(2,1)S(1)}, bf16[144,3584]{1,0:T(8,128)(2,1)}, u32[]{:S(2)}) copy-start(bf16[144,3584]{1,0:T(8,128)(2,1)} %get-tuple-element.25.own_ref) | copy-start | bytes 3096580
  59.6 3.0 %collective-permute-start.10 = (f32[1,144]{1,0:T(1,128)S(1)}, f32[1,144]{1,0:T(1,128)S(1)}, u32[]{:S(2)}, u32[]{:S(2)}) collective-permute-start(f32[1,144]{1,0:T(1,128)S(1)} %get-tuple-element.35.own_row), channel_id=1, source_target_pairs={{0,1},{1,0},{2,3},{3,2},{4,5},{5,4},{6,7},{7,6},{8,9},{9,8},{10,11... | collective-permute-start | bytes 1736 | tf_op jit(solution)/shard_map/ppermute | solution.py:319
  61.8 15.1 %collective-permute-start.11 = (f32[8,144]{1,0:T(8,128)S(1)}, f32[8,144]{1,0:T(8,128)S(1)}, u32[]{:S(2)}, u32[]{:S(2)}) collective-permute-start(f32[8,144]{1,0:T(8,128)S(1)} %get-tuple-element.36), channel_id=1, source_target_pairs={{0,509},{1,4},{4,1},{5,8},{8,5},{9,12},{12,9},{13,16},{16,13},{17,... | collective-permute-start | bytes 13832 | tf_op jit(solution)/shard_map/ppermute | solution.py:319
  62.6 14.3 %collective-permute-start.12 = (f32[2,144]{1,0:T(2,128)S(1)}, f32[2,144]{1,0:T(2,128)S(1)}, u32[]{:S(2)}, u32[]{:S(2)}) collective-permute-start(f32[2,144]{1,0:T(2,128)S(1)} %pad_maximum_fusion), channel_id=1, source_target_pairs={{0,510},{1,511},{2,4},{3,5},{4,2},{5,3},{6,8},{7,9},{8,6},{9,7},{1... | collective-permute-start | bytes 3464 | tf_op jit(solution)/shard_map/ppermute | solution.py:319
  67.8 11.2 %collective-permute-start.14 = (f32[1,144]{1,0:T(1,128)S(1)}, f32[1,144]{1,0:T(1,128)S(1)}, u32[]{:S(2)}, u32[]{:S(2)}) collective-permute-start(f32[1,144]{1,0:T(1,128)S(1)} %get-tuple-element.35.own_row), channel_id=1, source_target_pairs={{2,511},{3,6},{6,3},{7,10},{10,7},{11,14},{14,11},{15,18},{18,15},... | collective-permute-start | bytes 1736 | tf_op jit(solution)/shard_map/ppermute | solution.py:319
  74.9 5.5 %collective-permute-start.13 = (f32[2,144]{1,0:T(2,128)S(1)}, f32[2,144]{1,0:T(2,128)S(1)}, u32[]{:S(2)}, u32[]{:S(2)}) collective-permute-start(f32[2,144]{1,0:T(2,128)S(1)} %pad_maximum_fusion), channel_id=1, source_target_pairs={{0,2},{1,3},{2,0},{3,1},{4,6},{5,7},{6,4},{7,5},{8,10},{9,11},{10,... | collective-permute-start | bytes 3464 | tf_op jit(solution)/shard_map/ppermute | solution.py:319
  76.9 3.5 %copy-start.2 = (bf16[72,3584]{1,0:T(8,128)(2,1)S(1)}, bf16[72,3584]{1,0:T(8,128)(2,1)}, u32[]{:S(2)}) copy-start(bf16[72,3584]{1,0:T(8,128)(2,1)} %query_ref.1) | copy-start | bytes 1548292
  76.9 3.5 %copy-start.3 = (bf16[72,3584]{1,0:T(8,128)(2,1)S(1)}, bf16[72,3584]{1,0:T(8,128)(2,1)}, u32[]{:S(2)}) copy-start(bf16[72,3584]{1,0:T(8,128)(2,1)} %passage_ref.1) | copy-start | bytes 1548292
  76.9 3.5 %copy-start.4 = (f32[144,1]{1,0:T(8,128)S(1)}, f32[144,1]{1,0:T(8,128)}, u32[]{:S(2)}) copy-start(f32[144,1]{1,0:T(8,128)} %get-tuple-element.41.scale_ref) | copy-start | bytes 1732
